TPU v7x, 32 devices: a whole 2x2x4 slice. The times are simulated.
32 devices in a mesh: section: 2 (over y), fsdp: 16 (over z, x, core).
Axes of the slice: x: 2, y: 2, z: 4, core: 2. Of those that a mesh axis runs over, the one named last changes fastest.
Arguments:
- clips: bfloat16 [64, 4, 8, 4, 256], P('fsdp'), may hold values from -30 to 30
- plan: int32 [16, 4], P('fsdp'), may hold values from 0 to 3, each once within a row
- gains: float32 [2, 256], P('section'), may hold values from 0.1 to 1.9
- weights: bfloat16 [2, 6912, 256], P('section', 'fsdp'), may hold values from -0.078125 to 0.078125
- cotangent: bfloat16 [64, 4, 8, 4, 256], P('fsdp'), may hold values from -6 to 6
Outputs:
- acts: bfloat16 [2, 64, 4, 8, 4, 256], P('section', 'fsdp')
- grad_in: bfloat16 [2, 64, 4, 8, 4, 256], P('section', 'fsdp')
- weight_grad: float32 [2, 6912, 256], P('section', 'fsdp')
Inputs may be any that keep to these rules, and one draw needn't show every extreme that they name: Each row of plan names every clip of its group once.
All inputs are finite; a program needn't handle non-finite values.
Results may differ from a plain program's by a relative error of at most 0.012.
The roundings to bfloat16 on the way count: a program that leaves them out, or rounds other values in their place, can miss the bound.
Values may be sent and summed in bfloat16 or wider, within the bound.
No kernel may reach another device: no remote copies, remote signals or barrier semaphores. Data moves between devices by JAX's collectives and lax.ppermute only.
A program may use at most 64 MiB of HBM per device.

v0:
```python
import math

import jax
import jax.numpy as jnp
from jax import lax
from jax.sharding import PartitionSpec as P

EPSILON = 1e-06


def shifted(value, axis, by):
    peers = lax.axis_size(axis)
    pairs = [(i, i + by) for i in range(peers) if 0 <= i + by < peers]
    return lax.ppermute(value, axis, pairs)


def unfold(volume):
    frames, height, breadth, channels = volume.shape
    padded = jnp.pad(volume, ((1, 1), (1, 1), (1, 1), (0, 0)))
    pieces = []
    for along_t in range(3):
        for along_h in range(3):
            for along_w in range(3):
                pieces.append(
                    padded[
                        along_t : along_t + frames,
                        along_h : along_h + height,
                        along_w : along_w + breadth,
                        :,
                    ]
                )
    return jnp.concatenate(pieces, axis=-1).reshape(frames * height * breadth, 27 * channels)


def normalize(volume, gain_row):
    values = volume.astype(jnp.float32)
    inverse = lax.rsqrt(jnp.mean(values * values, axis=-1, keepdims=True) + EPSILON)
    normed = values * inverse * gain_row
    return (values, inverse, normed)


def active_columns(volume, gain_row):
    values, inverse, normed = normalize(volume, gain_row)
    return unfold(jnp.maximum(normed, 0.0).astype(jnp.bfloat16))


def forward_block(volume, gain_row, full_weight):
    values, inverse, normed = normalize(volume, gain_row)
    active = jnp.maximum(normed, 0.0).astype(jnp.bfloat16)
    branch = jnp.dot(unfold(active), full_weight, preferred_element_type=jnp.float32)
    return (values + branch.reshape(values.shape)).astype(jnp.bfloat16)


def backward_block(volume, upstream, gain_row, reversed_weight):
    values, inverse, normed = normalize(volume, gain_row)
    channels = values.shape[-1]
    columns = unfold(upstream).reshape(-1, 27, channels)
    spread = lax.dot_general(
        columns, reversed_weight, (((1, 2), (0, 2)), ((), ())), preferred_element_type=jnp.float32
    )
    spread = spread.reshape(values.shape)
    scaled = gain_row * jnp.where(normed > 0.0, spread, 0.0)
    mixing = jnp.mean(values * scaled, axis=-1, keepdims=True)
    grad_input = upstream.astype(jnp.float32) + inverse * scaled - values * inverse**3 * mixing
    return grad_input.astype(jnp.bfloat16)


def weight_term(volume, upstream, gain_row):
    columns = active_columns(volume, gain_row)
    flattened = upstream.reshape(-1, upstream.shape[-1])
    return lax.dot_general(
        columns, flattened, (((0,), (0,)), ((), ())), preferred_element_type=jnp.float32
    )


def on_device(clips, plan, gains, weights, cotangent):
    section_index = lax.axis_index("section")
    leading = section_index == 0
    micro_count = plan.shape[1]
    ordered = jnp.take(clips, plan[0], axis=0)
    gain_row = gains[0]
    channels = weights.shape[2]
    full_weight = lax.all_gather(weights[0], "fsdp", axis=0, tiled=True)
    reversed_weight = full_weight.reshape(27, channels, channels)[::-1]
    fsdp_count = lax.axis_size("fsdp")
    voxels = clips.shape[1] * clips.shape[2] * clips.shape[3]
    factor = 1.0 / math.sqrt(fsdp_count * micro_count * voxels)

    def forward_many(volumes):
        return lax.map(lambda clip_in: forward_block(clip_in, gain_row, full_weight), volumes)

    def backward_many(volumes, upstreams):
        return lax.map(
            lambda paired: backward_block(paired[0], paired[1], gain_row, reversed_weight),
            (volumes, upstreams),
        )

    first_pass = forward_many(ordered)
    passed = shifted(first_pass, "section", 1)
    section_inputs = jnp.where(leading, ordered, passed)
    section_outputs = forward_many(section_inputs)
    first_back = backward_many(section_inputs, cotangent)
    returned = shifted(first_back, "section", -1)
    upstream_all = jnp.where(leading, returned, cotangent)
    grads_in = backward_many(section_inputs, upstream_all)

    def accumulate(running, paired):
        return (running + weight_term(paired[0], paired[1], gain_row), None)

    summed, unused = lax.scan(
        accumulate, jnp.zeros(full_weight.shape, jnp.float32), (section_inputs, upstream_all)
    )
    weight_grad = lax.psum_scatter(summed, "fsdp", scatter_dimension=0, tiled=True)
    return (section_outputs[None], grads_in[None], (weight_grad * factor)[None])


def solution(mesh):
    placed = (
        P("fsdp", None, None, None, None),
        P("fsdp", None),
        P("section", None),
        P("section", "fsdp", None),
        P("fsdp", None, None, None, None),
    )
    return jax.shard_map(
        on_device,
        mesh=mesh,
        in_specs=placed,
        out_specs=(
            P("section", "fsdp", None, None, None, None),
            P("section", "fsdp", None, None, None, None),
            P("section", "fsdp", None),
        ),
        check_vma=False,
    )
```

profile of v0, /device:TPU:0, one launch (start us, length us, event | category | flops | bytes accessed | tf_op | source)
XLA Modules:
  0.0 324.0 jit_solution(1688926617521706747)
XLA Ops:
  8.6 0.8 gather_fusion
  10.3 49.9 %all-gather.3.cloned.1.call-done = bf16[1,6912,256]{2,1,0:T(8,128)(2,1)} async-done(((bf16[1,432,256]{2,1,0:T(8,128)(2,1)}), bf16[1,6912,256]{2,1,0:T(8,128)(2,1)}) %all-gather.3.cloned.1.call-update) | async-done | bytes 3538960 | tf_op jit(solution)/shard_map/all_gather | solution.py:83
  60.3 14.6 %while.61 = (s32[]{:T(128)}, bf16[4,4,8,4,256]{4,3,2,1,0:T(4,128)(2,1)S(1)}, bf16[4,4,8,4,256]{4,3,2,1,0:T(4,128)(2,1)S(1)}, f32[1,256]{1,0:T(1,128)}, bf16[6912,256]{1,0:T(8,128)(2,1)}, /*index=5*/s32[]{:T(128)}) while((s32[]{:T(128)}, bf16[4,4,8,4,256]{4,3,2,1,0:T(4,128)(2,1)S(1)}, bf16[4,4,8,4,256]{4,3,2,1,0:T(4,128)(2,1)S(1)}, ...), condition=%wide.region_2.3_spmd, body=%wide.region_0.0_spmd.sunk | while | flops 453509248 | bytes 23609484 | solution.py:90
  61.9 1.4 copy-done.1
  65.6 1.4 copy-done.1
  69.2 1.4 copy-done.1
  72.8 1.4 copy-done.1
  74.9 3.4 %collective-permute-start = (bf16[4,4,8,4,256]{4,3,2,1,0:T(4,128)(2,1)S(1)}, bf16[4,4,8,4,256]{4,3,2,1,0:T(4,128)(2,1)S(1)}, u32[]{:S(2)}, u32[]{:S(2)}) collective-permute-start(bf16[4,4,8,4,256]{4,3,2,1,0:T(4,128)(2,1)S(1)} %get-tuple-element.352), channel_id=1, source_target_pairs={{0,16},{1,17},{2,18},{3,19},{4,20},{5,21},{6,22},{7,23},{8,24},{9,... | collective-permute-start | bytes 786440 | tf_op jit(solution)/shard_map/ppermute | solution.py:14
  78.4 4.3 %rev.3 = bf16[27,256,256]{2,1,0:T(8,128)(2,1)} reverse(bf16[27,256,256]{2,1,0:T(8,128)(2,1)} %bitcast.695), dimensions={0} | reverse | bytes 7077888 | tf_op jit(solution)/shard_map/rev | solution.py:84
  82.6 1.6 collective-permute-done
  84.7 15.2 %while.63 = (s32[]{:T(128)}, bf16[4,4,8,4,256]{4,3,2,1,0:T(4,128)(2,1)S(1)}, bf16[4,4,8,4,256]{4,3,2,1,0:T(4,128)(2,1)S(1)}, bf16[4,4,8,4,256]{4,2,3,1,0:T(8,128...) while((s32[]{:T(128)}, bf16[4,4,8,4,256]{4,3,2,1,0:T(4,128)(2,1)S(1)}, ...), condition=%wide.region_9.10_spmd, body=%wide.region_6.9_spmd.sunk | while | flops 453607808 | bytes 23992964 | solution.py:93
  85.4 1.5 copy-done.3
  86.9 1.4 fusion.503
  89.2 1.5 copy-done.3
  90.7 1.4 fusion.503
  93.0 1.5 copy-done.3
  94.5 1.4 fusion.503
  96.8 1.5 copy-done.3
  98.2 1.4 fusion.503
  99.8 1.3 collective-permute-start.1
  101.2 11.7 %while.62 = (s32[]{:T(128)}, bf16[4,4,8,4,256]{4,3,2,1,0:T(4,128)(2,1)S(1)}, bf16[4,4,8,4,256]{4,2,3,1,0:T(8,128)(2,1)S(1)}, f32[1,256]{1,0:T(1,128)S(1)}, bf16[6912,256]{1,0:T(8,128)(2,1)}, /*index=5*/s32[]{:T(128)}) while((s32[]{:T(128)}, bf16[4,4,8,4,256]{4,3,2,1,0:T(4,128)(2,1)S(1)}, bf16[4,4,8,4,256]{4,2,3,1,0:T(8,128)(2,1)S(1)}, ...), condition=%wide.region_5.6_spmd, body=%wide.region_3.5_spmd.sunk | while | flops 453509248 | bytes 23474300 | solution.py:90
  102.1 1.4 copy-done.2
  105.0 1.4 copy-done.2
  108.0 1.4 copy-done.2
  110.9 1.4 copy-done.2
  113.6 111.3 %while.65 = (s32[]{:T(128)}, f32[6912,256]{1,0:T(8,128)}, bf16[4,4,8,4,256]{4,3,2,1,0:T(4,128)(2,1)S(1)}, f32[1,256]{1,0:T(1,128)S(1)}, bf16[4,4,8,4,256]{4,3,2,1,0:T(4,128)(2,1)S(1)}, /*index=5*/s32[]{:T(128)}, s32[]{:T(128)}) while((s32[]{:T(128)}, f32[6912,256]{1,0:T(8,128)}, bf16[4,4,8,4,256]{4,3,2,1,0:T(4,128)(2,1)S(1)}, ...), condition=%wide.region_16.17_spmd.clone, body=%wide.region_14.16_spmd.clone.sunk | while | flops 456949888 | bytes 23532144 | solution.py:110
  122.7 0.8 constant_dynamic-update-slice_fusion.8
  132.2 2.9 reshape.349
  135.1 4.1 %convolution_add_fusion.2 = f32[6912,256]{1,0:T(8,128)} fusion(bf16[128,6912]{1,0:T(8,128)(2,1)S(1)} %reshape.349, bf16[128,256]{1,0:T(8,128)(2,1)S(1)} %reshape.350, f32[6912,256]{1,0:T(8,128)} %get-tuple-element.728, pred[]{:T(512)S(6)} %compare.8), kind=kOutput, calls=%fused_computation.339.clone.1 | convolution fusion | flops 456523776 | bytes 15990785 | tf_op jit(solution)/shard_map/while/body/eval_jaxpr/dot_general | solution.py:71
  148.3 0.8 constant_dynamic-update-slice_fusion.8
  157.8 2.9 reshape.349
  160.7 7.1 %convolution_add_fusion.2 = f32[6912,256]{1,0:T(8,128)} fusion(bf16[128,6912]{1,0:T(8,128)(2,1)S(1)} %reshape.349, bf16[128,256]{1,0:T(8,128)(2,1)S(1)} %reshape.350, f32[6912,256]{1,0:T(8,128)} %get-tuple-element.728, pred[]{:T(512)S(6)} %compare.8), kind=kOutput, calls=%fused_computation.339.clone.1 | convolution fusion | flops 456523776 | bytes 15990785 | tf_op jit(solution)/shard_map/while/body/eval_jaxpr/dot_general | solution.py:71
  176.8 0.8 constant_dynamic-update-slice_fusion.8
  186.4 2.9 reshape.349
  189.3 7.1 %convolution_add_fusion.2 = f32[6912,256]{1,0:T(8,128)} fusion(bf16[128,6912]{1,0:T(8,128)(2,1)S(1)} %reshape.349, bf16[128,256]{1,0:T(8,128)(2,1)S(1)} %reshape.350, f32[6912,256]{1,0:T(8,128)} %get-tuple-element.728, pred[]{:T(512)S(6)} %compare.8), kind=kOutput, calls=%fused_computation.339.clone.1 | convolution fusion | flops 456523776 | bytes 15990785 | tf_op jit(solution)/shard_map/while/body/eval_jaxpr/dot_general | solution.py:71
  214.9 2.9 reshape.349
  217.8 7.1 %convolution_add_fusion.2 = f32[6912,256]{1,0:T(8,128)} fusion(bf16[128,6912]{1,0:T(8,128)(2,1)S(1)} %reshape.349, bf16[128,256]{1,0:T(8,128)(2,1)S(1)} %reshape.350, f32[6912,256]{1,0:T(8,128)} %get-tuple-element.728, pred[]{:T(512)S(6)} %compare.8), kind=kOutput, calls=%fused_computation.339.clone.1 | convolution fusion | flops 456523776 | bytes 15990785 | tf_op jit(solution)/shard_map/while/body/eval_jaxpr/dot_general | solution.py:71
  225.0 16.1 %while.64 = (s32[]{:T(128)}, bf16[4,4,8,4,256]{4,3,2,1,0:T(4,128)(2,1)S(1)}, bf16[4,4,8,4,256]{4,3,2,1,0:T(4,128)(2,1)S(1)}, bf16[4,4,8,4,256]{4,2,3,1,0:T(8,128...) while((s32[]{:T(128)}, bf16[4,4,8,4,256]{4,3,2,1,0:T(4,128)(2,1)S(1)}, ...), condition=%wide.region_13.14_spmd, body=%wide.region_10.13_spmd.sunk | while | flops 453607808 | bytes 23992964 | solution.py:93
  225.8 1.5 copy-done.4
  227.2 1.4 fusion.533
  229.6 1.7 copy-done.4
  231.3 1.4 fusion.533
  233.6 1.8 copy-done.4
  235.4 1.4 fusion.533
  237.7 1.8 copy-done.4
  239.5 1.4 fusion.533
  241.1 74.2 %reduce-scatter.2.cloned.1.call-done = f32[432,256]{1,0:T(8,128)} async-done(((f32[6912,256]{1,0:T(8,128)}), f32[432,256]{1,0:T(8,128)}) %reduce-scatter.2.cloned.1.call-update) | async-done | bytes 442384 | tf_op jit(solution)/shard_map/reduce_scatter | solution.py:113
  315.3 1.8 multiply_bitcast_fusion
  (708 shorter events, 94.0 us)
Async XLA Ops:
  7.2 1.5 copy-start
  7.2 53.0 %all-gather.3.cloned.1.call-start = ((), (), s32[]{:S(2)}) async-start(), calls=%async_computation.2 | async-start | bytes 3760128 | tf_op jit(solution)/shard_map/all_gather | solution.py:83
  7.9 307.4 %reduce-scatter.2.cloned.1.call-start = ((), (), s32[]{:S(2)}) async-start(), calls=%async_computation.1 | async-start | bytes 7520256 | tf_op jit(solution)/shard_map/reduce_scatter | solution.py:113
  60.3 1.2 copy-start.6
  61.3 2.0 copy-start.1
  64.0 1.2 copy-start.6
  64.9 2.0 copy-start.1
  67.6 1.2 copy-start.6
  68.6 2.0 copy-start.1
  71.3 1.2 copy-start.6
  72.2 2.0 copy-start.1
  74.9 9.4 %collective-permute-start = (bf16[4,4,8,4,256]{4,3,2,1,0:T(4,128)(2,1)S(1)}, bf16[4,4,8,4,256]{4,3,2,1,0:T(4,128)(2,1)S(1)}, u32[]{:S(2)}, u32[]{:S(2)}) collective-permute-start(bf16[4,4,8,4,256]{4,3,2,1,0:T(4,128)(2,1)S(1)} %get-tuple-element.352), channel_id=1, source_target_pairs={{0,16},{1,17},{2,18},{3,19},{4,20},{5,21},{6,22},{7,23},{8,24},{9,... | collective-permute-start | bytes 786440 | tf_op jit(solution)/shard_map/ppermute | solution.py:14
  78.3 6.3 %copy-start.5 = (bf16[4,4,8,4,256]{4,3,2,1,0:T(4,128)(2,1)S(1)}, bf16[4,4,8,4,256]{4,3,2,1,0:T(4,128)(2,1)}, u32[]{:S(2)}) copy-start(bf16[4,4,8,4,256]{4,3,2,1,0:T(4,128)(2,1)} %param.19) | copy-start | bytes 786436
  78.3 6.3 %copy-start.7 = (f32[1,256]{1,0:T(1,128)S(1)}, f32[1,256]{1,0:T(1,128)}, u32[]{:S(2)}) copy-start(f32[1,256]{1,0:T(1,128)} %get-tuple-element.752) | copy-start | bytes 3076
  84.9 2.0 copy-start.3
  88.7 2.0 copy-start.3
  92.5 2.0 copy-start.3
  96.2 2.0 copy-start.3
  99.8 13.1 %collective-permute-start.1 = (bf16[4,4,8,4,256]{4,3,2,1,0:T(4,128)(2,1)S(1)}, bf16[4,4,8,4,256]{4,3,2,1,0:T(4,128)(2,1)S(1)}, u32[]{:S(2)}, u32[]{:S(2)}) collective-permute-start(bf16[4,4,8,4,256]{4,3,2,1,0:T(4,128)(2,1)S(1)} %get-tuple-element.354), channel_id=1, source_target_pairs={{16,0},{17,1},{18,2},{19,3},{20,4},{21,5},{22,6},{23,7},{24,8},{25... | collective-permute-start | bytes 786440 | tf_op jit(solution)/shard_map/ppermute | solution.py:14
  101.5 2.0 copy-start.2
  104.4 2.0 copy-start.2
  107.3 2.0 copy-start.2
  110.3 2.0 copy-start.2
  112.9 0.7 copy-start.9
  225.2 2.0 copy-start.4
  229.0 2.3 copy-start.4
  233.1 2.3 copy-start.4
  237.2 2.3 copy-start.4
  241.1 76.0 %copy-start.8 = (bf16[4,4,8,4,256]{4,3,2,1,0:T(4,128)(2,1)}, bf16[4,4,8,4,256]{4,3,2,1,0:T(4,128)(2,1)S(1)}, u32[]{:S(2)}) copy-start(bf16[4,4,8,4,256]{4,3,2,1,0:T(4,128)(2,1)S(1)} %get-tuple-element.355) | copy-start | bytes 786436
Sparse Core Ops, SparseCore 0:
  10.3 49.8 all-gather.2
  225.1 90.2 reduce-scatter.1
where the time goes:
time: 325 us; the launch traced here: 324 us
  waiting for transfers between devices  126 us (39%)
  local copies, waits for them, and re-layouts  118 us (36%)
  matrix products  41.5 us (13%)
  other arithmetic  14.6 us (4%)
  between operations  14.2 us (4%)
  starting transfers between devices  4.78 us (1%)
  loops' own time  4.48 us (1%)
    while x548, local copies, waits for them, and re-layouts  96 us
    reduce_scatter x1, waiting for transfers between devices, on_device(): lax.psum_scatter(summed, 'fsdp', scatter_dimension=0, tiled=True)  74.2 us
    all_gather x1, waiting for transfers between devices, on_device(): full_weight = lax.all_gather(weights[0], 'fsdp', axis=0, tiled=True)  49.9 us
    dot_general x4, matrix products, weight_term(): lax.dot_general(columns, flattened, (((0,), (0,)), ((), ())), preferred_e...  25.3 us
    reshape x4, local copies, waits for them, and re-layouts, unfold(): jnp.concatenate(pieces, axis=-1)  11.6 us
    dot_general x8, matrix products, backward_block(): lax.dot_general(columns, reversed_weight, (((1, 2), (0, 2)), ((), ())), p...  11.2 us
  transfers between devices with their start and end apart: 4, of which 3 were waited for; matrix products, arithmetic and copies ran while one was open for 6% of the time, Pallas kernels for 0%

commit v1 on v0

v1 whole, which is shorter than its diff:
```python
import functools
import math

import jax
import jax.numpy as jnp
from jax import lax
from jax.experimental import pallas as pl
from jax.experimental.pallas import tpu as pltpu
from jax.sharding import PartitionSpec as P

EPSILON = 1e-06
ROW_TILE = 16
VMEM_LIMIT = 48 * 1024 * 1024


def normalize(values, gain_row):
    inverse = lax.rsqrt(jnp.mean(values * values, axis=-1, keepdims=True) + EPSILON)
    return inverse, values * inverse * gain_row


def activate(values, gain_row):
    inverse, normed = normalize(values, gain_row)
    return jnp.maximum(normed, 0.0).astype(jnp.bfloat16)


def back(values, upstream, spread, gain_row):
    inverse, normed = normalize(values, gain_row)
    scaled = gain_row * jnp.where(normed > 0.0, spread, 0.0)
    mixing = jnp.mean(values * scaled, axis=-1, keepdims=True)
    return upstream + inverse * scaled - values * (inverse * inverse * inverse) * mixing


def fill_columns(cols_ref, values, dims):
    micro, frames, height, width, channels = dims
    plane = height * width
    voxels = frames * plane
    total = micro * voxels
    row = lax.broadcasted_iota(jnp.int32, (plane, channels), 0)
    across = row % width
    down = row // width
    zero = jnp.zeros((micro, plane, cols_ref.shape[2]), jnp.bfloat16)
    cols_ref[:, :plane, :] = zero
    cols_ref[:, plane + voxels :, :] = zero

    def masked(rolled, inside):
        kept = rolled.reshape(total // plane, plane, channels) * inside.astype(jnp.float32)[None]
        return kept.reshape(total, channels)

    for by_w in (-1, 0, 1):
        if by_w == 0:
            along = values
        else:
            inside = (across + by_w >= 0) & (across + by_w < width)
            along = masked(pltpu.roll(values, (-by_w) % total, 0), inside)
        for by_h in (-1, 0, 1):
            if by_h == 0:
                moved = along
            else:
                inside = (down + by_h >= 0) & (down + by_h < height)
                moved = masked(pltpu.roll(along, (-by_h * width) % total, 0), inside)
            j = 3 * (by_h + 1) + by_w + 1
            cols_ref[:, plane : plane + voxels, j * channels : (j + 1) * channels] = moved.astype(
                jnp.bfloat16
            ).reshape(micro, voxels, channels)


def frame_columns(cols_ref, by_t, dims, begin, end):
    micro, frames, height, width, channels = dims
    plane = height * width
    voxels = frames * plane
    start = plane * (by_t + 1)
    return cols_ref[:, start : start + voxels, begin:end].reshape(micro * voxels, end - begin)


def convolve(cols_ref, weight_ref, dims):
    channels = dims[4]
    total = None
    for by_t in (-1, 0, 1):
        first = 9 * (by_t + 1) * channels
        term = jnp.dot(
            frame_columns(cols_ref, by_t, dims, 0, 9 * channels),
            weight_ref[first : first + 9 * channels, :],
            preferred_element_type=jnp.float32,
        )
        total = term if total is None else total + term
    return total


def convolve_back(cols_ref, weight_ref, dims):
    channels = dims[4]
    total = None
    for by_t in (-1, 0, 1):
        for j in range(9):
            k = 26 - (9 * (by_t + 1) + j)
            term = lax.dot_general(
                frame_columns(cols_ref, by_t, dims, j * channels, (j + 1) * channels),
                weight_ref[k * channels : (k + 1) * channels, :],
                (((1,), (1,)), ((), ())),
                preferred_element_type=jnp.float32,
            )
            total = term if total is None else total + term
    return total


def gather_copies(place_ref, pieces, weight_ref, sems):
    copies = []
    for at, piece in enumerate(pieces):
        rows = piece.shape[0]
        start = place_ref[at] if len(pieces) > 1 else 0
        if len(pieces) > 1:
            start = pl.multiple_of(start, ROW_TILE)
        copies.append(pltpu.make_async_copy(piece, weight_ref.at[pl.ds(start, rows)], sems.at[at]))
    return copies


def take_clips(plan_ref, clips_ref, dims):
    micro, channels = dims[0], dims[4]
    picked = [clips_ref[plan_ref[m]] for m in range(micro)]
    return jnp.concatenate(picked, axis=0).astype(jnp.float32)


def first_kernel(dims, count, flag_ref, plan_ref, place_ref, clips_ref, cotangent_ref, gain_ref, *rest):
    pieces, (out_ref, weight_ref, cols_ref, sems) = rest[:count], rest[count:]
    copies = gather_copies(place_ref, pieces, weight_ref, sems)
    for copy in copies:
        copy.start()
    total = dims[0] * dims[1] * dims[2] * dims[3]
    leading = flag_ref[0] == 0
    ordered = take_clips(plan_ref, clips_ref, dims)
    upstream = cotangent_ref[...].reshape(total, dims[4]).astype(jnp.float32)
    active = activate(ordered, gain_ref[...]).astype(jnp.float32)
    fill_columns(cols_ref, jnp.where(leading, active, upstream), dims)
    for copy in copies:
        copy.wait()

    @pl.when(leading)
    def _():
        branch = convolve(cols_ref, weight_ref, dims)
        out_ref[...] = (take_clips(plan_ref, clips_ref, dims) + branch).astype(jnp.bfloat16)

    @pl.when(jnp.logical_not(leading))
    def _():
        out_ref[...] = convolve_back(cols_ref, weight_ref, dims).astype(jnp.bfloat16)


def second_kernel(dims, count, flag_ref, plan_ref, place_ref, clips_ref, cotangent_ref, gain_ref, last_gain_ref,
                  mine_ref, theirs_ref, *rest):
    grad_ref, pieces = rest[0], rest[1 : 1 + count]
    turned_ref, cols_ref, sums_ref, sems = rest[1 + count :]
    channels = dims[4]
    total = dims[0] * dims[1] * dims[2] * dims[3]
    leading = flag_ref[0] == 0
    mine = mine_ref[...].astype(jnp.float32)
    theirs = theirs_ref[...].astype(jnp.float32)
    hidden = jnp.where(leading, mine, theirs)
    spread = jnp.where(leading, theirs, mine)
    cotangent = cotangent_ref[...].reshape(total, channels).astype(jnp.float32)
    upstream = back(hidden, cotangent, spread, last_gain_ref[...]).astype(jnp.bfloat16)
    grad_ref[...] = upstream
    ordered = take_clips(plan_ref, clips_ref, dims)
    active = activate(jnp.where(leading, ordered, hidden), gain_ref[...])
    turned_ref[...] = active.T
    fill_columns(cols_ref, jnp.where(leading, upstream.astype(jnp.float32), cotangent), dims)
    for by_t in (-1, 0, 1):
        for j in range(9):
            k = 26 - (9 * (by_t + 1) + j)
            sums_ref[k * channels : (k + 1) * channels, :] = jnp.dot(
                turned_ref[...],
                frame_columns(cols_ref, by_t, dims, j * channels, (j + 1) * channels),
                preferred_element_type=jnp.float32,
            ).astype(jnp.bfloat16)
    copies = []
    at = 0
    for number, piece in enumerate(pieces):
        rows = piece.shape[-2]
        if len(piece.shape) == 2:
            copies.append(pltpu.make_async_copy(sums_ref, piece, sems.at[0]))
        else:
            for inner in range(piece.shape[0]):
                start = pl.multiple_of(place_ref[at], ROW_TILE)
                copies.append(
                    pltpu.make_async_copy(sums_ref.at[pl.ds(start, rows)], piece.at[inner], sems.at[at])
                )
                at += 1
    for copy in copies:
        copy.start()
    for copy in copies:
        copy.wait()


def third_kernel(dims, count, flag_ref, plan_ref, place_ref, clips_ref, gain_ref, mine_ref, theirs_ref, grad_ref,
                 *rest):
    pieces, (acts_ref, grads_ref, weight_ref, cols_ref, sems) = rest[:count], rest[count:]
    copies = gather_copies(place_ref, pieces, weight_ref, sems)
    for copy in copies:
        copy.start()
    leading = flag_ref[0] == 0
    gain_row = gain_ref[...]

    @pl.when(leading)
    def _():
        fill_columns(cols_ref, grad_ref[...].astype(jnp.float32), dims)

    @pl.when(jnp.logical_not(leading))
    def _():
        hidden = theirs_ref[...].astype(jnp.float32)
        fill_columns(cols_ref, activate(hidden, gain_row).astype(jnp.float32), dims)

    for copy in copies:
        copy.wait()

    @pl.when(leading)
    def _():
        spread = convolve_back(cols_ref, weight_ref, dims)
        ordered = take_clips(plan_ref, clips_ref, dims)
        upstream = grad_ref[...].astype(jnp.float32)
        grads_ref[...] = back(ordered, upstream, spread, gain_row).astype(jnp.bfloat16)
        acts_ref[...] = mine_ref[...]

    @pl.when(jnp.logical_not(leading))
    def _():
        branch = convolve(cols_ref, weight_ref, dims)
        acts_ref[...] = (theirs_ref[...].astype(jnp.float32) + branch).astype(jnp.bfloat16)
        grads_ref[...] = grad_ref[...]


def swap(value, axis, by):
    return lax.ppermute(value, axis, [(i, i ^ by) for i in range(lax.axis_size(axis))])


def plain_sum(left, right):
    return left.astype(jnp.float32) + right.astype(jnp.float32)


def on_device(clips, plan, gains, weights, cotangent):
    section = lax.axis_index("section")
    peers = lax.axis_size("fsdp")
    place = lax.axis_index("fsdp")
    micro, frames, height, width, channels = clips.shape
    dims = clips.shape
    voxels = frames * height * width
    total = micro * voxels
    rows = weights.shape[1]
    all_rows = rows * peers
    factor = 1.0 / math.sqrt(peers * total)
    flag = section.astype(jnp.int32).reshape(1)
    order = plan[0]
    flat_clips = clips.reshape(micro, voxels, channels)
    flat_cotangent = cotangent.reshape(micro, voxels, channels)
    other_gain = swap(gains, "section", 1)
    last_gain = jnp.where(section == 0, other_gain, gains)
    split = peers == 16 and rows % ROW_TILE == 0

    own = weights[0]
    if split:
        far = {0: own}
        for by in (4, 8, 12):
            far[by] = swap(own, "fsdp", by)
        near = {}
        for by in (0, 4, 8, 12):
            near[by] = far[by]
            near[by + 2] = swap(far[by], "fsdp", 2)
        held = dict(near)
        for by in near:
            held[by + 1] = swap(near[by], "fsdp", 1)
        offsets = sorted(held)
        pieces = [held[by] for by in offsets]
        places = jnp.stack([(place ^ by) * rows for by in offsets]).astype(jnp.int32)
    else:
        pieces = [lax.all_gather(own, "fsdp", axis=0, tiled=True)]
        places = jnp.zeros((1,), jnp.int32)

    count = len(pieces)
    smem = pl.BlockSpec(memory_space=pltpu.SMEM)
    vmem = pl.BlockSpec(memory_space=pltpu.VMEM)
    anywhere = pl.BlockSpec(memory_space=pl.ANY)
    weight_scratch = pltpu.VMEM((all_rows, channels), jnp.bfloat16)
    cols_scratch = pltpu.VMEM((micro, voxels + 2 * height * width, 9 * channels), jnp.bfloat16)
    volume = jax.ShapeDtypeStruct((total, channels), jnp.bfloat16)
    flops = 2 * total * all_rows * channels
    params = pltpu.CompilerParams(vmem_limit_bytes=VMEM_LIMIT)
    cost = pl.CostEstimate(flops=flops, bytes_accessed=2 * all_rows * channels, transcendentals=0)

    mine = pl.pallas_call(
        functools.partial(first_kernel, dims, count),
        out_shape=volume,
        in_specs=[smem] * 3 + [vmem] * 3 + [anywhere] * count,
        out_specs=vmem,
        scratch_shapes=[weight_scratch, cols_scratch, pltpu.SemaphoreType.DMA((count,))],
        compiler_params=params,
        cost_estimate=cost,
    )(flag, order, places, flat_clips, flat_cotangent, gains, *pieces)

    theirs = swap(mine, "section", 1)

    if split:
        shapes = [jax.ShapeDtypeStruct((2, rows, channels), jnp.bfloat16)] * 8
        outward = []
        for by in (0, 4, 8, 12):
            outward += [by, by + 2, by + 1, by + 3]
        out_places = jnp.stack([(place ^ by) * rows for by in outward]).astype(jnp.int32)
    else:
        shapes = [jax.ShapeDtypeStruct((all_rows, channels), jnp.bfloat16)]
        out_places = places
    grad, *partial_sums = pl.pallas_call(
        functools.partial(second_kernel, dims, len(shapes)),
        out_shape=[volume] + shapes,
        in_specs=[smem] * 3 + [vmem] * 6,
        out_specs=[vmem] + [anywhere] * len(shapes),
        scratch_shapes=[
            pltpu.VMEM((channels, total), jnp.bfloat16),
            cols_scratch,
            weight_scratch,
            pltpu.SemaphoreType.DMA((2 * len(shapes),)),
        ],
        compiler_params=params,
        cost_estimate=cost,
    )(flag, order, out_places, flat_clips, flat_cotangent, gains, last_gain, mine, theirs)

    if split:
        arrived = []
        for at in (3, 2, 1, 0):
            kept, sent = partial_sums[2 * at], partial_sums[2 * at + 1]
            both = plain_sum(kept, swap(sent, "fsdp", 1))
            across = swap(both[1].astype(jnp.bfloat16), "fsdp", 2)
            chip_pair = both[0] + across.astype(jnp.float32)
            if at:
                arrived.append(swap(chip_pair.astype(jnp.bfloat16), "fsdp", 4 * at).astype(jnp.float32))
            else:
                arrived.append(chip_pair)
        weight_grad = sum(arrived[1:], arrived[0]) * factor
    else:
        summed = partial_sums[0].astype(jnp.float32)
        weight_grad = lax.psum_scatter(summed, "fsdp", scatter_dimension=0, tiled=True) * factor

    acts, grads = pl.pallas_call(
        functools.partial(third_kernel, dims, count),
        out_shape=[volume, volume],
        in_specs=[smem] * 3 + [vmem] * 5 + [anywhere] * count,
        out_specs=[vmem, vmem],
        scratch_shapes=[weight_scratch, cols_scratch, pltpu.SemaphoreType.DMA((count,))],
        compiler_params=params,
        cost_estimate=cost,
    )(flag, order, places, flat_clips, gains, mine, theirs, grad, *pieces)
    return (acts.reshape(1, *dims), grads.reshape(1, *dims), weight_grad[None])


def solution(mesh):
    placed = (
        P("fsdp", None, None, None, None),
        P("fsdp", None),
        P("section", None),
        P("section", "fsdp", None),
        P("fsdp", None, None, None, None),
    )
    return jax.shard_map(
        on_device,
        mesh=mesh,
        in_specs=placed,
        out_specs=(
            P("section", "fsdp", None, None, None, None),
            P("section", "fsdp", None, None, None, None),
            P("section", "fsdp", None),
        ),
        check_vma=False,
    )
```

time: 325 us -> 102 us (0.31)
  local copies, waits for them, and re-layouts: 118 us -> 7.68 us
  waiting for transfers between devices: 126 us -> 40.8 us
  matrix products: 41.5 us -> 0 us
  Pallas kernels: 0 us -> 24.2 us
  starting transfers between devices: 4.78 us -> 23 us
  between operations: 14.2 us -> 0.86 us
  other arithmetic: 14.6 us -> 4.79 us
  loops' own time: 4.48 us -> 0 us
    while x549 -> x0, local copies, waits for them, and re-layouts: 96 us -> none
    reduce_scatter x1 -> x0, waiting for transfers between devices: 74.2 us -> none  [on_device(): lax.psum_scatter(summed, 'fsdp', scatter_dimension=0, tiled=True)]
    all_gather x1 -> x0, waiting for transfers between devices: 49.9 us -> none  [on_device(): full_weight = lax.all_gather(weights[0], 'fsdp', axis=0, tiled=True)]
    dot_general x20 -> x0, matrix products: 41.5 us -> none  [the longest x4 25.3 us: weight_term(): lax.dot_general(columns, flattened, (((0,), (0,)), ((), ())), preferred_e...]
    ppermute x2 -> x28, waiting for transfers between devices: 1.65 us -> 40.8 us  [swap(): lax.ppermute(value, axis, [(i, i ^ by) for i in range(lax.axis_size(axis))])]
    pallas_call x0 -> x3, Pallas kernels: none -> 24.2 us  [the longest x1 8.39 us: on_device(): pl.pallas_call(functools.partial(second_kernel, dims, len(shapes)), out_s...]
    ppermute x2 -> x28, starting transfers between devices: 4.7 us -> 23 us  [swap(): lax.ppermute(value, axis, [(i, i ^ by) for i in range(lax.axis_size(axis))])]
    reshape x8 -> x4, local copies, waits for them, and re-layouts: 11.7 us -> 3.69 us  [the longest x2 1.53 us: on_device(): return (acts.reshape(1, *dims), grads.reshape(1, *dims), weight_grad[None])]
  transfers between devices with their start and end apart: 4 -> 28, of which waited for: 3 -> 11; matrix products, arithmetic and copies ran while one was open for 6% -> 7% of each run, Pallas kernels for 0% -> 8%
where the time goes in v1:
time: 102 us; the launch traced here: 101 us
  waiting for transfers between devices  40.8 us (40%)
  Pallas kernels  24.2 us (24%)
  starting transfers between devices  23 us (23%)
  local copies, waits for them, and re-layouts  7.68 us (8%)
  other arithmetic  4.79 us (5%)
    ppermute x28, waiting for transfers between devices, swap(): lax.ppermute(value, axis, [(i, i ^ by) for i in range(lax.axis_size(axis))])  40.8 us
    ppermute x28, starting transfers between devices, swap(): lax.ppermute(value, axis, [(i, i ^ by) for i in range(lax.axis_size(axis))])  23 us
    pallas_call x1, Pallas kernels, on_device(): pl.pallas_call(functools.partial(second_kernel, dims, len(shapes)), out_s...  8.39 us
    pallas_call x1, Pallas kernels, on_device(): pl.pallas_call(functools.partial(third_kernel, dims, count), out_shape=[v...  8 us
    pallas_call x1, Pallas kernels, on_device(): pl.pallas_call(functools.partial(first_kernel, dims, count), out_shape=vo...  7.77 us
    unnamed x24, local copies, waits for them, and re-layouts  2.97 us
    convert_element_type x3, other arithmetic, on_device(): chip_pair.astype(jnp.bfloat16)  2.23 us
    broadcast_in_dim x1, other arithmetic, on_device(): return (acts.reshape(1, *dims), grads.reshape(1, *dims), weight_grad[None])  2.16 us
  transfers between devices with their start and end apart: 28, of which 11 were waited for; matrix products, arithmetic and copies ran while one was open for 7% of the time, Pallas kernels for 8%

profile of v1, /device:TPU:0, one launch (start us, length us, event | category | flops | bytes accessed | tf_op | source)
XLA Modules:
  0.0 101.3 jit_solution(7907676162289495943)
XLA Ops:
  0.6 5.1 %collective-permute-start.11 = (bf16[432,256]{1,0:T(8,128)(2,1)}, bf16[432,256]{1,0:T(8,128)(2,1)S(1)}, u32[]{:S(2)}, u32[]{:S(2)}) collective-permute-start(bf16[432,256]{1,0:T(8,128)(2,1)} %bitcast.57), channel_id=1, source_target_pairs={{0,12},{1,13},{2,14},{3,15},{4,8},{5,9},{6,10},{7,11},{8,4},{9,5},... | collective-permute-start | bytes 663560 | tf_op jit(solution)/shard_map/ppermute | solution.py:228
  5.7 0.6 collective-permute-start.3
  6.4 1.6 %collective-permute-start.1 = (bf16[432,256]{1,0:T(8,128)(2,1)}, bf16[432,256]{1,0:T(8,128)(2,1)S(1)}, u32[]{:S(2)}, u32[]{:S(2)}) collective-permute-start(bf16[432,256]{1,0:T(8,128)(2,1)} %bitcast.60), channel_id=1, source_target_pairs={{0,2},{1,3},{2,0},{3,1},{4,6},{5,7},{6,4},{7,5},{8,10},{9,11},{10,... | collective-permute-start | bytes 663560 | tf_op jit(solution)/shard_map/ppermute | solution.py:228
  8.0 4.3 %collective-permute-done.11.rest_12_ = bf16[432,256]{1,0:T(8,128)(2,1)S(1)} collective-permute-done((bf16[432,256]{1,0:T(8,128)(2,1)}, bf16[432,256]{1,0:T(8,128)(2,1)S(1)}, u32[]{:S(2)}, u32[]{:S(2)}) %collective-permute-start.11) | collective-permute-done | bytes 221216 | tf_op jit(solution)/shard_map/ppermute | solution.py:228
  12.4 1.7 %collective-permute-start.13 = (bf16[432,256]{1,0:T(8,128)(2,1)S(1)}, bf16[432,256]{1,0:T(8,128)(2,1)S(1)}, u32[]{:S(2)}, u32[]{:S(2)}) collective-permute-start(bf16[432,256]{1,0:T(8,128)(2,1)S(1)} %collective-permute-done.11.rest_12_), channel_id=1, source_target_pairs={{0,2},{1,3},{2,0},{3,1},{4,6},{5,7},{6,4},{7,5},{8,10},{9,11},{10,... | collective-permute-start | bytes 663560 | tf_op jit(solution)/shard_map/ppermute | solution.py:228
  14.0 10.7 %collective-permute-done.7.rest_8_ = bf16[432,256]{1,0:T(8,128)(2,1)S(1)} collective-permute-done((bf16[432,256]{1,0:T(8,128)(2,1)}, bf16[432,256]{1,0:T(8,128)(2,1)S(1)}, u32[]{:S(2)}, u32[]{:S(2)}) %collective-permute-start.7) | collective-permute-done | bytes 221216 | tf_op jit(solution)/shard_map/ppermute | solution.py:228
  24.8 1.5 %collective-permute-start.9 = (bf16[432,256]{1,0:T(8,128)(2,1)S(1)}, bf16[432,256]{1,0:T(8,128)(2,1)S(1)}, u32[]{:S(2)}, u32[]{:S(2)}) collective-permute-start(bf16[432,256]{1,0:T(8,128)(2,1)S(1)} %collective-permute-done.7.rest_8_), channel_id=1, source_target_pairs={{0,2},{1,3},{2,0},{3,1},{4,6},{5,7},{6,4},{7,5},{8,10},{9,11},{10,... | collective-permute-start | bytes 663560 | tf_op jit(solution)/shard_map/ppermute | solution.py:228
  26.3 0.2 collective-permute-start.8
  26.5 0.5 collective-permute-start.5
  27.0 0.5 collective-permute-start.2
  27.5 5.4 %collective-permute-done.9.rest_10_ = bf16[432,256]{1,0:T(8,128)(2,1)S(1)} collective-permute-done((bf16[432,256]{1,0:T(8,128)(2,1)S(1)}, bf16[432,256]{1,0:T(8,128)(2,1)S(1)}, u32[]{:S(2)}, u32[]{:S(2)}) %collective-permute-start.9) | collective-permute-done | bytes 221216 | tf_op jit(solution)/shard_map/ppermute | solution.py:228
  33.0 0.5 collective-permute-start.10
  33.5 3.8 %collective-permute-done.5.rest_6_ = bf16[432,256]{1,0:T(8,128)(2,1)S(1)} collective-permute-done((bf16[432,256]{1,0:T(8,128)(2,1)S(1)}, bf16[432,256]{1,0:T(8,128)(2,1)S(1)}, u32[]{:S(2)}, u32[]{:S(2)}) %collective-permute-start.5) | collective-permute-done | bytes 221216 | tf_op jit(solution)/shard_map/ppermute | solution.py:228
  37.3 1.1 %reshape.26.clips_ref = bf16[4,128,256]{2,1,0:T(8,128)(2,1)S(1)} reshape(bf16[4,4,8,4,256]{4,3,2,1,0:T(4,128)(2,1)} %param.5) | data formatting | bytes 524288 | tf_op jit(solution)/shard_map/reshape | solution.py:248
  38.5 1.1 %reshape.27.cotangent_ref = bf16[4,128,256]{2,1,0:T(8,128)(2,1)S(1)} reshape(bf16[4,4,8,4,256]{4,3,2,1,0:T(4,128)(2,1)} %param.9) | data formatting | bytes 524288 | tf_op jit(solution)/shard_map/reshape | solution.py:249
  39.7 0.7 copy-done.6
  40.4 0.6 copy-done
  41.0 0.9 copy-done.7
  42.0 7.8 %shard_map.76.mine_ref = bf16[512,256]{1,0:T(8,128)(2,1)S(1)} custom-call(s32[1]{0:T(128)} %bitcast.flag_ref, s32[4]{0:T(128)S(1)} %bitcast.64, s32[16]{0:T(128)S(1)} %stack.86.place_ref, bf16[4,128,256]{2,1,0:T(8,128)(2,1)S(1)} %reshape.26.clips_ref, bf16[4,128,256]{2,1,0:T(8,128)(2,1)S(1)} %reshape.27.cotangent_ref, f32[1,256]{1,0:T(1,128)S(1)} %copy-done, ...), custom_call_target="tpu_custom_call" | custom-call | flops 1811939328 | bytes 3538944 | tf_op jit(solution)/shard_map/pallas_call | solution.py:284
  49.8 0.7 copy-done.4
  50.4 1.5 %collective-permute-start.15 = (bf16[512,256]{1,0:T(8,128)(2,1)S(1)}, bf16[512,256]{1,0:T(8,128)(2,1)S(1)}, u32[]{:S(2)}, u32[]{:S(2)}) collective-permute-start(bf16[512,256]{1,0:T(8,128)(2,1)S(1)} %shard_map.76.mine_ref), channel_id=1, source_target_pairs={{0,16},{16,0},{1,17},{17,1},{2,18},{18,2},{3,19},{19,3},{4,20},{20... | collective-permute-start | bytes 786440 | tf_op jit(solution)/shard_map/ppermute | solution.py:228
  52.0 0.5 collective-permute-start.16
  52.6 6.6 %collective-permute-done.16 = f32[1,256]{1,0:T(1,128)S(1)} collective-permute-done((f32[1,256]{1,0:T(1,128)S(1)}, f32[1,256]{1,0:T(1,128)S(1)}, u32[]{:S(2)}, u32[]{:S(2)}) %collective-permute-start.16) | collective-permute-done | bytes 1056 | tf_op jit(solution)/shard_map/ppermute | solution.py:228
  59.2 8.4 %shard_map.77 = (bf16[512,256]{1,0:T(8,128)(2,1)S(1)}, bf16[2,432,256]{2,1,0:T(8,128)(2,1)S(1)}, bf16[2,432,256]{2,1,0:T(8,128)(2,1)S(1)}, bf16[2,432,256]{2,1,0...) custom-call(s32[1]{0:T(128)} %bitcast.flag_ref, ...), custom_call_target="tpu_custom_call" | custom-call | flops 1811939328 | bytes 3538944 | tf_op jit(solution)/shard_map/pallas_call | solution.py:305
  67.6 0.5 collective-permute-start.20
  68.2 0.4 collective-permute-start.26
  68.6 0.8 collective-permute-done.17
  69.5 1.6 %collective-permute-start.18 = (bf16[432,256]{1,0:T(8,128)(2,1)S(1)}, bf16[432,256]{1,0:T(8,128)(2,1)S(1)}, u32[]{:S(2)}, u32[]{:S(2)}) collective-permute-start(bf16[432,256]{1,0:T(8,128)(2,1)S(1)} %fusion.10), channel_id=1, source_target_pairs={{0,2},{1,3},{2,0},{3,1},{4,6},{5,7},{6,4},{7,5},{8,10},{9,11},{10,... | collective-permute-start | bytes 663560 | tf_op jit(solution)/shard_map/ppermute | solution.py:228
  71.2 0.6 collective-permute-start.21
  71.8 0.1 convert_add_fusion.1
  72.0 1.6 %collective-permute-start.24 = (bf16[432,256]{1,0:T(8,128)(2,1)S(1)}, bf16[432,256]{1,0:T(8,128)(2,1)S(1)}, u32[]{:S(2)}, u32[]{:S(2)}) collective-permute-start(bf16[432,256]{1,0:T(8,128)(2,1)S(1)} %fusion.12), channel_id=1, source_target_pairs={{0,2},{1,3},{2,0},{3,1},{4,6},{5,7},{6,4},{7,5},{8,10},{9,11},{10,... | collective-permute-start | bytes 663560 | tf_op jit(solution)/shard_map/ppermute | solution.py:228
  73.5 0.1 convert_add_fusion
  73.7 0.8 fusion.13
  74.4 0.5 collective-permute-start.27
  75.0 2.9 %collective-permute-done.18 = bf16[432,256]{1,0:T(8,128)(2,1)S(1)} collective-permute-done((bf16[432,256]{1,0:T(8,128)(2,1)S(1)}, bf16[432,256]{1,0:T(8,128)(2,1)S(1)}, u32[]{:S(2)}, u32[]{:S(2)}) %collective-permute-start.18) | collective-permute-done | bytes 221216 | tf_op jit(solution)/shard_map/ppermute | solution.py:228
  77.9 0.7 fusion.9
  78.6 2.5 %collective-permute-start.19 = (bf16[432,256]{1,0:T(8,128)(2,1)}, bf16[432,256]{1,0:T(8,128)(2,1)}, u32[]{:S(2)}, u32[]{:S(2)}) collective-permute-start(bf16[432,256]{1,0:T(8,128)(2,1)} %fusion.9), channel_id=1, source_target_pairs={{0,12},{1,13},{2,14},{3,15},{4,8},{5,9},{6,10},{7,11},{8,4},{9,5},... | collective-permute-start | bytes 663560 | tf_op jit(solution)/shard_map/ppermute | solution.py:228
  81.1 1.5 %collective-permute-done.21 = bf16[432,256]{1,0:T(8,128)(2,1)S(1)} collective-permute-done((bf16[432,256]{1,0:T(8,128)(2,1)S(1)}, bf16[432,256]{1,0:T(8,128)(2,1)S(1)}, u32[]{:S(2)}, u32[]{:S(2)}) %collective-permute-start.21) | collective-permute-done | bytes 221216 | tf_op jit(solution)/shard_map/ppermute | solution.py:228
  82.6 0.7 fusion.7
  83.4 0.8 collective-permute-start.22
  84.2 3.2 %collective-permute-done.24 = bf16[432,256]{1,0:T(8,128)(2,1)S(1)} collective-permute-done((bf16[432,256]{1,0:T(8,128)(2,1)S(1)}, bf16[432,256]{1,0:T(8,128)(2,1)S(1)}, u32[]{:S(2)}, u32[]{:S(2)}) %collective-permute-start.24) | collective-permute-done | bytes 221216 | tf_op jit(solution)/shard_map/ppermute | solution.py:228
  87.4 0.7 fusion.5
  88.1 8.0 %shard_map.78 = (bf16[512,256]{1,0:T(8,128)(2,1)S(1)}, bf16[512,256]{1,0:T(8,128)(2,1)S(1)}) custom-call(s32[1]{0:T(128)} %bitcast.flag_ref, s32[4]{0:T(128)S(1)} %bitcast.66, s32[16]{0:T(128)S(1)} %stack.86.place_ref, bf16[4,128,256]{2,1,0:T(8,128)(2,1)S(1)} %reshape.26.clips_ref, f32[1,256]{1,0:T(1,128)S(1)} %copy-done, ...), custom_call_target="tpu_custom_call" | custom-call | flops 1811939328 | bytes 3538944 | tf_op jit(solution)/shard_map/pallas_call | solution.py:336
  96.1 0.8 reshape.28
  96.9 0.8 reshape.29
  97.7 0.7 collective-permute-done.22
  98.4 0.7 collective-permute-done.25
  99.1 2.2 %fusion.3 = f32[1,432,256]{2,1,0:T(8,128)} fusion(f32[2,432,256]{2,1,0:T(8,128)S(1)} %copy-done.11, bf16[432,256]{1,0:T(8,128)(2,1)} %collective-permute-done.27, bf16[432,256]{1,0:T(8,128)(2,1)} %collective-permute-done.25, bf16[432,256]{1,0:T(8,128)(2,1)} %collective-permute-done.22, bf16[432,256]{1,0:T(8,128)(2,1)} %collective-permute-done.19), kind=kLoop, calls=%fused_computation.9 | loop fusion | flops 995328 | bytes 1769472 | tf_op jit(solution)/shard_map/broadcast_in_dim | solution.py:345
  (54 shorter events, 0.7 us)
Async XLA Ops:
  0.6 11.7 %collective-permute-start.11 = (bf16[432,256]{1,0:T(8,128)(2,1)}, bf16[432,256]{1,0:T(8,128)(2,1)S(1)}, u32[]{:S(2)}, u32[]{:S(2)}) collective-permute-start(bf16[432,256]{1,0:T(8,128)(2,1)} %bitcast.57), channel_id=1, source_target_pairs={{0,12},{1,13},{2,14},{3,15},{4,8},{5,9},{6,10},{7,11},{8,4},{9,5},... | collective-permute-start | bytes 663560 | tf_op jit(solution)/shard_map/ppermute | solution.py:228
  5.7 19.0 %collective-permute-start.7 = (bf16[432,256]{1,0:T(8,128)(2,1)}, bf16[432,256]{1,0:T(8,128)(2,1)S(1)}, u32[]{:S(2)}, u32[]{:S(2)}) collective-permute-start(bf16[432,256]{1,0:T(8,128)(2,1)} %bitcast.58), channel_id=1, source_target_pairs={{0,8},{1,9},{2,10},{3,11},{4,12},{5,13},{6,14},{7,15},{8,0},{9,1},... | collective-permute-start | bytes 663560 | tf_op jit(solution)/shard_map/ppermute | solution.py:228
  5.7 19.0 %collective-permute-start.3 = (bf16[432,256]{1,0:T(8,128)(2,1)}, bf16[432,256]{1,0:T(8,128)(2,1)S(1)}, u32[]{:S(2)}, u32[]{:S(2)}) collective-permute-start(bf16[432,256]{1,0:T(8,128)(2,1)} %bitcast.59), channel_id=1, source_target_pairs={{0,4},{1,5},{2,6},{3,7},{4,0},{5,1},{6,2},{7,3},{8,12},{9,13},{10,... | collective-permute-start | bytes 663560 | tf_op jit(solution)/shard_map/ppermute | solution.py:228
  6.4 19.9 %collective-permute-start.1 = (bf16[432,256]{1,0:T(8,128)(2,1)}, bf16[432,256]{1,0:T(8,128)(2,1)S(1)}, u32[]{:S(2)}, u32[]{:S(2)}) collective-permute-start(bf16[432,256]{1,0:T(8,128)(2,1)} %bitcast.60), channel_id=1, source_target_pairs={{0,2},{1,3},{2,0},{3,1},{4,6},{5,7},{6,4},{7,5},{8,10},{9,11},{10,... | collective-permute-start | bytes 663560 | tf_op jit(solution)/shard_map/ppermute | solution.py:228
  8.0 18.5 %collective-permute-start = (bf16[432,256]{1,0:T(8,128)(2,1)}, bf16[432,256]{1,0:T(8,128)(2,1)S(1)}, u32[]{:S(2)}, u32[]{:S(2)}) collective-permute-start(bf16[432,256]{1,0:T(8,128)(2,1)} %bitcast.61), channel_id=1, source_target_pairs={{0,1},{1,0},{2,3},{3,2},{4,5},{5,4},{6,7},{7,6},{8,9},{9,8},{10,11... | collective-permute-start | bytes 663560 | tf_op jit(solution)/shard_map/ppermute | solution.py:228
  12.4 14.7 %collective-permute-start.13 = (bf16[432,256]{1,0:T(8,128)(2,1)S(1)}, bf16[432,256]{1,0:T(8,128)(2,1)S(1)}, u32[]{:S(2)}, u32[]{:S(2)}) collective-permute-start(bf16[432,256]{1,0:T(8,128)(2,1)S(1)} %collective-permute-done.11.rest_12_), channel_id=1, source_target_pairs={{0,2},{1,3},{2,0},{3,1},{4,6},{5,7},{6,4},{7,5},{8,10},{9,11},{10,... | collective-permute-start | bytes 663560 | tf_op jit(solution)/shard_map/ppermute | solution.py:228
  24.8 2.3 %collective-permute-start.12 = (bf16[432,256]{1,0:T(8,128)(2,1)S(1)}, bf16[432,256]{1,0:T(8,128)(2,1)S(1)}, u32[]{:S(2)}, u32[]{:S(2)}) collective-permute-start(bf16[432,256]{1,0:T(8,128)(2,1)S(1)} %collective-permute-done.11.rest_12_), channel_id=1, source_target_pairs={{0,1},{1,0},{2,3},{3,2},{4,5},{5,4},{6,7},{7,6},{8,9},{9,8},{10,11... | collective-permute-start | bytes 663560 | tf_op jit(solution)/shard_map/ppermute | solution.py:228
  24.8 8.2 %collective-permute-start.9 = (bf16[432,256]{1,0:T(8,128)(2,1)S(1)}, bf16[432,256]{1,0:T(8,128)(2,1)S(1)}, u32[]{:S(2)}, u32[]{:S(2)}) collective-permute-start(bf16[432,256]{1,0:T(8,128)(2,1)S(1)} %collective-permute-done.7.rest_8_), channel_id=1, source_target_pairs={{0,2},{1,3},{2,0},{3,1},{4,6},{5,7},{6,4},{7,5},{8,10},{9,11},{10,... | collective-permute-start | bytes 663560 | tf_op jit(solution)/shard_map/ppermute | solution.py:228
  26.3 6.7 %collective-permute-start.8 = (bf16[432,256]{1,0:T(8,128)(2,1)S(1)}, bf16[432,256]{1,0:T(8,128)(2,1)S(1)}, u32[]{:S(2)}, u32[]{:S(2)}) collective-permute-start(bf16[432,256]{1,0:T(8,128)(2,1)S(1)} %collective-permute-done.7.rest_8_), channel_id=1, source_target_pairs={{0,1},{1,0},{2,3},{3,2},{4,5},{5,4},{6,7},{7,6},{8,9},{9,8},{10,11... | collective-permute-start | bytes 663560 | tf_op jit(solution)/shard_map/ppermute | solution.py:228
  26.5 10.9 %collective-permute-start.5 = (bf16[432,256]{1,0:T(8,128)(2,1)S(1)}, bf16[432,256]{1,0:T(8,128)(2,1)S(1)}, u32[]{:S(2)}, u32[]{:S(2)}) collective-permute-start(bf16[432,256]{1,0:T(8,128)(2,1)S(1)} %collective-permute-done.3.rest_4_), channel_id=1, source_target_pairs={{0,2},{1,3},{2,0},{3,1},{4,6},{5,7},{6,4},{7,5},{8,10},{9,11},{10,... | collective-permute-start | bytes 663560 | tf_op jit(solution)/shard_map/ppermute | solution.py:228
  27.0 12.6 %collective-permute-start.4 = (bf16[432,256]{1,0:T(8,128)(2,1)S(1)}, bf16[432,256]{1,0:T(8,128)(2,1)S(1)}, u32[]{:S(2)}, u32[]{:S(2)}) collective-permute-start(bf16[432,256]{1,0:T(8,128)(2,1)S(1)} %collective-permute-done.3.rest_4_), channel_id=1, source_target_pairs={{0,1},{1,0},{2,3},{3,2},{4,5},{5,4},{6,7},{7,6},{8,9},{9,8},{10,11... | collective-permute-start | bytes 663560 | tf_op jit(solution)/shard_map/ppermute | solution.py:228
  27.0 12.6 %collective-permute-start.2 = (bf16[432,256]{1,0:T(8,128)(2,1)S(1)}, bf16[432,256]{1,0:T(8,128)(2,1)S(1)}, u32[]{:S(2)}, u32[]{:S(2)}) collective-permute-start(bf16[432,256]{1,0:T(8,128)(2,1)S(1)} %collective-permute-done.1.rest_2_), channel_id=1, source_target_pairs={{0,1},{1,0},{2,3},{3,2},{4,5},{5,4},{6,7},{7,6},{8,9},{9,8},{10,11... | collective-permute-start | bytes 663560 | tf_op jit(solution)/shard_map/ppermute | solution.py:228
  33.0 7.3 %collective-permute-start.14 = (bf16[432,256]{1,0:T(8,128)(2,1)S(1)}, bf16[432,256]{1,0:T(8,128)(2,1)}, u32[]{:S(2)}, u32[]{:S(2)}) collective-permute-start(bf16[432,256]{1,0:T(8,128)(2,1)S(1)} %collective-permute-done.13.rest_14_), channel_id=1, source_target_pairs={{0,1},{1,0},{2,3},{3,2},{4,5},{5,4},{6,7},{7,6},{8,9},{9,8},{10,11... | collective-permute-start | bytes 663560 | tf_op jit(solution)/shard_map/ppermute | solution.py:228
  33.0 7.3 %collective-permute-start.10 = (bf16[432,256]{1,0:T(8,128)(2,1)S(1)}, bf16[432,256]{1,0:T(8,128)(2,1)}, u32[]{:S(2)}, u32[]{:S(2)}) collective-permute-start(bf16[432,256]{1,0:T(8,128)(2,1)S(1)} %collective-permute-done.9.rest_10_), channel_id=1, source_target_pairs={{0,1},{1,0},{2,3},{3,2},{4,5},{5,4},{6,7},{7,6},{8,9},{9,8},{10,11... | collective-permute-start | bytes 663560 | tf_op jit(solution)/shard_map/ppermute | solution.py:228
  37.3 3.0 %copy-start.2 = (bf16[432,256]{1,0:T(8,128)(2,1)}, bf16[432,256]{1,0:T(8,128)(2,1)S(1)}, u32[]{:S(2)}) copy-start(bf16[432,256]{1,0:T(8,128)(2,1)S(1)} %collective-permute-done.5.rest_6_) | copy-start | bytes 663556
  37.3 3.0 %collective-permute-start.6 = (bf16[432,256]{1,0:T(8,128)(2,1)S(1)}, bf16[432,256]{1,0:T(8,128)(2,1)}, u32[]{:S(2)}, u32[]{:S(2)}) collective-permute-start(bf16[432,256]{1,0:T(8,128)(2,1)S(1)} %collective-permute-done.5.rest_6_), channel_id=1, source_target_pairs={{0,1},{1,0},{2,3},{3,2},{4,5},{5,4},{6,7},{7,6},{8,9},{9,8},{10,11... | collective-permute-start | bytes 663560 | tf_op jit(solution)/shard_map/ppermute | solution.py:228
  38.4 1.9 %copy-start.1 = (bf16[1,432,256]{2,1,0:T(8,128)(2,1)S(1)}, bf16[1,432,256]{2,1,0:T(8,128)(2,1)}, u32[]{:S(2)}) copy-start(bf16[1,432,256]{2,1,0:T(8,128)(2,1)} %param.8) | copy-start | bytes 663556
  39.6 0.7 copy-start.6
  40.3 0.7 copy-start
  40.4 0.7 copy-start.9
  41.0 0.9 copy-start.7
  49.7 0.7 copy-start.4
  50.4 8.7 %collective-permute-start.15 = (bf16[512,256]{1,0:T(8,128)(2,1)S(1)}, bf16[512,256]{1,0:T(8,128)(2,1)S(1)}, u32[]{:S(2)}, u32[]{:S(2)}) collective-permute-start(bf16[512,256]{1,0:T(8,128)(2,1)S(1)} %shard_map.76.mine_ref), channel_id=1, source_target_pairs={{0,16},{16,0},{1,17},{17,1},{2,18},{18,2},{3,19},{19,3},{4,20},{20... | collective-permute-start | bytes 786440 | tf_op jit(solution)/shard_map/ppermute | solution.py:228
  52.0 7.2 %collective-permute-start.16 = (f32[1,256]{1,0:T(1,128)S(1)}, f32[1,256]{1,0:T(1,128)S(1)}, u32[]{:S(2)}, u32[]{:S(2)}) collective-permute-start(f32[1,256]{1,0:T(1,128)S(1)} %copy-done), channel_id=1, source_target_pairs={{0,16},{16,0},{1,17},{17,1},{2,18},{18,2},{3,19},{19,3},{4,20},{20... | collective-permute-start | bytes 3080 | tf_op jit(solution)/shard_map/ppermute | solution.py:228
  67.6 1.9 %collective-permute-start.17 = (bf16[2,432,256]{2,1,0:T(8,128)(2,1)S(1)}, bf16[2,432,256]{2,1,0:T(8,128)(2,1)S(1)}, u32[]{:S(2)}, u32[]{:S(2)}) collective-permute-start(bf16[2,432,256]{2,1,0:T(8,128)(2,1)S(1)} %get-tuple-element.18), channel_id=1, source_target_pairs={{0,1},{1,0},{2,3},{3,2},{4,5},{5,4},{6,7},{7,6},{8,9},{9,8},{10,11... | collective-permute-start | bytes 1327112 | tf_op jit(solution)/shard_map/ppermute | solution.py:228
  67.6 3.5 %collective-permute-start.20 = (bf16[2,432,256]{2,1,0:T(8,128)(2,1)S(1)}, bf16[2,432,256]{2,1,0:T(8,128)(2,1)S(1)}, u32[]{:S(2)}, u32[]{:S(2)}) collective-permute-start(bf16[2,432,256]{2,1,0:T(8,128)(2,1)S(1)} %get-tuple-element.20), channel_id=1, source_target_pairs={{0,1},{1,0},{2,3},{3,2},{4,5},{5,4},{6,7},{7,6},{8,9},{9,8},{10,11... | collective-permute-start | bytes 1327112 | tf_op jit(solution)/shard_map/ppermute | solution.py:228
  68.1 3.7 %collective-permute-start.23 = (bf16[2,432,256]{2,1,0:T(8,128)(2,1)S(1)}, bf16[2,432,256]{2,1,0:T(8,128)(2,1)S(1)}, u32[]{:S(2)}, u32[]{:S(2)}) collective-permute-start(bf16[2,432,256]{2,1,0:T(8,128)(2,1)S(1)} %get-tuple-element.22), channel_id=1, source_target_pairs={{0,1},{1,0},{2,3},{3,2},{4,5},{5,4},{6,7},{7,6},{8,9},{9,8},{10,11... | collective-permute-start | bytes 1327112 | tf_op jit(solution)/shard_map/ppermute | solution.py:228
  68.2 5.3 %collective-permute-start.26 = (bf16[2,432,256]{2,1,0:T(8,128)(2,1)S(1)}, bf16[2,432,256]{2,1,0:T(8,128)(2,1)S(1)}, u32[]{:S(2)}, u32[]{:S(2)}) collective-permute-start(bf16[2,432,256]{2,1,0:T(8,128)(2,1)S(1)} %get-tuple-element.24), channel_id=1, source_target_pairs={{0,1},{1,0},{2,3},{3,2},{4,5},{5,4},{6,7},{7,6},{8,9},{9,8},{10,11... | collective-permute-start | bytes 1327112 | tf_op jit(solution)/shard_map/ppermute | solution.py:228
  69.5 8.3 %collective-permute-start.18 = (bf16[432,256]{1,0:T(8,128)(2,1)S(1)}, bf16[432,256]{1,0:T(8,128)(2,1)S(1)}, u32[]{:S(2)}, u32[]{:S(2)}) collective-permute-start(bf16[432,256]{1,0:T(8,128)(2,1)S(1)} %fusion.10), channel_id=1, source_target_pairs={{0,2},{1,3},{2,0},{3,1},{4,6},{5,7},{6,4},{7,5},{8,10},{9,11},{10,... | collective-permute-start | bytes 663560 | tf_op jit(solution)/shard_map/ppermute | solution.py:228
  71.2 11.4 %collective-permute-start.21 = (bf16[432,256]{1,0:T(8,128)(2,1)S(1)}, bf16[432,256]{1,0:T(8,128)(2,1)S(1)}, u32[]{:S(2)}, u32[]{:S(2)}) collective-permute-start(bf16[432,256]{1,0:T(8,128)(2,1)S(1)} %fusion.11), channel_id=1, source_target_pairs={{0,2},{1,3},{2,0},{3,1},{4,6},{5,7},{6,4},{7,5},{8,10},{9,11},{10,... | collective-permute-start | bytes 663560 | tf_op jit(solution)/shard_map/ppermute | solution.py:228
  72.0 15.4 %collective-permute-start.24 = (bf16[432,256]{1,0:T(8,128)(2,1)S(1)}, bf16[432,256]{1,0:T(8,128)(2,1)S(1)}, u32[]{:S(2)}, u32[]{:S(2)}) collective-permute-start(bf16[432,256]{1,0:T(8,128)(2,1)S(1)} %fusion.12), channel_id=1, source_target_pairs={{0,2},{1,3},{2,0},{3,1},{4,6},{5,7},{6,4},{7,5},{8,10},{9,11},{10,... | collective-permute-start | bytes 663560 | tf_op jit(solution)/shard_map/ppermute | solution.py:228
  73.7 9.0 %copy-start.10 = (f32[2,432,256]{2,1,0:T(8,128)}, f32[2,432,256]{2,1,0:T(8,128)S(1)}, u32[]{:S(2)}) copy-start(f32[2,432,256]{2,1,0:T(8,128)S(1)} %convert_add_fusion) | copy-start | bytes 2654212
  74.4 23.3 %collective-permute-start.27 = (bf16[432,256]{1,0:T(8,128)(2,1)}, bf16[432,256]{1,0:T(8,128)(2,1)}, u32[]{:S(2)}, u32[]{:S(2)}) collective-permute-start(bf16[432,256]{1,0:T(8,128)(2,1)} %fusion.13), channel_id=1, source_target_pairs={{0,2},{1,3},{2,0},{3,1},{4,6},{5,7},{6,4},{7,5},{8,10},{9,11},{10,... | collective-permute-start | bytes 663560 | tf_op jit(solution)/shard_map/ppermute | solution.py:228
  78.6 19.1 %collective-permute-start.19 = (bf16[432,256]{1,0:T(8,128)(2,1)}, bf16[432,256]{1,0:T(8,128)(2,1)}, u32[]{:S(2)}, u32[]{:S(2)}) collective-permute-start(bf16[432,256]{1,0:T(8,128)(2,1)} %fusion.9), channel_id=1, source_target_pairs={{0,12},{1,13},{2,14},{3,15},{4,8},{5,9},{6,10},{7,11},{8,4},{9,5},... | collective-permute-start | bytes 663560 | tf_op jit(solution)/shard_map/ppermute | solution.py:228
  83.4 4.8 %copy-start.3 = (bf16[432,256]{1,0:T(8,128)(2,1)S(1)}, bf16[432,256]{1,0:T(8,128)(2,1)}, u32[]{:S(2)}) copy-start(bf16[432,256]{1,0:T(8,128)(2,1)} %copy-done.2) | copy-start | bytes 663556
  83.4 4.8 %copy-start.5 = (bf16[432,256]{1,0:T(8,128)(2,1)S(1)}, bf16[432,256]{1,0:T(8,128)(2,1)}, u32[]{:S(2)}) copy-start(bf16[432,256]{1,0:T(8,128)(2,1)} %copy-done.4) | copy-start | bytes 663556
  83.4 4.8 %copy-start.8 = (bf16[432,256]{1,0:T(8,128)(2,1)S(1)}, bf16[432,256]{1,0:T(8,128)(2,1)}, u32[]{:S(2)}) copy-start(bf16[432,256]{1,0:T(8,128)(2,1)} %copy-done.6) | copy-start | bytes 663556
  83.4 15.0 %collective-permute-start.22 = (bf16[432,256]{1,0:T(8,128)(2,1)}, bf16[432,256]{1,0:T(8,128)(2,1)}, u32[]{:S(2)}, u32[]{:S(2)}) collective-permute-start(bf16[432,256]{1,0:T(8,128)(2,1)} %fusion.7), channel_id=1, source_target_pairs={{0,8},{1,9},{2,10},{3,11},{4,12},{5,13},{6,14},{7,15},{8,0},{9,1},... | collective-permute-start | bytes 663560 | tf_op jit(solution)/shard_map/ppermute | solution.py:228
  88.1 11.0 %collective-permute-start.25 = (bf16[432,256]{1,0:T(8,128)(2,1)}, bf16[432,256]{1,0:T(8,128)(2,1)}, u32[]{:S(2)}, u32[]{:S(2)}) collective-permute-start(bf16[432,256]{1,0:T(8,128)(2,1)} %fusion.5), channel_id=1, source_target_pairs={{0,4},{1,5},{2,6},{3,7},{4,0},{5,1},{6,2},{7,3},{8,12},{9,13},{10,... | collective-permute-start | bytes 663560 | tf_op jit(solution)/shard_map/ppermute | solution.py:228
  96.1 3.0 %copy-start.11 = (f32[2,432,256]{2,1,0:T(8,128)S(1)}, f32[2,432,256]{2,1,0:T(8,128)}, u32[]{:S(2)}) copy-start(f32[2,432,256]{2,1,0:T(8,128)} %copy-done.10) | copy-start | bytes 2654212

commit v2 on v0

v2 whole, which is shorter than its diff:
```python
import functools
import math

import jax
import jax.numpy as jnp
from jax import lax
from jax.experimental import pallas as pl
from jax.experimental.pallas import tpu as pltpu
from jax.sharding import PartitionSpec as P

EPSILON = 1e-06
ROW_TILE = 16
VMEM_LIMIT = 20 * 1024 * 1024
LAST_VMEM_LIMIT = 24 * 1024 * 1024


def normalize(values, gain_row):
    inverse = lax.rsqrt(jnp.mean(values * values, axis=-1, keepdims=True) + EPSILON)
    return inverse, values * inverse * gain_row


def activate(values, gain_row):
    inverse, normed = normalize(values, gain_row)
    return jnp.maximum(normed, 0.0).astype(jnp.bfloat16)


def back(values, upstream, spread, gain_row):
    inverse, normed = normalize(values, gain_row)
    scaled = gain_row * jnp.where(normed > 0.0, spread, 0.0)
    mixing = jnp.mean(values * scaled, axis=-1, keepdims=True)
    return upstream + inverse * scaled - values * (inverse * inverse * inverse) * mixing


def fill_columns(cols_ref, values, dims):
    micro, frames, height, width, channels = dims
    plane = height * width
    voxels = frames * plane
    total = micro * voxels
    row = lax.broadcasted_iota(jnp.int32, (plane, channels), 0)
    across = row % width
    down = row // width
    zero = jnp.zeros((micro, plane, cols_ref.shape[2]), jnp.bfloat16)
    cols_ref[:, :plane, :] = zero
    cols_ref[:, plane + voxels :, :] = zero

    def masked(rolled, inside):
        kept = rolled.reshape(total // plane, plane, channels) * inside.astype(jnp.float32)[None]
        return kept.reshape(total, channels)

    for by_w in (-1, 0, 1):
        if by_w == 0:
            along = values
        else:
            inside = (across + by_w >= 0) & (across + by_w < width)
            along = masked(pltpu.roll(values, (-by_w) % total, 0), inside)
        for by_h in (-1, 0, 1):
            if by_h == 0:
                moved = along
            else:
                inside = (down + by_h >= 0) & (down + by_h < height)
                moved = masked(pltpu.roll(along, (-by_h * width) % total, 0), inside)
            j = 3 * (by_h + 1) + by_w + 1
            cols_ref[:, plane : plane + voxels, j * channels : (j + 1) * channels] = moved.astype(
                jnp.bfloat16
            ).reshape(micro, voxels, channels)


def frame_columns(cols_ref, by_t, dims, begin, end):
    micro, frames, height, width, channels = dims
    plane = height * width
    voxels = frames * plane
    start = plane * (by_t + 1)
    return cols_ref[:, start : start + voxels, begin:end].reshape(micro * voxels, end - begin)


def half_pieces(half, dims):
    channels = dims[4]
    middle = channels // 2
    parts = []
    at = 0
    for k in range(14) if half == 0 else range(13, 27):
        low, high = 0, channels
        if k == 13:
            low, high = (0, middle) if half == 0 else (middle, channels)
        parts.append((k, low, high, at))
        at += high - low
    return parts


def half_forward(cols_ref, weight_ref, dims, half):
    channels = dims[4]
    middle = 9 * channels // 2
    if half == 0:
        runs = ((-1, 0, 2 * middle, 0), (0, 0, middle, 2 * middle))
    else:
        runs = ((0, middle, 2 * middle, 0), (1, 0, 2 * middle, middle))
    terms = [
        jnp.dot(
            frame_columns(cols_ref, by_t, dims, begin, end),
            weight_ref[at : at + end - begin, :],
            preferred_element_type=jnp.float32,
        )
        for by_t, begin, end, at in runs
    ]
    return terms[0] + terms[1]


def half_spread(cols_ref, weight_ref, dims, half):
    channels = dims[4]
    total, partial = None, None
    for k, low, high, at in half_pieces(half, dims):
        by_t, j = (26 - k) // 9 - 1, (26 - k) % 9
        term = lax.dot_general(
            frame_columns(cols_ref, by_t, dims, j * channels, (j + 1) * channels),
            weight_ref[at : at + high - low, :],
            (((1,), (1,)), ((), ())),
            preferred_element_type=jnp.float32,
        )
        if high - low < channels:
            partial = term
        else:
            total = term if total is None else total + term
    middle = channels // 2
    if half == 0:
        return jnp.concatenate([total[:, :middle] + partial, total[:, middle:]], axis=1)
    return jnp.concatenate([total[:, :middle], total[:, middle:] + partial], axis=1)


def half_gradient(turned_ref, cols_ref, sums_ref, dims, half):
    channels = dims[4]
    for k, low, high, at in half_pieces(half, dims):
        by_t, j = (26 - k) // 9 - 1, (26 - k) % 9
        sums_ref[at : at + high - low, :] = jnp.dot(
            turned_ref[low:high, :],
            frame_columns(cols_ref, by_t, dims, j * channels, (j + 1) * channels),
            preferred_element_type=jnp.float32,
        ).astype(jnp.bfloat16)


def where_am_i(split):
    place = lax.axis_index("fsdp")
    near = place // (lax.axis_size("fsdp") // 2) if split else 0
    return lax.axis_index("section"), place, near


def lay_pieces(place, pieces, weight_ref):
    if len(pieces) == 1:
        weight_ref[...] = pieces[0][...]
        return
    for by, piece in enumerate(pieces):
        rows = piece.shape[0]
        start = pl.multiple_of(((place ^ by) % len(pieces)) * rows, ROW_TILE)
        weight_ref[pl.ds(start, rows), :] = piece[...]


def take_clips(plan_ref, clips_ref, dims):
    picked = [clips_ref[plan_ref[m]] for m in range(dims[0])]
    return jnp.concatenate(picked, axis=0).astype(jnp.float32)


def on_half(section, half, run):
    for at in (0, 1):
        for part in (0, 1):

            @pl.when((section == at) & (half == part))
            def _(at=at, part=part):
                run(at, part)


def fetch(pairs, sems):
    copies = [pltpu.make_async_copy(source, target, sems.at[at]) for at, (source, target) in enumerate(pairs)]
    for copy in copies:
        copy.start()
    return copies


def wait_all(copies):
    for copy in copies:
        copy.wait()


def prepare_kernel(dims, split, plan_ref, clips_ref, cotangent_ref, gain_ref, early_ref, cols_ref, token_ref):
    section, place, near = where_am_i(split)
    total = dims[0] * dims[1] * dims[2] * dims[3]
    active = activate(take_clips(plan_ref, clips_ref, dims), gain_ref[...])
    upstream = cotangent_ref[...].reshape(total, dims[4]).astype(jnp.float32)
    fill_columns(cols_ref, jnp.where(section == 0, active.astype(jnp.float32), upstream), dims)
    token_ref[...] = jnp.zeros_like(token_ref)


def near_kernel(dims, split, count, cols_ref, early_ref, *rest):
    pieces, (out_ref, token_ref, kept_ref, weight_ref, sems) = rest[:count], rest[count:]
    section, place, near = where_am_i(split)
    lay_pieces(place, pieces, weight_ref)
    copies = fetch([(weight_ref, kept_ref)], sems)

    def run(at, part):
        conv = half_forward if at == 0 else half_spread
        out_ref[...] = conv(cols_ref, weight_ref, dims, part)

    on_half(section, near, run)
    token_ref[...] = early_ref[...]
    wait_all(copies)


def far_kernel(dims, split, count, plan_ref, clips_ref, early_ref, cols_ref, base_ref, *rest):
    pieces, (out_ref, kept_ref, weight_ref, held_ref, sems) = rest[:count], rest[count:]
    section, place, near = where_am_i(split)
    arriving = fetch([(clips_ref, held_ref)], sems)
    lay_pieces(place, pieces, weight_ref)
    leaving = pltpu.make_async_copy(weight_ref, kept_ref, sems.at[1])
    leaving.start()
    wait_all(arriving)

    def run(at, part):
        conv = half_forward if at == 0 else half_spread
        value = base_ref[...] + conv(cols_ref, weight_ref, dims, part)
        if at == 0:
            value = value + take_clips(plan_ref, held_ref, dims)
        out_ref[...] = value.astype(jnp.bfloat16)

    on_half(section, 1 - near, run)
    leaving.wait()


def hand_out(place, ways, sums_ref, outs):
    if not ways:
        outs[0][...] = sums_ref[...]
        return
    rows = outs[0].shape[1]
    for at, out in enumerate(outs):
        for inner in (0, 1):
            owner = (place ^ (ways[at // 2] + at % 2 + 2 * inner)) % (sums_ref.shape[0] // rows)
            out[inner] = sums_ref[pl.ds(pl.multiple_of(owner * rows, ROW_TILE), rows), :]


def gradient_kernel(dims, split, plan_ref, clips_ref, cotangent_ref, gain_ref, last_gain_ref, mine_ref, theirs_ref,
                    early_cols_ref, grad_ref, hidden_ref, turned_ref, cols_ref, *rest):
    outs = rest[:-6]
    sums_ref, held_clips, held_cotangent, held_gain, held_last, sems = rest[-6:]
    section, place, near = where_am_i(split)
    channels = dims[4]
    total = dims[0] * dims[1] * dims[2] * dims[3]
    arriving = fetch(
        [
            (cotangent_ref, held_cotangent),
            (last_gain_ref, held_last),
            (clips_ref, held_clips),
            (gain_ref, held_gain),
        ],
        sems,
    )
    leading = section == 0
    mine = mine_ref[...].astype(jnp.float32)
    theirs = theirs_ref[...].astype(jnp.float32)
    hidden = jnp.where(leading, mine, theirs)
    spread = jnp.where(leading, theirs, mine)
    hidden_ref[...] = hidden.astype(jnp.bfloat16)
    wait_all(arriving)
    cotangent = held_cotangent[...].reshape(total, channels).astype(jnp.float32)
    upstream = back(hidden, cotangent, spread, held_last[...]).astype(jnp.bfloat16)
    grad_ref[...] = upstream
    unit = jnp.where(leading, take_clips(plan_ref, held_clips, dims), hidden)
    turned_ref[...] = activate(unit, held_gain[...]).T

    @pl.when(leading)
    def _():
        fill_columns(cols_ref, upstream.astype(jnp.float32), dims)

    @pl.when(jnp.logical_not(leading))
    def _():
        cols_ref[...] = early_cols_ref[...]

    for part in (0, 1):

        @pl.when(near != part)
        def _(part=part):
            half_gradient(turned_ref, cols_ref, sums_ref, dims, part)

    hand_out(place, (12, 8) if split else (), sums_ref, outs)


def rest_kernel(dims, split, turned_ref, cols_ref, *rest):
    outs, sums_ref = rest[:-1], rest[-1]
    section, place, near = where_am_i(split)
    for part in (0, 1):

        @pl.when(near == part)
        def _(part=part):
            half_gradient(turned_ref, cols_ref, sums_ref, dims, part)

    hand_out(place, (4, 0) if split else (), sums_ref, outs)


def last_kernel(dims, split, plan_ref, clips_ref, gain_ref, hidden_ref, grad_ref, near_ref, far_ref, acts_ref,
                grads_ref, weight_ref, cols_ref, held_clips, held_gain, held_hidden, held_grad, sems):
    section, place, near = where_am_i(split)
    half_rows = weight_ref.shape[0] // 2
    first = pl.multiple_of(near * half_rows, ROW_TILE) if split else 0
    second = pl.multiple_of((1 - near) * half_rows, ROW_TILE) if split else half_rows
    arriving = fetch(
        [
            (near_ref, weight_ref.at[pl.ds(first, half_rows)]),
            (far_ref, weight_ref.at[pl.ds(second, half_rows)]),
            (hidden_ref, held_hidden),
            (grad_ref, held_grad),
            (gain_ref, held_gain),
            (clips_ref, held_clips),
        ],
        sems,
    )
    wait_all(arriving)
    halves = weight_ref.at[pl.ds(0, half_rows)], weight_ref.at[pl.ds(half_rows, half_rows)]
    gain_row = held_gain[...]

    @pl.when(section == 0)
    def _():
        upstream = held_grad[...].astype(jnp.float32)
        fill_columns(cols_ref, upstream, dims)
        spread = half_spread(cols_ref, halves[0], dims, 0) + half_spread(cols_ref, halves[1], dims, 1)
        ordered = take_clips(plan_ref, held_clips, dims)
        grads_ref[...] = back(ordered, upstream, spread, gain_row).astype(jnp.bfloat16)
        acts_ref[...] = held_hidden[...]

    @pl.when(section != 0)
    def _():
        hidden = held_hidden[...].astype(jnp.float32)
        fill_columns(cols_ref, activate(hidden, gain_row).astype(jnp.float32), dims)
        branch = half_forward(cols_ref, halves[0], dims, 0) + half_forward(cols_ref, halves[1], dims, 1)
        acts_ref[...] = (hidden + branch).astype(jnp.bfloat16)
        grads_ref[...] = held_grad[...]


def swap(value, axis, by):
    return lax.ppermute(value, axis, [(i, i ^ by) for i in range(lax.axis_size(axis))])


def widen(value):
    return value.astype(jnp.float32)


def narrow(value):
    return value.astype(jnp.bfloat16)


def together(*values):
    return lax.optimization_barrier(values)


def on_device(clips, plan, gains, weights, cotangent):
    section = lax.axis_index("section")
    peers = lax.axis_size("fsdp")
    micro, frames, height, width, channels = clips.shape
    dims = clips.shape
    voxels = frames * height * width
    total = micro * voxels
    rows = weights.shape[1]
    all_rows = rows * peers
    half_rows = all_rows // 2
    factor = 1.0 / math.sqrt(peers * total)
    order = plan[0]
    flat_clips = clips.reshape(micro, voxels, channels)
    flat_cotangent = cotangent.reshape(micro, voxels, channels)
    split = peers == 16 and rows % ROW_TILE == 0

    smem = pl.BlockSpec(memory_space=pltpu.SMEM)
    vmem = pl.BlockSpec(memory_space=pltpu.VMEM)
    anywhere = pl.BlockSpec(memory_space=pl.ANY)
    half_weight = pltpu.VMEM((half_rows, channels), jnp.bfloat16)
    clips_scratch = pltpu.VMEM((micro, voxels, channels), jnp.bfloat16)
    volume_scratch = pltpu.VMEM((total, channels), jnp.bfloat16)
    gain_scratch = pltpu.VMEM((1, channels), jnp.float32)
    cols_shape = (micro, voxels + 2 * height * width, 9 * channels)
    volume = jax.ShapeDtypeStruct((total, channels), jnp.bfloat16)
    turned_out = jax.ShapeDtypeStruct((channels, total), jnp.bfloat16)
    cols_out = jax.ShapeDtypeStruct(cols_shape, jnp.bfloat16)
    half_out = jax.ShapeDtypeStruct((half_rows, channels), jnp.bfloat16)
    token_out = jax.ShapeDtypeStruct((8, 128), jnp.float32)

    def call(kernel, share, *, limit=VMEM_LIMIT, **config):
        flops = int(2 * total * all_rows * channels * share)
        return pl.pallas_call(
            functools.partial(kernel, dims, split),
            compiler_params=pltpu.CompilerParams(vmem_limit_bytes=limit),
            cost_estimate=pl.CostEstimate(flops=flops, bytes_accessed=2 * all_rows * channels, transcendentals=0),
            **config,
        )

    other_gain = swap(gains, "section", 1)
    last_gain = jnp.where(section == 0, other_gain, gains)

    early_cols, token = call(
        prepare_kernel,
        0.2,
        out_shape=[cols_out, token_out],
        in_specs=[smem] + [vmem] * 3 + [anywhere],
        out_specs=[vmem] * 2,
    )(order, flat_clips, flat_cotangent, gains, last_gain)

    own = weights[0]
    if split:
        held = {0: own}
        held[2] = swap(own, "fsdp", 2)
        held[4] = swap(own, "fsdp", 4)
        held[8] = swap(own, "fsdp", 8)
        held[4], held[2], token = together(held[4], held[2], token)
        held[6] = swap(held[4], "fsdp", 2)
        held[12] = swap(held[8], "fsdp", 4)
        held[8], held[6] = together(held[8], held[6])
        held[10] = swap(held[8], "fsdp", 2)
        held[14] = swap(held[12], "fsdp", 2)
        for by in (0, 2, 4, 6):
            held[by + 1] = swap(held[by], "fsdp", 1)
        near = [held[by] for by in range(8)]
    else:
        full = lax.all_gather(own, "fsdp", axis=0, tiled=True)
        near, far = [full[:half_rows]], [full[half_rows:]]
    count = len(near)

    base, token, near_weight = call(
        lambda dims, split, *refs: near_kernel(dims, split, count, *refs),
        0.5,
        out_shape=[jax.ShapeDtypeStruct((total, channels), jnp.float32), token_out, half_out],
        in_specs=[vmem] * (2 + count),
        out_specs=[vmem] * 2 + [anywhere],
        scratch_shapes=[half_weight, pltpu.SemaphoreType.DMA((1,))],
    )(early_cols, token, *near)

    if split:
        held[14], token = together(held[14], token)
        for by in (8, 10, 12, 14):
            held[by + 1] = swap(held[by], "fsdp", 1)
        far = [held[by] for by in range(8, 16)]

    mine, far_weight = call(
        lambda dims, split, *refs: far_kernel(dims, split, count, *refs),
        0.5,
        out_shape=[volume, half_out],
        in_specs=[smem] + [anywhere] * 2 + [vmem] * (2 + count),
        out_specs=[vmem, anywhere],
        scratch_shapes=[half_weight, clips_scratch, pltpu.SemaphoreType.DMA((2,))],
    )(order, flat_clips, token, early_cols, base, *far)

    theirs = swap(mine, "section", 1)

    shapes = [jax.ShapeDtypeStruct((2, rows, channels), jnp.bfloat16)] * 4 if split else [half_out]
    grad, hidden, turned, late_cols, *far_sums = call(
        gradient_kernel,
        0.5,
        out_shape=[volume, volume, turned_out, cols_out] + shapes,
        in_specs=[smem] + [anywhere] * 4 + [vmem] * 3,
        out_specs=[vmem] * (4 + len(shapes)),
        scratch_shapes=[
            half_weight,
            clips_scratch,
            clips_scratch,
            gain_scratch,
            gain_scratch,
            pltpu.SemaphoreType.DMA((4,)),
        ],
    )(order, flat_clips, flat_cotangent, gains, last_gain, mine, theirs, early_cols)

    near_sums = call(
        rest_kernel,
        0.5,
        out_shape=shapes,
        in_specs=[vmem] * 2,
        out_specs=[vmem] * len(shapes),
        scratch_shapes=[half_weight],
    )(turned, late_cols)

    if split:

        def core_sum(kept, sent):
            both = widen(kept) + widen(swap(sent, "fsdp", 1))
            return both[0], narrow(both[1])

        kept_12, send_12 = core_sum(*far_sums[:2])
        kept_8, send_8 = core_sum(*far_sums[2:])
        kept_4, send_4 = core_sum(*near_sums[:2])
        kept_0, send_0 = core_sum(*near_sums[2:])
        came_12 = swap(send_12, "fsdp", 2)
        came_12, send_8 = together(came_12, send_8)
        came_8 = swap(send_8, "fsdp", 2)
        from_4 = swap(narrow(kept_12 + widen(came_12)), "fsdp", 4)
        came_8, send_4 = together(came_8, send_4)
        came_4 = swap(send_4, "fsdp", 2)
        ready = narrow(kept_8 + widen(came_8) + widen(from_4))
        from_8 = swap(ready, "fsdp", 8)
        came_4, send_0 = together(came_4, send_0)
        came_0 = swap(send_0, "fsdp", 2)
        late = swap(narrow(kept_4 + widen(came_4)), "fsdp", 4)
        weight_grad = (kept_0 + widen(came_0) + widen(late) + widen(from_8)) * factor
        grad, _ = together(grad, ready)
    else:
        summed = widen(jnp.concatenate([near_sums[0], far_sums[0]], axis=0))
        weight_grad = lax.psum_scatter(summed, "fsdp", scatter_dimension=0, tiled=True) * factor

    acts, grads = call(
        last_kernel,
        1.0,
        limit=LAST_VMEM_LIMIT,
        out_shape=[volume, volume],
        in_specs=[smem] + [anywhere] * 6,
        out_specs=[vmem, vmem],
        scratch_shapes=[
            pltpu.VMEM((all_rows, channels), jnp.bfloat16),
            pltpu.VMEM(cols_shape, jnp.bfloat16),
            clips_scratch,
            gain_scratch,
            volume_scratch,
            volume_scratch,
            pltpu.SemaphoreType.DMA((6,)),
        ],
    )(order, flat_clips, gains, hidden, grad, near_weight, far_weight)
    return (acts.reshape(1, *dims), grads.reshape(1, *dims), weight_grad[None])


def solution(mesh):
    placed = (
        P("fsdp", None, None, None, None),
        P("fsdp", None),
        P("section", None),
        P("section", "fsdp", None),
        P("fsdp", None, None, None, None),
    )
    return jax.shard_map(
        on_device,
        mesh=mesh,
        in_specs=placed,
        out_specs=(
            P("section", "fsdp", None, None, None, None),
            P("section", "fsdp", None, None, None, None),
            P("section", "fsdp", None),
        ),
        check_vma=False,
    )
```

time: 325 us -> 83.7 us (0.26)
  local copies, waits for them, and re-layouts: 118 us -> 5.94 us
  waiting for transfers between devices: 126 us -> 43.5 us
  matrix products: 41.5 us -> 0 us
  starting transfers between devices: 4.78 us -> 18.5 us
  between operations: 14.2 us -> 0.82 us
  Pallas kernels: 0 us -> 13.2 us
  other arithmetic: 14.6 us -> 1.46 us
  loops' own time: 4.48 us -> 0 us
    while x549 -> x0, local copies, waits for them, and re-layouts: 96 us -> none
    reduce_scatter x1 -> x0, waiting for transfers between devices: 74.2 us -> none  [on_device(): lax.psum_scatter(summed, 'fsdp', scatter_dimension=0, tiled=True)]
    all_gather x1 -> x0, waiting for transfers between devices: 49.9 us -> none  [on_device(): full_weight = lax.all_gather(weights[0], 'fsdp', axis=0, tiled=True)]
    ppermute x2 -> x28, waiting for transfers between devices: 1.65 us -> 43.5 us  [swap(): lax.ppermute(value, axis, [(i, i ^ by) for i in range(lax.axis_size(axis))])]
    dot_general x20 -> x0, matrix products: 41.5 us -> none  [the longest x4 25.3 us: weight_term(): lax.dot_general(columns, flattened, (((0,), (0,)), ((), ())), preferred_e...]
    ppermute x2 -> x28, starting transfers between devices: 4.7 us -> 18.5 us  [swap(): lax.ppermute(value, axis, [(i, i ^ by) for i in range(lax.axis_size(axis))])]
    pallas_call x0 -> x6, Pallas kernels: none -> 13.2 us  [the longest x1 3.69 us: on_device(): call(last_kernel, 1.0, limit=LAST_VMEM_LIMIT, out_shape=[volume, volume],...]
    reshape x8 -> x4, local copies, waits for them, and re-layouts: 11.7 us -> 3.57 us  [the longest x2 1.53 us: on_device(): return (acts.reshape(1, *dims), grads.reshape(1, *dims), weight_grad[None])]
  transfers between devices with their start and end apart: 4 -> 28, of which waited for: 3 -> 16; matrix products, arithmetic and copies ran while one was open for 6% -> 5% of each run, Pallas kernels for 0% -> 9%
where the time goes in v2:
time: 83.7 us; the launch traced here: 83.5 us
  waiting for transfers between devices  43.5 us (52%)
  starting transfers between devices  18.5 us (22%)
  Pallas kernels  13.2 us (16%)
  local copies, waits for them, and re-layouts  5.94 us (7%)
  other arithmetic  1.46 us (2%)
    ppermute x28, waiting for transfers between devices, swap(): lax.ppermute(value, axis, [(i, i ^ by) for i in range(lax.axis_size(axis))])  43.5 us
    ppermute x28, starting transfers between devices, swap(): lax.ppermute(value, axis, [(i, i ^ by) for i in range(lax.axis_size(axis))])  18.5 us
    pallas_call x1, Pallas kernels, on_device(): call(last_kernel, 1.0, limit=LAST_VMEM_LIMIT, out_shape=[volume, volume],...  3.69 us
    pallas_call x1, Pallas kernels, on_device(): call(gradient_kernel, 0.5, out_shape=[volume, volume, turned_out, cols_ou...  3.17 us
    unnamed x10, local copies, waits for them, and re-layouts  2.28 us
    pallas_call x1, Pallas kernels, on_device(): call(lambda dims, split, *refs: far_kernel(dims, split, count, *refs), 0....  2.22 us
    pallas_call x1, Pallas kernels, on_device(): call(lambda dims, split, *refs: near_kernel(dims, split, count, *refs), 0...  1.69 us
  transfers between devices with their start and end apart: 28, of which 16 were waited for; matrix products, arithmetic and copies ran while one was open for 5% of the time, Pallas kernels for 9%

profile of v2, /device:TPU:0, one launch (start us, length us, event | category | flops | bytes accessed | tf_op | source)
XLA Modules:
  0.0 83.5 jit_solution(16989459886735650312)
XLA Ops:
  0.6 3.0 %collective-permute-start = (f32[1,256]{1,0:T(1,128)}, f32[1,256]{1,0:T(1,128)S(1)}, u32[]{:S(2)}, u32[]{:S(2)}) collective-permute-start(f32[1,256]{1,0:T(1,128)} %gain_ref.5), channel_id=1, source_target_pairs={{0,16},{16,0},{1,17},{17,1},{2,18},{18,2},{3,19},{19,3},{4,20},{20... | collective-permute-start | bytes 3080 | tf_op jit(solution)/shard_map/ppermute | solution.py:335
  3.7 1.5 %collective-permute-start.5 = (bf16[432,256]{1,0:T(8,128)(2,1)}, bf16[432,256]{1,0:T(8,128)(2,1)S(1)}, u32[]{:S(2)}, u32[]{:S(2)}) collective-permute-start(bf16[432,256]{1,0:T(8,128)(2,1)} %bitcast.44), channel_id=1, source_target_pairs={{0,2},{1,3},{2,0},{3,1},{4,6},{5,7},{6,4},{7,5},{8,10},{9,11},{10,... | collective-permute-start | bytes 663560 | tf_op jit(solution)/shard_map/ppermute | solution.py:335
  5.2 1.6 %collective-permute-start.4 = (bf16[432,256]{1,0:T(8,128)(2,1)}, bf16[432,256]{1,0:T(8,128)(2,1)S(1)}, u32[]{:S(2)}, u32[]{:S(2)}) collective-permute-start(bf16[432,256]{1,0:T(8,128)(2,1)} %bitcast.45), channel_id=1, source_target_pairs={{0,4},{1,5},{2,6},{3,7},{4,0},{5,1},{6,2},{7,3},{8,12},{9,13},{10,... | collective-permute-start | bytes 663560 | tf_op jit(solution)/shard_map/ppermute | solution.py:335
  6.7 2.6 %collective-permute-start.1 = (bf16[432,256]{1,0:T(8,128)(2,1)}, bf16[432,256]{1,0:T(8,128)(2,1)S(1)}, u32[]{:S(2)}, u32[]{:S(2)}) collective-permute-start(bf16[432,256]{1,0:T(8,128)(2,1)} %bitcast.46), channel_id=1, source_target_pairs={{0,8},{1,9},{2,10},{3,11},{4,12},{5,13},{6,14},{7,15},{8,0},{9,1},... | collective-permute-start | bytes 663560 | tf_op jit(solution)/shard_map/ppermute | solution.py:335
  9.3 1.0 %reshape.22.clips_ref.refs_1_ = bf16[4,128,256]{2,1,0:T(8,128)(2,1)S(1)} reshape(bf16[4,4,8,4,256]{4,3,2,1,0:T(4,128)(2,1)} %param.5) | data formatting | bytes 524288 | tf_op jit(solution)/shard_map/reshape | solution.py:362
  10.3 1.0 %reshape.23.cotangent_ref = bf16[4,128,256]{2,1,0:T(8,128)(2,1)S(1)} reshape(bf16[4,4,8,4,256]{4,3,2,1,0:T(4,128)(2,1)} %param.9) | data formatting | bytes 524288 | tf_op jit(solution)/shard_map/reshape | solution.py:363
  11.4 0.7 copy-done.1
  12.1 0.7 copy-done.3
  12.7 1.2 %shard_map.76 = (bf16[4,192,2304]{2,1,0:T(8,128)(2,1)S(1)}, f32[8,128]{1,0:T(8,128)S(1)}) custom-call(s32[4]{0:T(128)S(1)} %bitcast.49, bf16[4,128,256]{2,1,0:T(8,128)(2,1)S(1)} %reshape.22.clips_ref.refs_1_, bf16[4,128,256]{2,1,0:T(8,128)(2,1)S(1)} %reshape.23.cotangent_ref, f32[1,256]{1,0:T(1,128)S(1)} %copy-done.1, ...), custom_call_target="tpu_custom_call" | custom-call | flops 362387872 | bytes 3538944 | tf_op jit(solution)/shard_map/pallas_call | solution.py:392
  13.9 2.7 %collective-permute-done.4.refs_6_ = bf16[432,256]{1,0:T(8,128)(2,1)S(1)} collective-permute-done((bf16[432,256]{1,0:T(8,128)(2,1)}, bf16[432,256]{1,0:T(8,128)(2,1)S(1)}, u32[]{:S(2)}, u32[]{:S(2)}) %collective-permute-start.4) | collective-permute-done | bytes 221216 | tf_op jit(solution)/shard_map/ppermute | solution.py:335
  16.6 0.5 collective-permute-start.9
  17.1 2.0 %collective-permute-done.1.refs_5_ = bf16[432,256]{1,0:T(8,128)(2,1)S(1)} collective-permute-done((bf16[432,256]{1,0:T(8,128)(2,1)}, bf16[432,256]{1,0:T(8,128)(2,1)S(1)}, u32[]{:S(2)}, u32[]{:S(2)}) %collective-permute-start.1) | collective-permute-done | bytes 221216 | tf_op jit(solution)/shard_map/ppermute | solution.py:335
  19.1 0.3 collective-permute-start.2
  19.4 0.5 collective-permute-start.8
  19.9 2.6 %collective-permute-done.9.refs_8_ = bf16[432,256]{1,0:T(8,128)(2,1)S(1)} collective-permute-done((bf16[432,256]{1,0:T(8,128)(2,1)S(1)}, bf16[432,256]{1,0:T(8,128)(2,1)S(1)}, u32[]{:S(2)}, u32[]{:S(2)}) %collective-permute-start.9) | collective-permute-done | bytes 221216 | tf_op jit(solution)/shard_map/ppermute | solution.py:335
  22.5 2.5 %collective-permute-done.2.refs_9_ = bf16[432,256]{1,0:T(8,128)(2,1)S(1)} collective-permute-done((bf16[432,256]{1,0:T(8,128)(2,1)S(1)}, bf16[432,256]{1,0:T(8,128)(2,1)S(1)}, u32[]{:S(2)}, u32[]{:S(2)}) %collective-permute-start.2) | collective-permute-done | bytes 221216 | tf_op jit(solution)/shard_map/ppermute | solution.py:335
  25.0 0.5 collective-permute-start.3
  25.6 1.5 %collective-permute-start.12 = (bf16[432,256]{1,0:T(8,128)(2,1)S(1)}, bf16[432,256]{1,0:T(8,128)(2,1)S(1)}, u32[]{:S(2)}, u32[]{:S(2)}) collective-permute-start(bf16[432,256]{1,0:T(8,128)(2,1)S(1)} %collective-permute-done.1.refs_5_), channel_id=1, source_target_pairs={{0,2},{1,3},{2,0},{3,1},{4,6},{5,7},{6,4},{7,5},{8,10},{9,11},{10,... | collective-permute-start | bytes 663560 | tf_op jit(solution)/shard_map/ppermute | solution.py:335
  27.1 0.5 collective-permute-start.14
  27.6 0.9 %copy-done = bf16[1,432,256]{2,1,0:T(8,128)(2,1)S(1)} copy-done((bf16[1,432,256]{2,1,0:T(8,128)(2,1)S(1)}, bf16[1,432,256]{2,1,0:T(8,128)(2,1)}, u32[]{:S(2)}) %copy-start) | copy-done | bytes 221208
  28.5 1.7 %shard_map.77 = (f32[512,256]{1,0:T(8,128)S(1)}, f32[8,128]{1,0:T(8,128)S(1)}, bf16[3456,256]{1,0:T(8,128)(2,1)S(1)}) custom-call(bf16[4,192,2304]{2,1,0:T(8,128)(2,1)S(1)} %get-tuple-element.38.refs_0_.refs_3_.early_cols_ref, f32[8,128]{1,0:T(8,128)S(1)} %get-tuple-element.40.refs_1_, bf16[432,256]{1,0:T(8,128)(2,1)S(1)} %bitcast.48, ...), custom_call_target="tpu_custom_call" | custom-call | flops 905969664 | bytes 3538944 | tf_op jit(solution)/shard_map/pallas_call | solution.py:420
  30.2 2.5 %collective-permute-done.3.refs_11_ = bf16[432,256]{1,0:T(8,128)(2,1)S(1)} collective-permute-done((bf16[432,256]{1,0:T(8,128)(2,1)S(1)}, bf16[432,256]{1,0:T(8,128)(2,1)S(1)}, u32[]{:S(2)}, u32[]{:S(2)}) %collective-permute-start.3) | collective-permute-done | bytes 221216 | tf_op jit(solution)/shard_map/ppermute | solution.py:335
  32.7 2.4 %collective-permute-done.12.refs_7_ = bf16[432,256]{1,0:T(8,128)(2,1)S(1)} collective-permute-done((bf16[432,256]{1,0:T(8,128)(2,1)S(1)}, bf16[432,256]{1,0:T(8,128)(2,1)S(1)}, u32[]{:S(2)}, u32[]{:S(2)}) %collective-permute-start.12) | collective-permute-done | bytes 221216 | tf_op jit(solution)/shard_map/ppermute | solution.py:335
  35.1 0.5 collective-permute-start.15
  35.6 1.0 %collective-permute-done.13.refs_8_ = bf16[432,256]{1,0:T(8,128)(2,1)S(1)} collective-permute-done((bf16[432,256]{1,0:T(8,128)(2,1)S(1)}, bf16[432,256]{1,0:T(8,128)(2,1)S(1)}, u32[]{:S(2)}, u32[]{:S(2)}) %collective-permute-start.13) | collective-permute-done | bytes 221216 | tf_op jit(solution)/shard_map/ppermute | solution.py:335
  36.6 0.3 collective-permute-done.15.refs_12_
  36.9 2.2 %shard_map.78 = (bf16[512,256]{1,0:T(8,128)(2,1)S(1)}, bf16[3456,256]{1,0:T(8,128)(2,1)S(1)}) custom-call(s32[4]{0:T(128)S(1)} %bitcast.50, bf16[4,128,256]{2,1,0:T(8,128)(2,1)S(1)} %reshape.22.clips_ref.refs_1_, f32[8,128]{1,0:T(8,128)S(1)} %get-tuple-element.45.refs_2_, bf16[4,192,2304]{2,1,0:T(8,128)(2,1)S(1)} %get-tuple-element.38.refs_0_.refs_3_.early_cols_ref, ...), custom_call_target="tpu_custom_call" | custom-call | flops 905969664 | bytes 3538944 | tf_op jit(solution)/shard_map/pallas_call | solution.py:435
  39.1 0.6 collective-permute-start.16
  39.7 7.9 %collective-permute-done.16.theirs_ref = bf16[512,256]{1,0:T(8,128)(2,1)S(1)} collective-permute-done((bf16[512,256]{1,0:T(8,128)(2,1)S(1)}, bf16[512,256]{1,0:T(8,128)(2,1)S(1)}, u32[]{:S(2)}, u32[]{:S(2)}) %collective-permute-start.16) | collective-permute-done | bytes 262176 | tf_op jit(solution)/shard_map/ppermute | solution.py:335
  47.6 3.2 %shard_map.79 = (bf16[512,256]{1,0:T(8,128)(2,1)S(1)}, bf16[512,256]{1,0:T(8,128)(2,1)S(1)}, bf16[256,512]{1,0:T(8,128)(2,1)S(1)}, bf16[4,192,2304]{2,1,0:T(8,12...) custom-call(s32[4]{0:T(128)S(1)} %bitcast.51, ...), custom_call_target="tpu_custom_call" | custom-call | flops 905969664 | bytes 3538944 | tf_op jit(solution)/shard_map/pallas_call | solution.py:447
  50.9 0.5 collective-permute-start.17
  51.4 1.2 %shard_map.80 = (bf16[2,432,256]{2,1,0:T(8,128)(2,1)S(1)}, bf16[2,432,256]{2,1,0:T(8,128)(2,1)S(1)}, bf16[2,432,256]{2,1,0:T(8,128)(2,1)S(1)}, bf16[2,432,256]{2,1,0:T(8,128)(2,1)S(1)}) custom-call(bf16[256,512]{1,0:T(8,128)(2,1)S(1)} %get-tuple-element.57.turned_ref, bf16[4,192,2304]{2,1,0:T(8,128)(2,1)S(1)} %get-tuple-element.58.cols_ref), custom_call_target="tpu_custom_call" | custom-call | flops 905969664 | bytes 3538944 | tf_op jit(solution)/shard_map/pallas_call | solution.py:463
  52.7 0.4 collective-permute-start.23
  53.3 0.6 collective-permute-start.19
  54.0 0.4 collective-permute-done.21
  54.6 0.5 collective-permute-done.23
  55.2 5.6 %collective-permute-done.19 = bf16[432,256]{1,0:T(8,128)(2,1)S(1)} collective-permute-done((bf16[432,256]{1,0:T(8,128)(2,1)S(1)}, bf16[432,256]{1,0:T(8,128)(2,1)S(1)}, u32[]{:S(2)}, u32[]{:S(2)}) %collective-permute-start.19) | collective-permute-done | bytes 221216 | tf_op jit(solution)/shard_map/ppermute | solution.py:335
  60.8 0.6 collective-permute-start.20
  61.4 6.0 %collective-permute-done.20 = bf16[432,256]{1,0:T(8,128)(2,1)S(1)} collective-permute-done((bf16[432,256]{1,0:T(8,128)(2,1)S(1)}, bf16[432,256]{1,0:T(8,128)(2,1)S(1)}, u32[]{:S(2)}, u32[]{:S(2)}) %collective-permute-start.20) | collective-permute-done | bytes 221216 | tf_op jit(solution)/shard_map/ppermute | solution.py:335
  67.5 0.5 collective-permute-start.24
  68.1 1.4 %collective-permute-start.27 = (bf16[432,256]{1,0:T(8,128)(2,1)S(1)}, bf16[432,256]{1,0:T(8,128)(2,1)S(1)}, u32[]{:S(2)}, u32[]{:S(2)}) collective-permute-start(bf16[432,256]{1,0:T(8,128)(2,1)S(1)} %fusion.11), channel_id=1, source_target_pairs={{0,8},{1,9},{2,10},{3,11},{4,12},{5,13},{6,14},{7,15},{8,0},{9,1},... | collective-permute-start | bytes 663560 | tf_op jit(solution)/shard_map/ppermute | solution.py:335
  69.5 4.0 %collective-permute-done.24 = bf16[432,256]{1,0:T(8,128)(2,1)S(1)} collective-permute-done((bf16[432,256]{1,0:T(8,128)(2,1)S(1)}, bf16[432,256]{1,0:T(8,128)(2,1)S(1)}, u32[]{:S(2)}, u32[]{:S(2)}) %collective-permute-start.24) | collective-permute-done | bytes 221216 | tf_op jit(solution)/shard_map/ppermute | solution.py:335
  73.5 0.6 collective-permute-start.25
  74.1 3.7 %shard_map.81 = (bf16[512,256]{1,0:T(8,128)(2,1)S(1)}, bf16[512,256]{1,0:T(8,128)(2,1)S(1)}) custom-call(s32[4]{0:T(128)S(1)} %bitcast.52, bf16[4,128,256]{2,1,0:T(8,128)(2,1)S(1)} %reshape.22.clips_ref.refs_1_, f32[1,256]{1,0:T(1,128)S(1)} %copy-done.2, bf16[512,256]{1,0:T(8,128)(2,1)S(1)} %get-tuple-element.50.hidden_ref, ...), custom_call_target="tpu_custom_call" | custom-call | flops 1811939328 | bytes 3538944 | tf_op jit(solution)/shard_map/pallas_call | solution.py:499
  77.8 0.8 reshape.24
  78.6 0.8 reshape.25
  79.5 3.1 %collective-permute-done.26 = bf16[432,256]{1,0:T(8,128)(2,1)S(1)} collective-permute-done((bf16[432,256]{1,0:T(8,128)(2,1)S(1)}, bf16[432,256]{1,0:T(8,128)(2,1)S(1)}, u32[]{:S(2)}, u32[]{:S(2)}) %collective-permute-start.26) | collective-permute-done | bytes 221216 | tf_op jit(solution)/shard_map/ppermute | solution.py:335
  82.6 0.9 %fusion.6 = f32[1,432,256]{2,1,0:T(8,128)} fusion(f32[2,432,256]{2,1,0:T(8,128)S(1)} %convert_add_fusion, bf16[432,256]{1,0:T(8,128)(2,1)S(1)} %collective-permute-done.27, bf16[432,256]{1,0:T(8,128)(2,1)S(1)} %collective-permute-done.26, bf16[432,256]{1,0:T(8,128)(2,1)S(1)} %collective-permute-done.25), kind=kLoop, calls=%fused_computation.13 | loop fusion | flops 774144 | bytes 1548288 | tf_op jit(solution)/shard_map/broadcast_in_dim | solution.py:516
  (41 shorter events, 1.1 us)
Async XLA Ops:
  0.6 10.7 %collective-permute-start = (f32[1,256]{1,0:T(1,128)}, f32[1,256]{1,0:T(1,128)S(1)}, u32[]{:S(2)}, u32[]{:S(2)}) collective-permute-start(f32[1,256]{1,0:T(1,128)} %gain_ref.5), channel_id=1, source_target_pairs={{0,16},{16,0},{1,17},{17,1},{2,18},{18,2},{3,19},{19,3},{4,20},{20... | collective-permute-start | bytes 3080 | tf_op jit(solution)/shard_map/ppermute | solution.py:335
  3.7 10.3 %collective-permute-start.5 = (bf16[432,256]{1,0:T(8,128)(2,1)}, bf16[432,256]{1,0:T(8,128)(2,1)S(1)}, u32[]{:S(2)}, u32[]{:S(2)}) collective-permute-start(bf16[432,256]{1,0:T(8,128)(2,1)} %bitcast.44), channel_id=1, source_target_pairs={{0,2},{1,3},{2,0},{3,1},{4,6},{5,7},{6,4},{7,5},{8,10},{9,11},{10,... | collective-permute-start | bytes 663560 | tf_op jit(solution)/shard_map/ppermute | solution.py:335
  5.2 11.4 %collective-permute-start.4 = (bf16[432,256]{1,0:T(8,128)(2,1)}, bf16[432,256]{1,0:T(8,128)(2,1)S(1)}, u32[]{:S(2)}, u32[]{:S(2)}) collective-permute-start(bf16[432,256]{1,0:T(8,128)(2,1)} %bitcast.45), channel_id=1, source_target_pairs={{0,4},{1,5},{2,6},{3,7},{4,0},{5,1},{6,2},{7,3},{8,12},{9,13},{10,... | collective-permute-start | bytes 663560 | tf_op jit(solution)/shard_map/ppermute | solution.py:335
  6.7 12.3 %collective-permute-start.1 = (bf16[432,256]{1,0:T(8,128)(2,1)}, bf16[432,256]{1,0:T(8,128)(2,1)S(1)}, u32[]{:S(2)}, u32[]{:S(2)}) collective-permute-start(bf16[432,256]{1,0:T(8,128)(2,1)} %bitcast.46), channel_id=1, source_target_pairs={{0,8},{1,9},{2,10},{3,11},{4,12},{5,13},{6,14},{7,15},{8,0},{9,1},... | collective-permute-start | bytes 663560 | tf_op jit(solution)/shard_map/ppermute | solution.py:335
  11.4 0.7 copy-start.1
  12.1 0.7 copy-start.3
  16.6 5.9 %collective-permute-start.9 = (bf16[432,256]{1,0:T(8,128)(2,1)S(1)}, bf16[432,256]{1,0:T(8,128)(2,1)S(1)}, u32[]{:S(2)}, u32[]{:S(2)}) collective-permute-start(bf16[432,256]{1,0:T(8,128)(2,1)S(1)} %collective-permute-done.4.refs_6_), channel_id=1, source_target_pairs={{0,2},{1,3},{2,0},{3,1},{4,6},{5,7},{6,4},{7,5},{8,10},{9,11},{10,... | collective-permute-start | bytes 663560 | tf_op jit(solution)/shard_map/ppermute | solution.py:335
  19.1 5.9 %collective-permute-start.2 = (bf16[432,256]{1,0:T(8,128)(2,1)S(1)}, bf16[432,256]{1,0:T(8,128)(2,1)S(1)}, u32[]{:S(2)}, u32[]{:S(2)}) collective-permute-start(bf16[432,256]{1,0:T(8,128)(2,1)S(1)} %collective-permute-done.1.refs_5_), channel_id=1, source_target_pairs={{0,4},{1,5},{2,6},{3,7},{4,0},{5,1},{6,2},{7,3},{8,12},{9,13},{10,... | collective-permute-start | bytes 663560 | tf_op jit(solution)/shard_map/ppermute | solution.py:335
  19.4 6.1 %collective-permute-start.6 = (bf16[432,256]{1,0:T(8,128)(2,1)}, bf16[432,256]{1,0:T(8,128)(2,1)S(1)}, u32[]{:S(2)}, u32[]{:S(2)}) collective-permute-start(bf16[432,256]{1,0:T(8,128)(2,1)} %bitcast.47), channel_id=1, source_target_pairs={{0,1},{1,0},{2,3},{3,2},{4,5},{5,4},{6,7},{7,6},{8,9},{9,8},{10,11... | collective-permute-start | bytes 663560 | tf_op jit(solution)/shard_map/ppermute | solution.py:335
  19.4 7.6 %collective-permute-start.8 = (bf16[432,256]{1,0:T(8,128)(2,1)S(1)}, bf16[432,256]{1,0:T(8,128)(2,1)S(1)}, u32[]{:S(2)}, u32[]{:S(2)}) collective-permute-start(bf16[432,256]{1,0:T(8,128)(2,1)S(1)} %collective-permute-done.4.refs_6_), channel_id=1, source_target_pairs={{0,1},{1,0},{2,3},{3,2},{4,5},{5,4},{6,7},{7,6},{8,9},{9,8},{10,11... | collective-permute-start | bytes 663560 | tf_op jit(solution)/shard_map/ppermute | solution.py:335
  19.9 7.1 %collective-permute-start.7 = (bf16[432,256]{1,0:T(8,128)(2,1)S(1)}, bf16[432,256]{1,0:T(8,128)(2,1)S(1)}, u32[]{:S(2)}, u32[]{:S(2)}) collective-permute-start(bf16[432,256]{1,0:T(8,128)(2,1)S(1)} %collective-permute-done.5.refs_4_), channel_id=1, source_target_pairs={{0,1},{1,0},{2,3},{3,2},{4,5},{5,4},{6,7},{7,6},{8,9},{9,8},{10,11... | collective-permute-start | bytes 663560 | tf_op jit(solution)/shard_map/ppermute | solution.py:335
  22.5 5.1 %collective-permute-start.10 = (bf16[432,256]{1,0:T(8,128)(2,1)S(1)}, bf16[432,256]{1,0:T(8,128)(2,1)S(1)}, u32[]{:S(2)}, u32[]{:S(2)}) collective-permute-start(bf16[432,256]{1,0:T(8,128)(2,1)S(1)} %collective-permute-done.9.refs_8_), channel_id=1, source_target_pairs={{0,1},{1,0},{2,3},{3,2},{4,5},{5,4},{6,7},{7,6},{8,9},{9,8},{10,11... | collective-permute-start | bytes 663560 | tf_op jit(solution)/shard_map/ppermute | solution.py:335
  25.0 7.7 %collective-permute-start.3 = (bf16[432,256]{1,0:T(8,128)(2,1)S(1)}, bf16[432,256]{1,0:T(8,128)(2,1)S(1)}, u32[]{:S(2)}, u32[]{:S(2)}) collective-permute-start(bf16[432,256]{1,0:T(8,128)(2,1)S(1)} %collective-permute-done.2.refs_9_), channel_id=1, source_target_pairs={{0,2},{1,3},{2,0},{3,1},{4,6},{5,7},{6,4},{7,5},{8,10},{9,11},{10,... | collective-permute-start | bytes 663560 | tf_op jit(solution)/shard_map/ppermute | solution.py:335
  25.6 9.5 %collective-permute-start.12 = (bf16[432,256]{1,0:T(8,128)(2,1)S(1)}, bf16[432,256]{1,0:T(8,128)(2,1)S(1)}, u32[]{:S(2)}, u32[]{:S(2)}) collective-permute-start(bf16[432,256]{1,0:T(8,128)(2,1)S(1)} %collective-permute-done.1.refs_5_), channel_id=1, source_target_pairs={{0,2},{1,3},{2,0},{3,1},{4,6},{5,7},{6,4},{7,5},{8,10},{9,11},{10,... | collective-permute-start | bytes 663560 | tf_op jit(solution)/shard_map/ppermute | solution.py:335
  27.0 8.6 %collective-permute-start.11 = (bf16[432,256]{1,0:T(8,128)(2,1)S(1)}, bf16[432,256]{1,0:T(8,128)(2,1)S(1)}, u32[]{:S(2)}, u32[]{:S(2)}) collective-permute-start(bf16[432,256]{1,0:T(8,128)(2,1)S(1)} %collective-permute-done.1.refs_5_), channel_id=1, source_target_pairs={{0,1},{1,0},{2,3},{3,2},{4,5},{5,4},{6,7},{7,6},{8,9},{9,8},{10,11... | collective-permute-start | bytes 663560 | tf_op jit(solution)/shard_map/ppermute | solution.py:335
  27.1 8.6 %collective-permute-start.14 = (bf16[432,256]{1,0:T(8,128)(2,1)S(1)}, bf16[432,256]{1,0:T(8,128)(2,1)S(1)}, u32[]{:S(2)}, u32[]{:S(2)}) collective-permute-start(bf16[432,256]{1,0:T(8,128)(2,1)S(1)} %collective-permute-done.2.refs_9_), channel_id=1, source_target_pairs={{0,1},{1,0},{2,3},{3,2},{4,5},{5,4},{6,7},{7,6},{8,9},{9,8},{10,11... | collective-permute-start | bytes 663560 | tf_op jit(solution)/shard_map/ppermute | solution.py:335
  27.6 0.9 %copy-start = (bf16[1,432,256]{2,1,0:T(8,128)(2,1)S(1)}, bf16[1,432,256]{2,1,0:T(8,128)(2,1)}, u32[]{:S(2)}) copy-start(bf16[1,432,256]{2,1,0:T(8,128)(2,1)} %param.8) | copy-start | bytes 663556
  30.2 17.4 %copy-start.2 = (f32[1,256]{1,0:T(1,128)S(1)}, f32[1,256]{1,0:T(1,128)}, u32[]{:S(2)}) copy-start(f32[1,256]{1,0:T(1,128)} %gain_ref.5) | copy-start | bytes 3076
  35.1 1.5 %collective-permute-start.13 = (bf16[432,256]{1,0:T(8,128)(2,1)S(1)}, bf16[432,256]{1,0:T(8,128)(2,1)S(1)}, u32[]{:S(2)}, u32[]{:S(2)}) collective-permute-start(bf16[432,256]{1,0:T(8,128)(2,1)S(1)} %collective-permute-done.12.refs_7_), channel_id=1, source_target_pairs={{0,1},{1,0},{2,3},{3,2},{4,5},{5,4},{6,7},{7,6},{8,9},{9,8},{10,11... | collective-permute-start | bytes 663560 | tf_op jit(solution)/shard_map/ppermute | solution.py:335
  35.1 1.8 %collective-permute-start.15 = (bf16[432,256]{1,0:T(8,128)(2,1)S(1)}, bf16[432,256]{1,0:T(8,128)(2,1)S(1)}, u32[]{:S(2)}, u32[]{:S(2)}) collective-permute-start(bf16[432,256]{1,0:T(8,128)(2,1)S(1)} %collective-permute-done.3.refs_11_), channel_id=1, source_target_pairs={{0,1},{1,0},{2,3},{3,2},{4,5},{5,4},{6,7},{7,6},{8,9},{9,8},{10,11... | collective-permute-start | bytes 663560 | tf_op jit(solution)/shard_map/ppermute | solution.py:335
  39.1 8.5 %collective-permute-start.16 = (bf16[512,256]{1,0:T(8,128)(2,1)S(1)}, bf16[512,256]{1,0:T(8,128)(2,1)S(1)}, u32[]{:S(2)}, u32[]{:S(2)}) collective-permute-start(bf16[512,256]{1,0:T(8,128)(2,1)S(1)} %get-tuple-element.49.mine_ref), channel_id=1, source_target_pairs={{0,16},{16,0},{1,17},{17,1},{2,18},{18,2},{3,19},{19,3},{4,20},{20... | collective-permute-start | bytes 786440 | tf_op jit(solution)/shard_map/ppermute | solution.py:335
  50.8 2.4 %collective-permute-start.18 = (bf16[2,432,256]{2,1,0:T(8,128)(2,1)S(1)}, bf16[2,432,256]{2,1,0:T(8,128)(2,1)S(1)}, u32[]{:S(2)}, u32[]{:S(2)}) collective-permute-start(bf16[2,432,256]{2,1,0:T(8,128)(2,1)S(1)} %get-tuple-element.55), channel_id=1, source_target_pairs={{0,1},{1,0},{2,3},{3,2},{4,5},{5,4},{6,7},{7,6},{8,9},{9,8},{10,11... | collective-permute-start | bytes 1327112 | tf_op jit(solution)/shard_map/ppermute | solution.py:335
  50.9 3.0 %collective-permute-start.17 = (bf16[2,432,256]{2,1,0:T(8,128)(2,1)S(1)}, bf16[2,432,256]{2,1,0:T(8,128)(2,1)S(1)}, u32[]{:S(2)}, u32[]{:S(2)}) collective-permute-start(bf16[2,432,256]{2,1,0:T(8,128)(2,1)S(1)} %get-tuple-element.53), channel_id=1, source_target_pairs={{0,1},{1,0},{2,3},{3,2},{4,5},{5,4},{6,7},{7,6},{8,9},{9,8},{10,11... | collective-permute-start | bytes 1327112 | tf_op jit(solution)/shard_map/ppermute | solution.py:335
  52.6 1.9 %collective-permute-start.21 = (bf16[2,432,256]{2,1,0:T(8,128)(2,1)S(1)}, bf16[2,432,256]{2,1,0:T(8,128)(2,1)S(1)}, u32[]{:S(2)}, u32[]{:S(2)}) collective-permute-start(bf16[2,432,256]{2,1,0:T(8,128)(2,1)S(1)} %get-tuple-element.60), channel_id=1, source_target_pairs={{0,1},{1,0},{2,3},{3,2},{4,5},{5,4},{6,7},{7,6},{8,9},{9,8},{10,11... | collective-permute-start | bytes 1327112 | tf_op jit(solution)/shard_map/ppermute | solution.py:335
  52.7 2.3 %collective-permute-start.23 = (bf16[2,432,256]{2,1,0:T(8,128)(2,1)S(1)}, bf16[2,432,256]{2,1,0:T(8,128)(2,1)S(1)}, u32[]{:S(2)}, u32[]{:S(2)}) collective-permute-start(bf16[2,432,256]{2,1,0:T(8,128)(2,1)S(1)} %get-tuple-element.69), channel_id=1, source_target_pairs={{0,1},{1,0},{2,3},{3,2},{4,5},{5,4},{6,7},{7,6},{8,9},{9,8},{10,11... | collective-permute-start | bytes 1327112 | tf_op jit(solution)/shard_map/ppermute | solution.py:335
  53.3 7.5 %collective-permute-start.19 = (bf16[432,256]{1,0:T(8,128)(2,1)S(1)}, bf16[432,256]{1,0:T(8,128)(2,1)S(1)}, u32[]{:S(2)}, u32[]{:S(2)}) collective-permute-start(bf16[432,256]{1,0:T(8,128)(2,1)S(1)} %fusion.12), channel_id=1, source_target_pairs={{0,2},{1,3},{2,0},{3,1},{4,6},{5,7},{6,4},{7,5},{8,10},{9,11},{10,... | collective-permute-start | bytes 663560 | tf_op jit(solution)/shard_map/ppermute | solution.py:335
  54.4 19.7 %copy-start.4 = (s32[1,4]{1,0:T(1,128)S(1)}, s32[1,4]{1,0:T(1,128)}, u32[]{:S(2)}) copy-start(s32[1,4]{1,0:T(1,128)} %param.6) | copy-start | bytes 52
  60.8 6.6 %collective-permute-start.20 = (bf16[432,256]{1,0:T(8,128)(2,1)S(1)}, bf16[432,256]{1,0:T(8,128)(2,1)S(1)}, u32[]{:S(2)}, u32[]{:S(2)}) collective-permute-start(bf16[432,256]{1,0:T(8,128)(2,1)S(1)} %fusion.13), channel_id=1, source_target_pairs={{0,2},{1,3},{2,0},{3,1},{4,6},{5,7},{6,4},{7,5},{8,10},{9,11},{10,... | collective-permute-start | bytes 663560 | tf_op jit(solution)/shard_map/ppermute | solution.py:335
  61.4 6.6 %collective-permute-start.22 = (bf16[432,256]{1,0:T(8,128)(2,1)S(1)}, bf16[432,256]{1,0:T(8,128)(2,1)S(1)}, u32[]{:S(2)}, u32[]{:S(2)}) collective-permute-start(bf16[432,256]{1,0:T(8,128)(2,1)S(1)} %fusion.8), channel_id=1, source_target_pairs={{0,4},{1,5},{2,6},{3,7},{4,0},{5,1},{6,2},{7,3},{8,12},{9,13},{10,... | collective-permute-start | bytes 663560 | tf_op jit(solution)/shard_map/ppermute | solution.py:335
  67.5 6.0 %collective-permute-start.24 = (bf16[432,256]{1,0:T(8,128)(2,1)S(1)}, bf16[432,256]{1,0:T(8,128)(2,1)S(1)}, u32[]{:S(2)}, u32[]{:S(2)}) collective-permute-start(bf16[432,256]{1,0:T(8,128)(2,1)S(1)} %fusion.14), channel_id=1, source_target_pairs={{0,2},{1,3},{2,0},{3,1},{4,6},{5,7},{6,4},{7,5},{8,10},{9,11},{10,... | collective-permute-start | bytes 663560 | tf_op jit(solution)/shard_map/ppermute | solution.py:335
  68.1 11.3 %collective-permute-start.27 = (bf16[432,256]{1,0:T(8,128)(2,1)S(1)}, bf16[432,256]{1,0:T(8,128)(2,1)S(1)}, u32[]{:S(2)}, u32[]{:S(2)}) collective-permute-start(bf16[432,256]{1,0:T(8,128)(2,1)S(1)} %fusion.11), channel_id=1, source_target_pairs={{0,8},{1,9},{2,10},{3,11},{4,12},{5,13},{6,14},{7,15},{8,0},{9,1},... | collective-permute-start | bytes 663560 | tf_op jit(solution)/shard_map/ppermute | solution.py:335
  73.5 6.0 %collective-permute-start.25 = (bf16[432,256]{1,0:T(8,128)(2,1)S(1)}, bf16[432,256]{1,0:T(8,128)(2,1)S(1)}, u32[]{:S(2)}, u32[]{:S(2)}) collective-permute-start(bf16[432,256]{1,0:T(8,128)(2,1)S(1)} %fusion.15), channel_id=1, source_target_pairs={{0,2},{1,3},{2,0},{3,1},{4,6},{5,7},{6,4},{7,5},{8,10},{9,11},{10,... | collective-permute-start | bytes 663560 | tf_op jit(solution)/shard_map/ppermute | solution.py:335
  74.1 8.5 %collective-permute-start.26 = (bf16[432,256]{1,0:T(8,128)(2,1)S(1)}, bf16[432,256]{1,0:T(8,128)(2,1)S(1)}, u32[]{:S(2)}, u32[]{:S(2)}) collective-permute-start(bf16[432,256]{1,0:T(8,128)(2,1)S(1)} %fusion.1), channel_id=1, source_target_pairs={{0,4},{1,5},{2,6},{3,7},{4,0},{5,1},{6,2},{7,3},{8,12},{9,13},{10,... | collective-permute-start | bytes 663560 | tf_op jit(solution)/shard_map/ppermute | solution.py:335

commit v3 on v2

--- a/solution.py
+++ b/solution.py
@@ -203,21 +203,37 @@
     wait_all(copies)
 
 
-def far_kernel(dims, split, count, plan_ref, clips_ref, early_ref, cols_ref, base_ref, *rest):
-    pieces, (out_ref, kept_ref, weight_ref, held_ref, sems) = rest[:count], rest[count:]
+def split_gain(gain_row):
+    high = gain_row.astype(jnp.bfloat16).astype(jnp.float32)
+    middle = (gain_row - high).astype(jnp.bfloat16).astype(jnp.float32)
+    low = gain_row - high - middle
+    row = lax.broadcasted_iota(jnp.int32, (ROW_TILE, gain_row.shape[1]), 0)
+    parts = jnp.where(row == 0, high, jnp.where(row == 1, middle, jnp.where(row == 2, low, 0.0)))
+    return parts.astype(jnp.bfloat16)
+
+
+def join_gain(parts):
+    parts = parts.astype(jnp.float32)
+    return (parts[0:1] + parts[1:2]) + parts[2:3]
+
+
+def far_kernel(dims, split, count, plan_ref, clips_ref, gain_ref, early_ref, cols_ref, base_ref, *rest):
+    pieces, (out_ref, kept_ref, weight_ref, held_ref, held_gain, sems) = rest[:count], rest[count:]
+    total = base_ref.shape[0]
     section, place, near = where_am_i(split)
-    arriving = fetch([(clips_ref, held_ref)], sems)
+    arriving = fetch([(clips_ref, held_ref), (gain_ref, held_gain)], sems)
     lay_pieces(place, pieces, weight_ref)
-    leaving = pltpu.make_async_copy(weight_ref, kept_ref, sems.at[1])
+    leaving = pltpu.make_async_copy(weight_ref, kept_ref, sems.at[2])
     leaving.start()
     wait_all(arriving)
+    out_ref[total:, :] = split_gain(held_gain[...])
 
     def run(at, part):
         conv = half_forward if at == 0 else half_spread
         value = base_ref[...] + conv(cols_ref, weight_ref, dims, part)
         if at == 0:
             value = value + take_clips(plan_ref, held_ref, dims)
-        out_ref[...] = value.astype(jnp.bfloat16)
+        out_ref[:total, :] = value.astype(jnp.bfloat16)
 
     on_half(section, 1 - near, run)
     leaving.wait()
@@ -234,31 +250,31 @@
             out[inner] = sums_ref[pl.ds(pl.multiple_of(owner * rows, ROW_TILE), rows), :]
 
 
-def gradient_kernel(dims, split, plan_ref, clips_ref, cotangent_ref, gain_ref, last_gain_ref, mine_ref, theirs_ref,
+def gradient_kernel(dims, split, plan_ref, clips_ref, cotangent_ref, gain_ref, mine_ref, theirs_ref,
                     early_cols_ref, grad_ref, hidden_ref, turned_ref, cols_ref, *rest):
-    outs = rest[:-6]
-    sums_ref, held_clips, held_cotangent, held_gain, held_last, sems = rest[-6:]
+    outs = rest[:-5]
+    sums_ref, held_clips, held_cotangent, held_gain, sems = rest[-5:]
     section, place, near = where_am_i(split)
     channels = dims[4]
     total = dims[0] * dims[1] * dims[2] * dims[3]
     arriving = fetch(
         [
             (cotangent_ref, held_cotangent),
-            (last_gain_ref, held_last),
             (clips_ref, held_clips),
             (gain_ref, held_gain),
         ],
         sems,
     )
     leading = section == 0
-    mine = mine_ref[...].astype(jnp.float32)
-    theirs = theirs_ref[...].astype(jnp.float32)
+    mine = mine_ref[:total, :].astype(jnp.float32)
+    theirs = theirs_ref[:total, :].astype(jnp.float32)
+    last_gain = join_gain(jnp.where(leading, theirs_ref[total:, :].astype(jnp.float32), mine_ref[total:, :].astype(jnp.float32)))
     hidden = jnp.where(leading, mine, theirs)
     spread = jnp.where(leading, theirs, mine)
     hidden_ref[...] = hidden.astype(jnp.bfloat16)
     wait_all(arriving)
     cotangent = held_cotangent[...].reshape(total, channels).astype(jnp.float32)
-    upstream = back(hidden, cotangent, spread, held_last[...]).astype(jnp.bfloat16)
+    upstream = back(hidden, cotangent, spread, last_gain).astype(jnp.bfloat16)
     grad_ref[...] = upstream
     unit = jnp.where(leading, take_clips(plan_ref, held_clips, dims), hidden)
     turned_ref[...] = activate(unit, held_gain[...]).T
@@ -293,7 +309,7 @@
 
 
 def last_kernel(dims, split, plan_ref, clips_ref, gain_ref, hidden_ref, grad_ref, near_ref, far_ref, acts_ref,
-                grads_ref, weight_ref, cols_ref, held_clips, held_gain, held_hidden, held_grad, sems):
+                grads_ref, weight_ref, cols_ref, held_clips, held_gain, held_hidden, held_grad, made_acts, made_grads, sems):
     section, place, near = where_am_i(split)
     half_rows = weight_ref.shape[0] // 2
     first = pl.multiple_of(near * half_rows, ROW_TILE) if split else 0
@@ -319,16 +335,19 @@
         fill_columns(cols_ref, upstream, dims)
         spread = half_spread(cols_ref, halves[0], dims, 0) + half_spread(cols_ref, halves[1], dims, 1)
         ordered = take_clips(plan_ref, held_clips, dims)
-        grads_ref[...] = back(ordered, upstream, spread, gain_row).astype(jnp.bfloat16)
-        acts_ref[...] = held_hidden[...]
+        back_out = back(ordered, upstream, spread, gain_row).astype(jnp.bfloat16)
+        made_grads[...] = back_out.reshape(made_grads.shape)
+        made_acts[...] = held_hidden[...].reshape(made_acts.shape)
 
     @pl.when(section != 0)
     def _():
         hidden = held_hidden[...].astype(jnp.float32)
         fill_columns(cols_ref, activate(hidden, gain_row).astype(jnp.float32), dims)
         branch = half_forward(cols_ref, halves[0], dims, 0) + half_forward(cols_ref, halves[1], dims, 1)
-        acts_ref[...] = (hidden + branch).astype(jnp.bfloat16)
-        grads_ref[...] = held_grad[...]
+        made_acts[...] = (hidden + branch).astype(jnp.bfloat16).reshape(made_acts.shape)
+        made_grads[...] = held_grad[...].reshape(made_grads.shape)
+
+    wait_all(fetch([(made_acts, acts_ref), (made_grads, grads_ref)], sems))
 
 
 def swap(value, axis, by):
@@ -348,7 +367,6 @@
 
 
 def on_device(clips, plan, gains, weights, cotangent):
-    section = lax.axis_index("section")
     peers = lax.axis_size("fsdp")
     micro, frames, height, width, channels = clips.shape
     dims = clips.shape
@@ -386,8 +404,14 @@
             **config,
         )
 
-    other_gain = swap(gains, "section", 1)
-    last_gain = jnp.where(section == 0, other_gain, gains)
+    own = weights[0]
+    signal = gains
+    if split:
+        held = {0: own}
+        held[2] = swap(own, "fsdp", 2)
+        held[4] = swap(own, "fsdp", 4)
+        held[8] = swap(own, "fsdp", 8)
+        signal = held[4]
 
     early_cols, token = call(
         prepare_kernel,
@@ -395,18 +419,12 @@
         out_shape=[cols_out, token_out],
         in_specs=[smem] + [vmem] * 3 + [anywhere],
         out_specs=[vmem] * 2,
-    )(order, flat_clips, flat_cotangent, gains, last_gain)
-
-    own = weights[0]
+    )(order, flat_clips, flat_cotangent, gains, gains)
+
     if split:
-        held = {0: own}
-        held[2] = swap(own, "fsdp", 2)
-        held[4] = swap(own, "fsdp", 4)
-        held[8] = swap(own, "fsdp", 8)
-        held[4], held[2], token = together(held[4], held[2], token)
+        held[4], token = together(held[4], token)
         held[6] = swap(held[4], "fsdp", 2)
         held[12] = swap(held[8], "fsdp", 4)
-        held[8], held[6] = together(held[8], held[6])
         held[10] = swap(held[8], "fsdp", 2)
         held[14] = swap(held[12], "fsdp", 2)
         for by in (0, 2, 4, 6):
@@ -435,11 +453,11 @@
     mine, far_weight = call(
         lambda dims, split, *refs: far_kernel(dims, split, count, *refs),
         0.5,
-        out_shape=[volume, half_out],
-        in_specs=[smem] + [anywhere] * 2 + [vmem] * (2 + count),
+        out_shape=[jax.ShapeDtypeStruct((total + ROW_TILE, channels), jnp.bfloat16), half_out],
+        in_specs=[smem] + [anywhere] * 3 + [vmem] * (2 + count),
         out_specs=[vmem, anywhere],
-        scratch_shapes=[half_weight, clips_scratch, pltpu.SemaphoreType.DMA((2,))],
-    )(order, flat_clips, token, early_cols, base, *far)
+        scratch_shapes=[half_weight, clips_scratch, gain_scratch, pltpu.SemaphoreType.DMA((3,))],
+    )(order, flat_clips, gains, token, early_cols, base, *far)
 
     theirs = swap(mine, "section", 1)
 
@@ -448,17 +466,16 @@
         gradient_kernel,
         0.5,
         out_shape=[volume, volume, turned_out, cols_out] + shapes,
-        in_specs=[smem] + [anywhere] * 4 + [vmem] * 3,
+        in_specs=[smem] + [anywhere] * 3 + [vmem] * 3,
         out_specs=[vmem] * (4 + len(shapes)),
         scratch_shapes=[
             half_weight,
             clips_scratch,
             clips_scratch,
             gain_scratch,
-            gain_scratch,
-            pltpu.SemaphoreType.DMA((4,)),
+            pltpu.SemaphoreType.DMA((3,)),
         ],
-    )(order, flat_clips, flat_cotangent, gains, last_gain, mine, theirs, early_cols)
+    )(order, flat_clips, flat_cotangent, gains, mine, theirs, early_cols)
 
     near_sums = call(
         rest_kernel,
@@ -500,9 +517,9 @@
         last_kernel,
         1.0,
         limit=LAST_VMEM_LIMIT,
-        out_shape=[volume, volume],
+        out_shape=[jax.ShapeDtypeStruct((1, *dims), jnp.bfloat16)] * 2,
         in_specs=[smem] + [anywhere] * 6,
-        out_specs=[vmem, vmem],
+        out_specs=[anywhere, anywhere],
         scratch_shapes=[
             pltpu.VMEM((all_rows, channels), jnp.bfloat16),
             pltpu.VMEM(cols_shape, jnp.bfloat16),
@@ -510,10 +527,12 @@
             gain_scratch,
             volume_scratch,
             volume_scratch,
+            pltpu.VMEM((1, *dims), jnp.bfloat16),
+            pltpu.VMEM((1, *dims), jnp.bfloat16),
             pltpu.SemaphoreType.DMA((6,)),
         ],
     )(order, flat_clips, gains, hidden, grad, near_weight, far_weight)
-    return (acts.reshape(1, *dims), grads.reshape(1, *dims), weight_grad[None])
+    return (acts, grads, weight_grad[None])
 
 
 def solution(mesh):

time: 83.7 us -> 78.4 us (0.937)
  waiting for transfers between devices: 43.5 us -> 31.5 us
  starting transfers between devices: 18.5 us -> 25.9 us
  local copies, waits for them, and re-layouts: 5.94 us -> 4.41 us
    ppermute x28 -> x27, waiting for transfers between devices: 43.5 us -> 31.5 us  [swap(): lax.ppermute(value, axis, [(i, i ^ by) for i in range(lax.axis_size(axis))])]
    ppermute x28 -> x27, starting transfers between devices: 18.5 us -> 25.9 us  [swap(): lax.ppermute(value, axis, [(i, i ^ by) for i in range(lax.axis_size(axis))])]
    reshape x2 -> x0, local copies, waits for them, and re-layouts: 1.53 us -> none  [on_device(): return (acts.reshape(1, *dims), grads.reshape(1, *dims), weight_grad[None])]
    pallas_call x1, Pallas kernels: 3.69 us -> 4.53 us  [on_device(): call(last_kernel, 1.0, limit=LAST_VMEM_LIMIT, out_shape=[jax.ShapeDtypeSt...]
  transfers between devices with their start and end apart: 28 -> 27, of which waited for: 16 -> 13; matrix products, arithmetic and copies ran while one was open for 5% -> 3% of each run, Pallas kernels for 9% -> 11%
where the time goes in v3:
time: 78.4 us; the launch traced here: 78.1 us
  waiting for transfers between devices  31.5 us (40%)
  starting transfers between devices  25.9 us (33%)
  Pallas kernels  14 us (18%)
  local copies, waits for them, and re-layouts  4.41 us (6%)
  other arithmetic  1.45 us (2%)
  between operations  0.84 us (1%)
    ppermute x27, waiting for transfers between devices, swap(): lax.ppermute(value, axis, [(i, i ^ by) for i in range(lax.axis_size(axis))])  31.5 us
    ppermute x27, starting transfers between devices, swap(): lax.ppermute(value, axis, [(i, i ^ by) for i in range(lax.axis_size(axis))])  25.9 us
    pallas_call x1, Pallas kernels, on_device(): call(last_kernel, 1.0, limit=LAST_VMEM_LIMIT, out_shape=[jax.ShapeDtypeSt...  4.53 us
    pallas_call x1, Pallas kernels, on_device(): call(gradient_kernel, 0.5, out_shape=[volume, volume, turned_out, cols_ou...  3.14 us
    unnamed x10, local copies, waits for them, and re-layouts  2.28 us
    pallas_call x1, Pallas kernels, on_device(): call(lambda dims, split, *refs: far_kernel(dims, split, count, *refs), 0....  2.25 us
    pallas_call x1, Pallas kernels, on_device(): call(lambda dims, split, *refs: near_kernel(dims, split, count, *refs), 0...  1.7 us
  transfers between devices with their start and end apart: 27, of which 13 were waited for; matrix products, arithmetic and copies ran while one was open for 3% of the time, Pallas kernels for 11%

profile of v3, /device:TPU:0, one launch (start us, length us, event | category | flops | bytes accessed | tf_op | source)
XLA Modules:
  0.0 78.1 jit_solution(18046722430789353254)
XLA Ops:
  0.6 3.1 %collective-permute-start.3 = (bf16[432,256]{1,0:T(8,128)(2,1)}, bf16[432,256]{1,0:T(8,128)(2,1)S(1)}, u32[]{:S(2)}, u32[]{:S(2)}) collective-permute-start(bf16[432,256]{1,0:T(8,128)(2,1)} %bitcast.44), channel_id=1, source_target_pairs={{0,4},{1,5},{2,6},{3,7},{4,0},{5,1},{6,2},{7,3},{8,12},{9,13},{10,... | collective-permute-start | bytes 663560 | tf_op jit(solution)/shard_map/ppermute | solution.py:354
  3.7 2.6 %collective-permute-start = (bf16[432,256]{1,0:T(8,128)(2,1)}, bf16[432,256]{1,0:T(8,128)(2,1)S(1)}, u32[]{:S(2)}, u32[]{:S(2)}) collective-permute-start(bf16[432,256]{1,0:T(8,128)(2,1)} %bitcast.45), channel_id=1, source_target_pairs={{0,8},{1,9},{2,10},{3,11},{4,12},{5,13},{6,14},{7,15},{8,0},{9,1},... | collective-permute-start | bytes 663560 | tf_op jit(solution)/shard_map/ppermute | solution.py:354
  6.3 1.5 %collective-permute-start.5 = (bf16[432,256]{1,0:T(8,128)(2,1)}, bf16[432,256]{1,0:T(8,128)(2,1)S(1)}, u32[]{:S(2)}, u32[]{:S(2)}) collective-permute-start(bf16[432,256]{1,0:T(8,128)(2,1)} %bitcast.46), channel_id=1, source_target_pairs={{0,2},{1,3},{2,0},{3,1},{4,6},{5,7},{6,4},{7,5},{8,10},{9,11},{10,... | collective-permute-start | bytes 663560 | tf_op jit(solution)/shard_map/ppermute | solution.py:354
  7.8 1.0 %reshape.16.clips_ref.refs_1_ = bf16[4,128,256]{2,1,0:T(8,128)(2,1)S(1)} reshape(bf16[4,4,8,4,256]{4,3,2,1,0:T(4,128)(2,1)} %param.5) | data formatting | bytes 524288 | tf_op jit(solution)/shard_map/reshape | solution.py:380
  8.8 1.0 %reshape.17.cotangent_ref = bf16[4,128,256]{2,1,0:T(8,128)(2,1)S(1)} reshape(bf16[4,4,8,4,256]{4,3,2,1,0:T(4,128)(2,1)} %param.9) | data formatting | bytes 524288 | tf_op jit(solution)/shard_map/reshape | solution.py:381
  9.9 0.7 copy-done.1
  10.5 0.7 copy-done.3
  11.2 1.2 %shard_map.76 = (bf16[4,192,2304]{2,1,0:T(8,128)(2,1)S(1)}, f32[8,128]{1,0:T(8,128)S(1)}) custom-call(s32[4]{0:T(128)S(1)} %bitcast.49, bf16[4,128,256]{2,1,0:T(8,128)(2,1)S(1)} %reshape.16.clips_ref.refs_1_, bf16[4,128,256]{2,1,0:T(8,128)(2,1)S(1)} %reshape.17.cotangent_ref, f32[1,256]{1,0:T(1,128)S(1)} %copy-done.1, f32[1,256]{1,0:T(1,128)S(1)} %copy-done.1), custom_call_target="tpu_custom_call" | custom-call | flops 362387872 | bytes 3538944 | tf_op jit(solution)/shard_map/pallas_call | solution.py:416
  12.4 1.6 %collective-permute-done.3.refs_6_ = bf16[432,256]{1,0:T(8,128)(2,1)S(1)} collective-permute-done((bf16[432,256]{1,0:T(8,128)(2,1)}, bf16[432,256]{1,0:T(8,128)(2,1)S(1)}, u32[]{:S(2)}, u32[]{:S(2)}) %collective-permute-start.3) | collective-permute-done | bytes 221216 | tf_op jit(solution)/shard_map/ppermute | solution.py:354
  14.0 1.7 %collective-permute-start.8 = (bf16[432,256]{1,0:T(8,128)(2,1)S(1)}, bf16[432,256]{1,0:T(8,128)(2,1)S(1)}, u32[]{:S(2)}, u32[]{:S(2)}) collective-permute-start(bf16[432,256]{1,0:T(8,128)(2,1)S(1)} %collective-permute-done.3.refs_6_), channel_id=1, source_target_pairs={{0,2},{1,3},{2,0},{3,1},{4,6},{5,7},{6,4},{7,5},{8,10},{9,11},{10,... | collective-permute-start | bytes 663560 | tf_op jit(solution)/shard_map/ppermute | solution.py:354
  15.6 0.9 %collective-permute-done.refs_6_ = bf16[432,256]{1,0:T(8,128)(2,1)S(1)} collective-permute-done((bf16[432,256]{1,0:T(8,128)(2,1)}, bf16[432,256]{1,0:T(8,128)(2,1)S(1)}, u32[]{:S(2)}, u32[]{:S(2)}) %collective-permute-start) | collective-permute-done | bytes 221216 | tf_op jit(solution)/shard_map/ppermute | solution.py:354
  16.5 0.4 collective-permute-start.1
  17.0 1.5 %collective-permute-start.11 = (bf16[432,256]{1,0:T(8,128)(2,1)S(1)}, bf16[432,256]{1,0:T(8,128)(2,1)S(1)}, u32[]{:S(2)}, u32[]{:S(2)}) collective-permute-start(bf16[432,256]{1,0:T(8,128)(2,1)S(1)} %collective-permute-done.refs_6_), channel_id=1, source_target_pairs={{0,2},{1,3},{2,0},{3,1},{4,6},{5,7},{6,4},{7,5},{8,10},{9,11},{10,... | collective-permute-start | bytes 663560 | tf_op jit(solution)/shard_map/ppermute | solution.py:354
  18.5 0.2 collective-permute-start.7
  18.7 2.4 %collective-permute-done.8.refs_8_ = bf16[432,256]{1,0:T(8,128)(2,1)S(1)} collective-permute-done((bf16[432,256]{1,0:T(8,128)(2,1)S(1)}, bf16[432,256]{1,0:T(8,128)(2,1)S(1)}, u32[]{:S(2)}, u32[]{:S(2)}) %collective-permute-start.8) | collective-permute-done | bytes 221216 | tf_op jit(solution)/shard_map/ppermute | solution.py:354
  21.0 1.4 %collective-permute-done.1.refs_10_ = bf16[432,256]{1,0:T(8,128)(2,1)S(1)} collective-permute-done((bf16[432,256]{1,0:T(8,128)(2,1)S(1)}, bf16[432,256]{1,0:T(8,128)(2,1)S(1)}, u32[]{:S(2)}, u32[]{:S(2)}) %collective-permute-start.1) | collective-permute-done | bytes 221216 | tf_op jit(solution)/shard_map/ppermute | solution.py:354
  22.5 1.5 %collective-permute-start.2 = (bf16[432,256]{1,0:T(8,128)(2,1)S(1)}, bf16[432,256]{1,0:T(8,128)(2,1)S(1)}, u32[]{:S(2)}, u32[]{:S(2)}) collective-permute-start(bf16[432,256]{1,0:T(8,128)(2,1)S(1)} %collective-permute-done.1.refs_10_), channel_id=1, source_target_pairs={{0,2},{1,3},{2,0},{3,1},{4,6},{5,7},{6,4},{7,5},{8,10},{9,11},{10,... | collective-permute-start | bytes 663560 | tf_op jit(solution)/shard_map/ppermute | solution.py:354
  24.0 1.8 %collective-permute-done.11.refs_8_ = bf16[432,256]{1,0:T(8,128)(2,1)S(1)} collective-permute-done((bf16[432,256]{1,0:T(8,128)(2,1)S(1)}, bf16[432,256]{1,0:T(8,128)(2,1)S(1)}, u32[]{:S(2)}, u32[]{:S(2)}) %collective-permute-start.11) | collective-permute-done | bytes 221216 | tf_op jit(solution)/shard_map/ppermute | solution.py:354
  25.8 0.5 collective-permute-start.12
  26.3 0.9 %copy-done = bf16[1,432,256]{2,1,0:T(8,128)(2,1)S(1)} copy-done((bf16[1,432,256]{2,1,0:T(8,128)(2,1)S(1)}, bf16[1,432,256]{2,1,0:T(8,128)(2,1)}, u32[]{:S(2)}) %copy-start) | copy-done | bytes 221208
  27.2 1.7 %shard_map.77 = (f32[512,256]{1,0:T(8,128)S(1)}, f32[8,128]{1,0:T(8,128)S(1)}, bf16[3456,256]{1,0:T(8,128)(2,1)S(1)}) custom-call(bf16[4,192,2304]{2,1,0:T(8,128)(2,1)S(1)} %get-tuple-element.35.refs_0_.refs_4_.early_cols_ref, f32[8,128]{1,0:T(8,128)S(1)} %get-tuple-element.37.refs_1_, bf16[432,256]{1,0:T(8,128)(2,1)S(1)} %bitcast.48, ...), custom_call_target="tpu_custom_call" | custom-call | flops 905969664 | bytes 3538944 | tf_op jit(solution)/shard_map/pallas_call | solution.py:438
  28.9 1.1 %collective-permute-done.2.refs_12_ = bf16[432,256]{1,0:T(8,128)(2,1)S(1)} collective-permute-done((bf16[432,256]{1,0:T(8,128)(2,1)S(1)}, bf16[432,256]{1,0:T(8,128)(2,1)S(1)}, u32[]{:S(2)}, u32[]{:S(2)}) %collective-permute-start.2) | collective-permute-done | bytes 221216 | tf_op jit(solution)/shard_map/ppermute | solution.py:354
  30.1 1.5 %collective-permute-done.14.refs_13_ = bf16[432,256]{1,0:T(8,128)(2,1)S(1)} collective-permute-done((bf16[432,256]{1,0:T(8,128)(2,1)S(1)}, bf16[432,256]{1,0:T(8,128)(2,1)S(1)}, u32[]{:S(2)}, u32[]{:S(2)}) %collective-permute-start.14) | collective-permute-done | bytes 221216 | tf_op jit(solution)/shard_map/ppermute | solution.py:354
  31.5 2.2 %shard_map.78 = (bf16[528,256]{1,0:T(8,128)(2,1)S(1)}, bf16[3456,256]{1,0:T(8,128)(2,1)S(1)}) custom-call(s32[4]{0:T(128)S(1)} %bitcast.50, bf16[4,128,256]{2,1,0:T(8,128)(2,1)S(1)} %reshape.16.clips_ref.refs_1_, f32[1,256]{1,0:T(1,128)S(1)} %copy-done.2, f32[8,128]{1,0:T(8,128)S(1)} %get-tuple-element.40.refs_3_, ...), custom_call_target="tpu_custom_call" | custom-call | flops 905969664 | bytes 3538944 | tf_op jit(solution)/shard_map/pallas_call | solution.py:453
  33.8 1.4 %collective-permute-start.15 = (bf16[528,256]{1,0:T(8,128)(2,1)S(1)}, bf16[528,256]{1,0:T(8,128)(2,1)S(1)}, u32[]{:S(2)}, u32[]{:S(2)}) collective-permute-start(bf16[528,256]{1,0:T(8,128)(2,1)S(1)} %get-tuple-element.43.mine_ref), channel_id=1, source_target_pairs={{0,16},{16,0},{1,17},{17,1},{2,18},{18,2},{3,19},{19,3},{4,20},{20... | collective-permute-start | bytes 811016 | tf_op jit(solution)/shard_map/ppermute | solution.py:354
  35.2 7.2 %collective-permute-done.15.theirs_ref = bf16[528,256]{1,0:T(8,128)(2,1)S(1)} collective-permute-done((bf16[528,256]{1,0:T(8,128)(2,1)S(1)}, bf16[528,256]{1,0:T(8,128)(2,1)S(1)}, u32[]{:S(2)}, u32[]{:S(2)}) %collective-permute-start.15) | collective-permute-done | bytes 270368 | tf_op jit(solution)/shard_map/ppermute | solution.py:354
  42.4 3.1 %shard_map.79 = (bf16[512,256]{1,0:T(8,128)(2,1)S(1)}, bf16[512,256]{1,0:T(8,128)(2,1)S(1)}, bf16[256,512]{1,0:T(8,128)(2,1)S(1)}, bf16[4,192,2304]{2,1,0:T(8,12...) custom-call(s32[4]{0:T(128)S(1)} %bitcast.51, ...), custom_call_target="tpu_custom_call" | custom-call | flops 905969664 | bytes 3538944 | tf_op jit(solution)/shard_map/pallas_call | solution.py:465
  45.6 0.5 collective-permute-start.16
  46.1 1.2 %shard_map.80 = (bf16[2,432,256]{2,1,0:T(8,128)(2,1)S(1)}, bf16[2,432,256]{2,1,0:T(8,128)(2,1)S(1)}, bf16[2,432,256]{2,1,0:T(8,128)(2,1)S(1)}, bf16[2,432,256]{2,1,0:T(8,128)(2,1)S(1)}) custom-call(bf16[256,512]{1,0:T(8,128)(2,1)S(1)} %get-tuple-element.51.turned_ref, bf16[4,192,2304]{2,1,0:T(8,128)(2,1)S(1)} %get-tuple-element.52.cols_ref), custom_call_target="tpu_custom_call" | custom-call | flops 905969664 | bytes 3538944 | tf_op jit(solution)/shard_map/pallas_call | solution.py:480
  47.3 0.1 collective-permute-start.20
  47.5 0.4 collective-permute-start.22
  47.9 0.1 convert_add_fusion.2
  48.1 1.4 %collective-permute-start.18 = (bf16[432,256]{1,0:T(8,128)(2,1)S(1)}, bf16[432,256]{1,0:T(8,128)(2,1)S(1)}, u32[]{:S(2)}, u32[]{:S(2)}) collective-permute-start(bf16[432,256]{1,0:T(8,128)(2,1)S(1)} %fusion.12), channel_id=1, source_target_pairs={{0,2},{1,3},{2,0},{3,1},{4,6},{5,7},{6,4},{7,5},{8,10},{9,11},{10,... | collective-permute-start | bytes 663560 | tf_op jit(solution)/shard_map/ppermute | solution.py:354
  49.6 0.1 convert_add_fusion.1
  49.7 0.1 collective-permute-done.22
  49.8 0.1 convert_add_fusion
  50.0 5.5 %collective-permute-done.18 = bf16[432,256]{1,0:T(8,128)(2,1)S(1)} collective-permute-done((bf16[432,256]{1,0:T(8,128)(2,1)S(1)}, bf16[432,256]{1,0:T(8,128)(2,1)S(1)}, u32[]{:S(2)}, u32[]{:S(2)}) %collective-permute-start.18) | collective-permute-done | bytes 221216 | tf_op jit(solution)/shard_map/ppermute | solution.py:354
  55.6 1.4 %collective-permute-start.19 = (bf16[432,256]{1,0:T(8,128)(2,1)S(1)}, bf16[432,256]{1,0:T(8,128)(2,1)S(1)}, u32[]{:S(2)}, u32[]{:S(2)}) collective-permute-start(bf16[432,256]{1,0:T(8,128)(2,1)S(1)} %fusion.13), channel_id=1, source_target_pairs={{0,2},{1,3},{2,0},{3,1},{4,6},{5,7},{6,4},{7,5},{8,10},{9,11},{10,... | collective-permute-start | bytes 663560 | tf_op jit(solution)/shard_map/ppermute | solution.py:354
  57.0 1.2 %collective-permute-start.21 = (bf16[432,256]{1,0:T(8,128)(2,1)S(1)}, bf16[432,256]{1,0:T(8,128)(2,1)S(1)}, u32[]{:S(2)}, u32[]{:S(2)}) collective-permute-start(bf16[432,256]{1,0:T(8,128)(2,1)S(1)} %fusion.8), channel_id=1, source_target_pairs={{0,4},{1,5},{2,6},{3,7},{4,0},{5,1},{6,2},{7,3},{8,12},{9,13},{10,... | collective-permute-start | bytes 663560 | tf_op jit(solution)/shard_map/ppermute | solution.py:354
  58.2 4.0 %collective-permute-done.19 = bf16[432,256]{1,0:T(8,128)(2,1)S(1)} collective-permute-done((bf16[432,256]{1,0:T(8,128)(2,1)S(1)}, bf16[432,256]{1,0:T(8,128)(2,1)S(1)}, u32[]{:S(2)}, u32[]{:S(2)}) %collective-permute-start.19) | collective-permute-done | bytes 221216 | tf_op jit(solution)/shard_map/ppermute | solution.py:354
  62.2 1.3 %collective-permute-start.23 = (bf16[432,256]{1,0:T(8,128)(2,1)S(1)}, bf16[432,256]{1,0:T(8,128)(2,1)S(1)}, u32[]{:S(2)}, u32[]{:S(2)}) collective-permute-start(bf16[432,256]{1,0:T(8,128)(2,1)S(1)} %fusion.14), channel_id=1, source_target_pairs={{0,2},{1,3},{2,0},{3,1},{4,6},{5,7},{6,4},{7,5},{8,10},{9,11},{10,... | collective-permute-start | bytes 663560 | tf_op jit(solution)/shard_map/ppermute | solution.py:354
  63.6 2.4 %collective-permute-start.26 = (bf16[432,256]{1,0:T(8,128)(2,1)S(1)}, bf16[432,256]{1,0:T(8,128)(2,1)S(1)}, u32[]{:S(2)}, u32[]{:S(2)}) collective-permute-start(bf16[432,256]{1,0:T(8,128)(2,1)S(1)} %fusion.11), channel_id=1, source_target_pairs={{0,8},{1,9},{2,10},{3,11},{4,12},{5,13},{6,14},{7,15},{8,0},{9,1},... | collective-permute-start | bytes 663560 | tf_op jit(solution)/shard_map/ppermute | solution.py:354
  66.0 2.2 %collective-permute-done.23 = bf16[432,256]{1,0:T(8,128)(2,1)S(1)} collective-permute-done((bf16[432,256]{1,0:T(8,128)(2,1)S(1)}, bf16[432,256]{1,0:T(8,128)(2,1)S(1)}, u32[]{:S(2)}, u32[]{:S(2)}) %collective-permute-start.23) | collective-permute-done | bytes 221216 | tf_op jit(solution)/shard_map/ppermute | solution.py:354
  68.3 1.4 %collective-permute-start.24 = (bf16[432,256]{1,0:T(8,128)(2,1)S(1)}, bf16[432,256]{1,0:T(8,128)(2,1)S(1)}, u32[]{:S(2)}, u32[]{:S(2)}) collective-permute-start(bf16[432,256]{1,0:T(8,128)(2,1)S(1)} %fusion.15), channel_id=1, source_target_pairs={{0,2},{1,3},{2,0},{3,1},{4,6},{5,7},{6,4},{7,5},{8,10},{9,11},{10,... | collective-permute-start | bytes 663560 | tf_op jit(solution)/shard_map/ppermute | solution.py:354
  69.7 1.2 %collective-permute-start.25 = (bf16[432,256]{1,0:T(8,128)(2,1)S(1)}, bf16[432,256]{1,0:T(8,128)(2,1)S(1)}, u32[]{:S(2)}, u32[]{:S(2)}) collective-permute-start(bf16[432,256]{1,0:T(8,128)(2,1)S(1)} %fusion.1), channel_id=1, source_target_pairs={{0,4},{1,5},{2,6},{3,7},{4,0},{5,1},{6,2},{7,3},{8,12},{9,13},{10,... | collective-permute-start | bytes 663560 | tf_op jit(solution)/shard_map/ppermute | solution.py:354
  70.9 4.5 %shard_map.81 = (bf16[1,4,4,8,4,256]{5,4,3,2,1,0:T(4,128)(2,1)}, bf16[1,4,4,8,4,256]{5,4,3,2,1,0:T(4,128)(2,1)}) custom-call(s32[4]{0:T(128)S(1)} %bitcast.52, bf16[4,128,256]{2,1,0:T(8,128)(2,1)S(1)} %reshape.16.clips_ref.refs_1_, f32[1,256]{1,0:T(1,128)S(1)} %copy-done.2, bf16[512,256]{1,0:T(8,128)(2,1)S(1)} %get-tuple-element.44.hidden_ref, ...), custom_call_target="tpu_custom_call" | custom-call | flops 1811939328 | bytes 3538944 | tf_op jit(solution)/shard_map/pallas_call | solution.py:516
  75.5 1.8 %collective-permute-done.25 = bf16[432,256]{1,0:T(8,128)(2,1)S(1)} collective-permute-done((bf16[432,256]{1,0:T(8,128)(2,1)S(1)}, bf16[432,256]{1,0:T(8,128)(2,1)S(1)}, u32[]{:S(2)}, u32[]{:S(2)}) %collective-permute-start.25) | collective-permute-done | bytes 221216 | tf_op jit(solution)/shard_map/ppermute | solution.py:354
  77.2 0.9 %fusion.6 = f32[1,432,256]{2,1,0:T(8,128)} fusion(f32[2,432,256]{2,1,0:T(8,128)S(1)} %convert_add_fusion, bf16[432,256]{1,0:T(8,128)(2,1)S(1)} %collective-permute-done.26, bf16[432,256]{1,0:T(8,128)(2,1)S(1)} %collective-permute-done.25, bf16[432,256]{1,0:T(8,128)(2,1)S(1)} %collective-permute-done.24), kind=kLoop, calls=%fused_computation.13 | loop fusion | flops 774144 | bytes 1548288 | tf_op jit(solution)/shard_map/broadcast_in_dim | solution.py:535
  (36 shorter events, 0.5 us)
Async XLA Ops:
  0.6 13.3 %collective-permute-start.3 = (bf16[432,256]{1,0:T(8,128)(2,1)}, bf16[432,256]{1,0:T(8,128)(2,1)S(1)}, u32[]{:S(2)}, u32[]{:S(2)}) collective-permute-start(bf16[432,256]{1,0:T(8,128)(2,1)} %bitcast.44), channel_id=1, source_target_pairs={{0,4},{1,5},{2,6},{3,7},{4,0},{5,1},{6,2},{7,3},{8,12},{9,13},{10,... | collective-permute-start | bytes 663560 | tf_op jit(solution)/shard_map/ppermute | solution.py:354
  3.7 12.8 %collective-permute-start = (bf16[432,256]{1,0:T(8,128)(2,1)}, bf16[432,256]{1,0:T(8,128)(2,1)S(1)}, u32[]{:S(2)}, u32[]{:S(2)}) collective-permute-start(bf16[432,256]{1,0:T(8,128)(2,1)} %bitcast.45), channel_id=1, source_target_pairs={{0,8},{1,9},{2,10},{3,11},{4,12},{5,13},{6,14},{7,15},{8,0},{9,1},... | collective-permute-start | bytes 663560 | tf_op jit(solution)/shard_map/ppermute | solution.py:354
  6.3 10.6 %collective-permute-start.5 = (bf16[432,256]{1,0:T(8,128)(2,1)}, bf16[432,256]{1,0:T(8,128)(2,1)S(1)}, u32[]{:S(2)}, u32[]{:S(2)}) collective-permute-start(bf16[432,256]{1,0:T(8,128)(2,1)} %bitcast.46), channel_id=1, source_target_pairs={{0,2},{1,3},{2,0},{3,1},{4,6},{5,7},{6,4},{7,5},{8,10},{9,11},{10,... | collective-permute-start | bytes 663560 | tf_op jit(solution)/shard_map/ppermute | solution.py:354
  7.8 10.7 %collective-permute-start.4 = (bf16[432,256]{1,0:T(8,128)(2,1)}, bf16[432,256]{1,0:T(8,128)(2,1)S(1)}, u32[]{:S(2)}, u32[]{:S(2)}) collective-permute-start(bf16[432,256]{1,0:T(8,128)(2,1)} %bitcast.47), channel_id=1, source_target_pairs={{0,1},{1,0},{2,3},{3,2},{4,5},{5,4},{6,7},{7,6},{8,9},{9,8},{10,11... | collective-permute-start | bytes 663560 | tf_op jit(solution)/shard_map/ppermute | solution.py:354
  8.8 22.7 %copy-start.2 = (f32[1,256]{1,0:T(1,128)S(1)}, f32[1,256]{1,0:T(1,128)}, u32[]{:S(2)}) copy-start(f32[1,256]{1,0:T(1,128)} %gain_ref.5) | copy-start | bytes 3076
  9.9 0.7 copy-start.1
  10.5 0.7 copy-start.3
  14.0 7.1 %collective-permute-start.8 = (bf16[432,256]{1,0:T(8,128)(2,1)S(1)}, bf16[432,256]{1,0:T(8,128)(2,1)S(1)}, u32[]{:S(2)}, u32[]{:S(2)}) collective-permute-start(bf16[432,256]{1,0:T(8,128)(2,1)S(1)} %collective-permute-done.3.refs_6_), channel_id=1, source_target_pairs={{0,2},{1,3},{2,0},{3,1},{4,6},{5,7},{6,4},{7,5},{8,10},{9,11},{10,... | collective-permute-start | bytes 663560 | tf_op jit(solution)/shard_map/ppermute | solution.py:354
  16.5 5.9 %collective-permute-start.1 = (bf16[432,256]{1,0:T(8,128)(2,1)S(1)}, bf16[432,256]{1,0:T(8,128)(2,1)S(1)}, u32[]{:S(2)}, u32[]{:S(2)}) collective-permute-start(bf16[432,256]{1,0:T(8,128)(2,1)S(1)} %collective-permute-done.refs_6_), channel_id=1, source_target_pairs={{0,4},{1,5},{2,6},{3,7},{4,0},{5,1},{6,2},{7,3},{8,12},{9,13},{10,... | collective-permute-start | bytes 663560 | tf_op jit(solution)/shard_map/ppermute | solution.py:354
  17.0 7.0 %collective-permute-start.6 = (bf16[432,256]{1,0:T(8,128)(2,1)S(1)}, bf16[432,256]{1,0:T(8,128)(2,1)S(1)}, u32[]{:S(2)}, u32[]{:S(2)}) collective-permute-start(bf16[432,256]{1,0:T(8,128)(2,1)S(1)} %collective-permute-done.5.refs_4_), channel_id=1, source_target_pairs={{0,1},{1,0},{2,3},{3,2},{4,5},{5,4},{6,7},{7,6},{8,9},{9,8},{10,11... | collective-permute-start | bytes 663560 | tf_op jit(solution)/shard_map/ppermute | solution.py:354
  17.0 8.8 %collective-permute-start.11 = (bf16[432,256]{1,0:T(8,128)(2,1)S(1)}, bf16[432,256]{1,0:T(8,128)(2,1)S(1)}, u32[]{:S(2)}, u32[]{:S(2)}) collective-permute-start(bf16[432,256]{1,0:T(8,128)(2,1)S(1)} %collective-permute-done.refs_6_), channel_id=1, source_target_pairs={{0,2},{1,3},{2,0},{3,1},{4,6},{5,7},{6,4},{7,5},{8,10},{9,11},{10,... | collective-permute-start | bytes 663560 | tf_op jit(solution)/shard_map/ppermute | solution.py:354
  18.5 7.3 %collective-permute-start.7 = (bf16[432,256]{1,0:T(8,128)(2,1)S(1)}, bf16[432,256]{1,0:T(8,128)(2,1)S(1)}, u32[]{:S(2)}, u32[]{:S(2)}) collective-permute-start(bf16[432,256]{1,0:T(8,128)(2,1)S(1)} %collective-permute-done.3.refs_6_), channel_id=1, source_target_pairs={{0,1},{1,0},{2,3},{3,2},{4,5},{5,4},{6,7},{7,6},{8,9},{9,8},{10,11... | collective-permute-start | bytes 663560 | tf_op jit(solution)/shard_map/ppermute | solution.py:354
  21.0 5.3 %collective-permute-start.9 = (bf16[432,256]{1,0:T(8,128)(2,1)S(1)}, bf16[432,256]{1,0:T(8,128)(2,1)S(1)}, u32[]{:S(2)}, u32[]{:S(2)}) collective-permute-start(bf16[432,256]{1,0:T(8,128)(2,1)S(1)} %collective-permute-done.8.refs_8_), channel_id=1, source_target_pairs={{0,1},{1,0},{2,3},{3,2},{4,5},{5,4},{6,7},{7,6},{8,9},{9,8},{10,11... | collective-permute-start | bytes 663560 | tf_op jit(solution)/shard_map/ppermute | solution.py:354
  22.5 7.6 %collective-permute-start.2 = (bf16[432,256]{1,0:T(8,128)(2,1)S(1)}, bf16[432,256]{1,0:T(8,128)(2,1)S(1)}, u32[]{:S(2)}, u32[]{:S(2)}) collective-permute-start(bf16[432,256]{1,0:T(8,128)(2,1)S(1)} %collective-permute-done.1.refs_10_), channel_id=1, source_target_pairs={{0,2},{1,3},{2,0},{3,1},{4,6},{5,7},{6,4},{7,5},{8,10},{9,11},{10,... | collective-permute-start | bytes 663560 | tf_op jit(solution)/shard_map/ppermute | solution.py:354
  23.9 6.1 %collective-permute-start.10 = (bf16[432,256]{1,0:T(8,128)(2,1)S(1)}, bf16[432,256]{1,0:T(8,128)(2,1)S(1)}, u32[]{:S(2)}, u32[]{:S(2)}) collective-permute-start(bf16[432,256]{1,0:T(8,128)(2,1)S(1)} %collective-permute-done.refs_6_), channel_id=1, source_target_pairs={{0,1},{1,0},{2,3},{3,2},{4,5},{5,4},{6,7},{7,6},{8,9},{9,8},{10,11... | collective-permute-start | bytes 663560 | tf_op jit(solution)/shard_map/ppermute | solution.py:354
  25.8 4.3 %collective-permute-start.13 = (bf16[432,256]{1,0:T(8,128)(2,1)S(1)}, bf16[432,256]{1,0:T(8,128)(2,1)S(1)}, u32[]{:S(2)}, u32[]{:S(2)}) collective-permute-start(bf16[432,256]{1,0:T(8,128)(2,1)S(1)} %collective-permute-done.1.refs_10_), channel_id=1, source_target_pairs={{0,1},{1,0},{2,3},{3,2},{4,5},{5,4},{6,7},{7,6},{8,9},{9,8},{10,11... | collective-permute-start | bytes 663560 | tf_op jit(solution)/shard_map/ppermute | solution.py:354
  25.8 4.3 %collective-permute-start.12 = (bf16[432,256]{1,0:T(8,128)(2,1)S(1)}, bf16[432,256]{1,0:T(8,128)(2,1)S(1)}, u32[]{:S(2)}, u32[]{:S(2)}) collective-permute-start(bf16[432,256]{1,0:T(8,128)(2,1)S(1)} %collective-permute-done.11.refs_8_), channel_id=1, source_target_pairs={{0,1},{1,0},{2,3},{3,2},{4,5},{5,4},{6,7},{7,6},{8,9},{9,8},{10,11... | collective-permute-start | bytes 663560 | tf_op jit(solution)/shard_map/ppermute | solution.py:354
  26.3 0.9 %copy-start = (bf16[1,432,256]{2,1,0:T(8,128)(2,1)S(1)}, bf16[1,432,256]{2,1,0:T(8,128)(2,1)}, u32[]{:S(2)}) copy-start(bf16[1,432,256]{2,1,0:T(8,128)(2,1)} %param.8) | copy-start | bytes 663556
  30.1 1.5 %collective-permute-start.14 = (bf16[432,256]{1,0:T(8,128)(2,1)S(1)}, bf16[432,256]{1,0:T(8,128)(2,1)S(1)}, u32[]{:S(2)}, u32[]{:S(2)}) collective-permute-start(bf16[432,256]{1,0:T(8,128)(2,1)S(1)} %collective-permute-done.2.refs_12_), channel_id=1, source_target_pairs={{0,1},{1,0},{2,3},{3,2},{4,5},{5,4},{6,7},{7,6},{8,9},{9,8},{10,11... | collective-permute-start | bytes 663560 | tf_op jit(solution)/shard_map/ppermute | solution.py:354
  33.8 8.6 %collective-permute-start.15 = (bf16[528,256]{1,0:T(8,128)(2,1)S(1)}, bf16[528,256]{1,0:T(8,128)(2,1)S(1)}, u32[]{:S(2)}, u32[]{:S(2)}) collective-permute-start(bf16[528,256]{1,0:T(8,128)(2,1)S(1)} %get-tuple-element.43.mine_ref), channel_id=1, source_target_pairs={{0,16},{16,0},{1,17},{17,1},{2,18},{18,2},{3,19},{19,3},{4,20},{20... | collective-permute-start | bytes 811016 | tf_op jit(solution)/shard_map/ppermute | solution.py:354
  45.5 2.4 %collective-permute-start.17 = (bf16[2,432,256]{2,1,0:T(8,128)(2,1)S(1)}, bf16[2,432,256]{2,1,0:T(8,128)(2,1)S(1)}, u32[]{:S(2)}, u32[]{:S(2)}) collective-permute-start(bf16[2,432,256]{2,1,0:T(8,128)(2,1)S(1)} %get-tuple-element.49), channel_id=1, source_target_pairs={{0,1},{1,0},{2,3},{3,2},{4,5},{5,4},{6,7},{7,6},{8,9},{9,8},{10,11... | collective-permute-start | bytes 1327112 | tf_op jit(solution)/shard_map/ppermute | solution.py:354
  45.6 3.8 %collective-permute-start.16 = (bf16[2,432,256]{2,1,0:T(8,128)(2,1)S(1)}, bf16[2,432,256]{2,1,0:T(8,128)(2,1)S(1)}, u32[]{:S(2)}, u32[]{:S(2)}) collective-permute-start(bf16[2,432,256]{2,1,0:T(8,128)(2,1)S(1)} %get-tuple-element.47), channel_id=1, source_target_pairs={{0,1},{1,0},{2,3},{3,2},{4,5},{5,4},{6,7},{7,6},{8,9},{9,8},{10,11... | collective-permute-start | bytes 1327112 | tf_op jit(solution)/shard_map/ppermute | solution.py:354
  47.3 2.2 %collective-permute-start.20 = (bf16[2,432,256]{2,1,0:T(8,128)(2,1)S(1)}, bf16[2,432,256]{2,1,0:T(8,128)(2,1)S(1)}, u32[]{:S(2)}, u32[]{:S(2)}) collective-permute-start(bf16[2,432,256]{2,1,0:T(8,128)(2,1)S(1)} %get-tuple-element.54), channel_id=1, source_target_pairs={{0,1},{1,0},{2,3},{3,2},{4,5},{5,4},{6,7},{7,6},{8,9},{9,8},{10,11... | collective-permute-start | bytes 1327112 | tf_op jit(solution)/shard_map/ppermute | solution.py:354
  47.5 2.3 %collective-permute-start.22 = (bf16[2,432,256]{2,1,0:T(8,128)(2,1)S(1)}, bf16[2,432,256]{2,1,0:T(8,128)(2,1)S(1)}, u32[]{:S(2)}, u32[]{:S(2)}) collective-permute-start(bf16[2,432,256]{2,1,0:T(8,128)(2,1)S(1)} %get-tuple-element.63), channel_id=1, source_target_pairs={{0,1},{1,0},{2,3},{3,2},{4,5},{5,4},{6,7},{7,6},{8,9},{9,8},{10,11... | collective-permute-start | bytes 1327112 | tf_op jit(solution)/shard_map/ppermute | solution.py:354
  48.1 7.5 %collective-permute-start.18 = (bf16[432,256]{1,0:T(8,128)(2,1)S(1)}, bf16[432,256]{1,0:T(8,128)(2,1)S(1)}, u32[]{:S(2)}, u32[]{:S(2)}) collective-permute-start(bf16[432,256]{1,0:T(8,128)(2,1)S(1)} %fusion.12), channel_id=1, source_target_pairs={{0,2},{1,3},{2,0},{3,1},{4,6},{5,7},{6,4},{7,5},{8,10},{9,11},{10,... | collective-permute-start | bytes 663560 | tf_op jit(solution)/shard_map/ppermute | solution.py:354
  49.6 21.3 %copy-start.4 = (s32[1,4]{1,0:T(1,128)S(1)}, s32[1,4]{1,0:T(1,128)}, u32[]{:S(2)}) copy-start(s32[1,4]{1,0:T(1,128)} %param.6) | copy-start | bytes 52
  55.6 6.6 %collective-permute-start.19 = (bf16[432,256]{1,0:T(8,128)(2,1)S(1)}, bf16[432,256]{1,0:T(8,128)(2,1)S(1)}, u32[]{:S(2)}, u32[]{:S(2)}) collective-permute-start(bf16[432,256]{1,0:T(8,128)(2,1)S(1)} %fusion.13), channel_id=1, source_target_pairs={{0,2},{1,3},{2,0},{3,1},{4,6},{5,7},{6,4},{7,5},{8,10},{9,11},{10,... | collective-permute-start | bytes 663560 | tf_op jit(solution)/shard_map/ppermute | solution.py:354
  57.0 6.6 %collective-permute-start.21 = (bf16[432,256]{1,0:T(8,128)(2,1)S(1)}, bf16[432,256]{1,0:T(8,128)(2,1)S(1)}, u32[]{:S(2)}, u32[]{:S(2)}) collective-permute-start(bf16[432,256]{1,0:T(8,128)(2,1)S(1)} %fusion.8), channel_id=1, source_target_pairs={{0,4},{1,5},{2,6},{3,7},{4,0},{5,1},{6,2},{7,3},{8,12},{9,13},{10,... | collective-permute-start | bytes 663560 | tf_op jit(solution)/shard_map/ppermute | solution.py:354
  62.2 6.0 %collective-permute-start.23 = (bf16[432,256]{1,0:T(8,128)(2,1)S(1)}, bf16[432,256]{1,0:T(8,128)(2,1)S(1)}, u32[]{:S(2)}, u32[]{:S(2)}) collective-permute-start(bf16[432,256]{1,0:T(8,128)(2,1)S(1)} %fusion.14), channel_id=1, source_target_pairs={{0,2},{1,3},{2,0},{3,1},{4,6},{5,7},{6,4},{7,5},{8,10},{9,11},{10,... | collective-permute-start | bytes 663560 | tf_op jit(solution)/shard_map/ppermute | solution.py:354
  63.6 11.8 %collective-permute-start.26 = (bf16[432,256]{1,0:T(8,128)(2,1)S(1)}, bf16[432,256]{1,0:T(8,128)(2,1)S(1)}, u32[]{:S(2)}, u32[]{:S(2)}) collective-permute-start(bf16[432,256]{1,0:T(8,128)(2,1)S(1)} %fusion.11), channel_id=1, source_target_pairs={{0,8},{1,9},{2,10},{3,11},{4,12},{5,13},{6,14},{7,15},{8,0},{9,1},... | collective-permute-start | bytes 663560 | tf_op jit(solution)/shard_map/ppermute | solution.py:354
  68.3 7.2 %collective-permute-start.24 = (bf16[432,256]{1,0:T(8,128)(2,1)S(1)}, bf16[432,256]{1,0:T(8,128)(2,1)S(1)}, u32[]{:S(2)}, u32[]{:S(2)}) collective-permute-start(bf16[432,256]{1,0:T(8,128)(2,1)S(1)} %fusion.15), channel_id=1, source_target_pairs={{0,2},{1,3},{2,0},{3,1},{4,6},{5,7},{6,4},{7,5},{8,10},{9,11},{10,... | collective-permute-start | bytes 663560 | tf_op jit(solution)/shard_map/ppermute | solution.py:354
  69.7 7.6 %collective-permute-start.25 = (bf16[432,256]{1,0:T(8,128)(2,1)S(1)}, bf16[432,256]{1,0:T(8,128)(2,1)S(1)}, u32[]{:S(2)}, u32[]{:S(2)}) collective-permute-start(bf16[432,256]{1,0:T(8,128)(2,1)S(1)} %fusion.1), channel_id=1, source_target_pairs={{0,4},{1,5},{2,6},{3,7},{4,0},{5,1},{6,2},{7,3},{8,12},{9,13},{10,... | collective-permute-start | bytes 663560 | tf_op jit(solution)/shard_map/ppermute | solution.py:354

commit v4 on v3

--- a/solution.py
+++ b/solution.py
@@ -477,6 +477,15 @@
         ],
     )(order, flat_clips, flat_cotangent, gains, mine, theirs, early_cols)
 
+    if split:
+
+        def core_sum(kept, sent):
+            both = widen(kept) + widen(swap(sent, "fsdp", 1))
+            return both[0], both[1]
+
+        kept_12, send_12 = core_sum(*far_sums[:2])
+        send_12 = narrow(send_12)
+
     near_sums = call(
         rest_kernel,
         0.5,
@@ -487,26 +496,24 @@
     )(turned, late_cols)
 
     if split:
-
-        def core_sum(kept, sent):
-            both = widen(kept) + widen(swap(sent, "fsdp", 1))
-            return both[0], narrow(both[1])
-
-        kept_12, send_12 = core_sum(*far_sums[:2])
         kept_8, send_8 = core_sum(*far_sums[2:])
         kept_4, send_4 = core_sum(*near_sums[:2])
         kept_0, send_0 = core_sum(*near_sums[2:])
+        send_8 = narrow(send_8)
+        side_4 = swap(narrow(send_4), "fsdp", 4)
         came_12 = swap(send_12, "fsdp", 2)
-        came_12, send_8 = together(came_12, send_8)
+        for_8 = narrow(kept_12 + widen(came_12))
+        from_4 = swap(for_8, "fsdp", 4)
+        for_8, send_8 = together(for_8, send_8)
         came_8 = swap(send_8, "fsdp", 2)
-        from_4 = swap(narrow(kept_12 + widen(came_12)), "fsdp", 4)
-        came_8, send_4 = together(came_8, send_4)
-        came_4 = swap(send_4, "fsdp", 2)
         ready = narrow(kept_8 + widen(came_8) + widen(from_4))
         from_8 = swap(ready, "fsdp", 8)
-        came_4, send_0 = together(came_4, send_0)
+        send_0 = narrow(send_0 + widen(side_4))
+        came_8, send_0 = together(came_8, send_0)
         came_0 = swap(send_0, "fsdp", 2)
-        late = swap(narrow(kept_4 + widen(came_4)), "fsdp", 4)
+        direct_4 = narrow(kept_4)
+        from_4, direct_4 = together(from_4, direct_4)
+        late = swap(direct_4, "fsdp", 4)
         weight_grad = (kept_0 + widen(came_0) + widen(late) + widen(from_8)) * factor
         grad, _ = together(grad, ready)
     else:

time: 78.4 us -> 75.6 us (0.964)
  waiting for transfers between devices: 31.5 us -> 29.3 us
    ppermute x27, waiting for transfers between devices: 31.5 us -> 29.3 us  [swap(): lax.ppermute(value, axis, [(i, i ^ by) for i in range(lax.axis_size(axis))])]
where the time goes in v4:
time: 75.6 us; the launch traced here: 75.3 us
  waiting for transfers between devices  29.3 us (39%)
  starting transfers between devices  25.4 us (34%)
  Pallas kernels  14 us (19%)
  local copies, waits for them, and re-layouts  4.39 us (6%)
  other arithmetic  1.48 us (2%)
  between operations  0.81 us (1%)
    ppermute x27, waiting for transfers between devices, swap(): lax.ppermute(value, axis, [(i, i ^ by) for i in range(lax.axis_size(axis))])  29.3 us
    ppermute x27, starting transfers between devices, swap(): lax.ppermute(value, axis, [(i, i ^ by) for i in range(lax.axis_size(axis))])  25.4 us
    pallas_call x1, Pallas kernels, on_device(): call(last_kernel, 1.0, limit=LAST_VMEM_LIMIT, out_shape=[jax.ShapeDtypeSt...  4.53 us
    pallas_call x1, Pallas kernels, on_device(): call(gradient_kernel, 0.5, out_shape=[volume, volume, turned_out, cols_ou...  3.14 us
    unnamed x10, local copies, waits for them, and re-layouts  2.28 us
    pallas_call x1, Pallas kernels, on_device(): call(lambda dims, split, *refs: far_kernel(dims, split, count, *refs), 0....  2.25 us
    pallas_call x1, Pallas kernels, on_device(): call(lambda dims, split, *refs: near_kernel(dims, split, count, *refs), 0...  1.7 us
  transfers between devices with their start and end apart: 27, of which 13 were waited for; matrix products, arithmetic and copies ran while one was open for 3% of the time, Pallas kernels for 11%

profile of v4, /device:TPU:0, one launch (start us, length us, event | category | flops | bytes accessed | tf_op | source)
XLA Modules:
  0.0 75.3 jit_solution(10942016533839779491)
XLA Ops:
  0.6 3.1 %collective-permute-start.3 = (bf16[432,256]{1,0:T(8,128)(2,1)}, bf16[432,256]{1,0:T(8,128)(2,1)S(1)}, u32[]{:S(2)}, u32[]{:S(2)}) collective-permute-start(bf16[432,256]{1,0:T(8,128)(2,1)} %bitcast.44), channel_id=1, source_target_pairs={{0,4},{1,5},{2,6},{3,7},{4,0},{5,1},{6,2},{7,3},{8,12},{9,13},{10,... | collective-permute-start | bytes 663560 | tf_op jit(solution)/shard_map/ppermute | solution.py:354
  3.7 2.6 %collective-permute-start = (bf16[432,256]{1,0:T(8,128)(2,1)}, bf16[432,256]{1,0:T(8,128)(2,1)S(1)}, u32[]{:S(2)}, u32[]{:S(2)}) collective-permute-start(bf16[432,256]{1,0:T(8,128)(2,1)} %bitcast.45), channel_id=1, source_target_pairs={{0,8},{1,9},{2,10},{3,11},{4,12},{5,13},{6,14},{7,15},{8,0},{9,1},... | collective-permute-start | bytes 663560 | tf_op jit(solution)/shard_map/ppermute | solution.py:354
  6.3 1.5 %collective-permute-start.5 = (bf16[432,256]{1,0:T(8,128)(2,1)}, bf16[432,256]{1,0:T(8,128)(2,1)S(1)}, u32[]{:S(2)}, u32[]{:S(2)}) collective-permute-start(bf16[432,256]{1,0:T(8,128)(2,1)} %bitcast.46), channel_id=1, source_target_pairs={{0,2},{1,3},{2,0},{3,1},{4,6},{5,7},{6,4},{7,5},{8,10},{9,11},{10,... | collective-permute-start | bytes 663560 | tf_op jit(solution)/shard_map/ppermute | solution.py:354
  7.8 1.0 %reshape.16.clips_ref.refs_1_ = bf16[4,128,256]{2,1,0:T(8,128)(2,1)S(1)} reshape(bf16[4,4,8,4,256]{4,3,2,1,0:T(4,128)(2,1)} %param.5) | data formatting | bytes 524288 | tf_op jit(solution)/shard_map/reshape | solution.py:380
  8.8 1.0 %reshape.17.cotangent_ref = bf16[4,128,256]{2,1,0:T(8,128)(2,1)S(1)} reshape(bf16[4,4,8,4,256]{4,3,2,1,0:T(4,128)(2,1)} %param.9) | data formatting | bytes 524288 | tf_op jit(solution)/shard_map/reshape | solution.py:381
  9.9 0.7 copy-done.1
  10.5 0.7 copy-done.3
  11.2 1.2 %shard_map.76 = (bf16[4,192,2304]{2,1,0:T(8,128)(2,1)S(1)}, f32[8,128]{1,0:T(8,128)S(1)}) custom-call(s32[4]{0:T(128)S(1)} %bitcast.49, bf16[4,128,256]{2,1,0:T(8,128)(2,1)S(1)} %reshape.16.clips_ref.refs_1_, bf16[4,128,256]{2,1,0:T(8,128)(2,1)S(1)} %reshape.17.cotangent_ref, f32[1,256]{1,0:T(1,128)S(1)} %copy-done.1, f32[1,256]{1,0:T(1,128)S(1)} %copy-done.1), custom_call_target="tpu_custom_call" | custom-call | flops 362387872 | bytes 3538944 | tf_op jit(solution)/shard_map/pallas_call | solution.py:416
  12.4 1.6 %collective-permute-done.3.refs_6_ = bf16[432,256]{1,0:T(8,128)(2,1)S(1)} collective-permute-done((bf16[432,256]{1,0:T(8,128)(2,1)}, bf16[432,256]{1,0:T(8,128)(2,1)S(1)}, u32[]{:S(2)}, u32[]{:S(2)}) %collective-permute-start.3) | collective-permute-done | bytes 221216 | tf_op jit(solution)/shard_map/ppermute | solution.py:354
  14.0 1.7 %collective-permute-start.8 = (bf16[432,256]{1,0:T(8,128)(2,1)S(1)}, bf16[432,256]{1,0:T(8,128)(2,1)S(1)}, u32[]{:S(2)}, u32[]{:S(2)}) collective-permute-start(bf16[432,256]{1,0:T(8,128)(2,1)S(1)} %collective-permute-done.3.refs_6_), channel_id=1, source_target_pairs={{0,2},{1,3},{2,0},{3,1},{4,6},{5,7},{6,4},{7,5},{8,10},{9,11},{10,... | collective-permute-start | bytes 663560 | tf_op jit(solution)/shard_map/ppermute | solution.py:354
  15.6 0.9 %collective-permute-done.refs_6_ = bf16[432,256]{1,0:T(8,128)(2,1)S(1)} collective-permute-done((bf16[432,256]{1,0:T(8,128)(2,1)}, bf16[432,256]{1,0:T(8,128)(2,1)S(1)}, u32[]{:S(2)}, u32[]{:S(2)}) %collective-permute-start) | collective-permute-done | bytes 221216 | tf_op jit(solution)/shard_map/ppermute | solution.py:354
  16.5 0.4 collective-permute-start.1
  17.0 1.5 %collective-permute-start.11 = (bf16[432,256]{1,0:T(8,128)(2,1)S(1)}, bf16[432,256]{1,0:T(8,128)(2,1)S(1)}, u32[]{:S(2)}, u32[]{:S(2)}) collective-permute-start(bf16[432,256]{1,0:T(8,128)(2,1)S(1)} %collective-permute-done.refs_6_), channel_id=1, source_target_pairs={{0,2},{1,3},{2,0},{3,1},{4,6},{5,7},{6,4},{7,5},{8,10},{9,11},{10,... | collective-permute-start | bytes 663560 | tf_op jit(solution)/shard_map/ppermute | solution.py:354
  18.5 0.2 collective-permute-start.7
  18.7 2.4 %collective-permute-done.8.refs_8_ = bf16[432,256]{1,0:T(8,128)(2,1)S(1)} collective-permute-done((bf16[432,256]{1,0:T(8,128)(2,1)S(1)}, bf16[432,256]{1,0:T(8,128)(2,1)S(1)}, u32[]{:S(2)}, u32[]{:S(2)}) %collective-permute-start.8) | collective-permute-done | bytes 221216 | tf_op jit(solution)/shard_map/ppermute | solution.py:354
  21.0 1.4 %collective-permute-done.1.refs_10_ = bf16[432,256]{1,0:T(8,128)(2,1)S(1)} collective-permute-done((bf16[432,256]{1,0:T(8,128)(2,1)S(1)}, bf16[432,256]{1,0:T(8,128)(2,1)S(1)}, u32[]{:S(2)}, u32[]{:S(2)}) %collective-permute-start.1) | collective-permute-done | bytes 221216 | tf_op jit(solution)/shard_map/ppermute | solution.py:354
  22.5 1.5 %collective-permute-start.2 = (bf16[432,256]{1,0:T(8,128)(2,1)S(1)}, bf16[432,256]{1,0:T(8,128)(2,1)S(1)}, u32[]{:S(2)}, u32[]{:S(2)}) collective-permute-start(bf16[432,256]{1,0:T(8,128)(2,1)S(1)} %collective-permute-done.1.refs_10_), channel_id=1, source_target_pairs={{0,2},{1,3},{2,0},{3,1},{4,6},{5,7},{6,4},{7,5},{8,10},{9,11},{10,... | collective-permute-start | bytes 663560 | tf_op jit(solution)/shard_map/ppermute | solution.py:354
  24.0 1.8 %collective-permute-done.11.refs_8_ = bf16[432,256]{1,0:T(8,128)(2,1)S(1)} collective-permute-done((bf16[432,256]{1,0:T(8,128)(2,1)S(1)}, bf16[432,256]{1,0:T(8,128)(2,1)S(1)}, u32[]{:S(2)}, u32[]{:S(2)}) %collective-permute-start.11) | collective-permute-done | bytes 221216 | tf_op jit(solution)/shard_map/ppermute | solution.py:354
  25.8 0.5 collective-permute-start.12
  26.3 0.9 %copy-done = bf16[1,432,256]{2,1,0:T(8,128)(2,1)S(1)} copy-done((bf16[1,432,256]{2,1,0:T(8,128)(2,1)S(1)}, bf16[1,432,256]{2,1,0:T(8,128)(2,1)}, u32[]{:S(2)}) %copy-start) | copy-done | bytes 221208
  27.2 1.7 %shard_map.77 = (f32[512,256]{1,0:T(8,128)S(1)}, f32[8,128]{1,0:T(8,128)S(1)}, bf16[3456,256]{1,0:T(8,128)(2,1)S(1)}) custom-call(bf16[4,192,2304]{2,1,0:T(8,128)(2,1)S(1)} %get-tuple-element.32.refs_0_.refs_4_.early_cols_ref, f32[8,128]{1,0:T(8,128)S(1)} %get-tuple-element.34.refs_1_, bf16[432,256]{1,0:T(8,128)(2,1)S(1)} %bitcast.48, ...), custom_call_target="tpu_custom_call" | custom-call | flops 905969664 | bytes 3538944 | tf_op jit(solution)/shard_map/pallas_call | solution.py:438
  28.9 1.1 %collective-permute-done.2.refs_12_ = bf16[432,256]{1,0:T(8,128)(2,1)S(1)} collective-permute-done((bf16[432,256]{1,0:T(8,128)(2,1)S(1)}, bf16[432,256]{1,0:T(8,128)(2,1)S(1)}, u32[]{:S(2)}, u32[]{:S(2)}) %collective-permute-start.2) | collective-permute-done | bytes 221216 | tf_op jit(solution)/shard_map/ppermute | solution.py:354
  30.1 1.5 %collective-permute-done.14.refs_13_ = bf16[432,256]{1,0:T(8,128)(2,1)S(1)} collective-permute-done((bf16[432,256]{1,0:T(8,128)(2,1)S(1)}, bf16[432,256]{1,0:T(8,128)(2,1)S(1)}, u32[]{:S(2)}, u32[]{:S(2)}) %collective-permute-start.14) | collective-permute-done | bytes 221216 | tf_op jit(solution)/shard_map/ppermute | solution.py:354
  31.5 2.2 %shard_map.78 = (bf16[528,256]{1,0:T(8,128)(2,1)S(1)}, bf16[3456,256]{1,0:T(8,128)(2,1)S(1)}) custom-call(s32[4]{0:T(128)S(1)} %bitcast.50, bf16[4,128,256]{2,1,0:T(8,128)(2,1)S(1)} %reshape.16.clips_ref.refs_1_, f32[1,256]{1,0:T(1,128)S(1)} %copy-done.2, f32[8,128]{1,0:T(8,128)S(1)} %get-tuple-element.37.refs_3_, ...), custom_call_target="tpu_custom_call" | custom-call | flops 905969664 | bytes 3538944 | tf_op jit(solution)/shard_map/pallas_call | solution.py:453
  33.8 1.4 %collective-permute-start.15 = (bf16[528,256]{1,0:T(8,128)(2,1)S(1)}, bf16[528,256]{1,0:T(8,128)(2,1)S(1)}, u32[]{:S(2)}, u32[]{:S(2)}) collective-permute-start(bf16[528,256]{1,0:T(8,128)(2,1)S(1)} %get-tuple-element.40.mine_ref), channel_id=1, source_target_pairs={{0,16},{16,0},{1,17},{17,1},{2,18},{18,2},{3,19},{19,3},{4,20},{20... | collective-permute-start | bytes 811016 | tf_op jit(solution)/shard_map/ppermute | solution.py:354
  35.2 7.2 %collective-permute-done.15.theirs_ref = bf16[528,256]{1,0:T(8,128)(2,1)S(1)} collective-permute-done((bf16[528,256]{1,0:T(8,128)(2,1)S(1)}, bf16[528,256]{1,0:T(8,128)(2,1)S(1)}, u32[]{:S(2)}, u32[]{:S(2)}) %collective-permute-start.15) | collective-permute-done | bytes 270368 | tf_op jit(solution)/shard_map/ppermute | solution.py:354
  42.4 3.1 %shard_map.79 = (bf16[512,256]{1,0:T(8,128)(2,1)S(1)}, bf16[512,256]{1,0:T(8,128)(2,1)S(1)}, bf16[256,512]{1,0:T(8,128)(2,1)S(1)}, bf16[4,192,2304]{2,1,0:T(8,12...) custom-call(s32[4]{0:T(128)S(1)} %bitcast.51, ...), custom_call_target="tpu_custom_call" | custom-call | flops 905969664 | bytes 3538944 | tf_op jit(solution)/shard_map/pallas_call | solution.py:465
  45.6 0.5 collective-permute-start.16
  46.1 1.2 %shard_map.81 = (bf16[2,432,256]{2,1,0:T(8,128)(2,1)S(1)}, bf16[2,432,256]{2,1,0:T(8,128)(2,1)S(1)}, bf16[2,432,256]{2,1,0:T(8,128)(2,1)S(1)}, bf16[2,432,256]{2,1,0:T(8,128)(2,1)S(1)}) custom-call(bf16[256,512]{1,0:T(8,128)(2,1)S(1)} %get-tuple-element.53.turned_ref, bf16[4,192,2304]{2,1,0:T(8,128)(2,1)S(1)} %get-tuple-element.54.cols_ref), custom_call_target="tpu_custom_call" | custom-call | flops 905969664 | bytes 3538944 | tf_op jit(solution)/shard_map/pallas_call | solution.py:489
  47.3 0.1 collective-permute-start.21
  47.5 0.4 collective-permute-start.22
  47.9 0.1 convert_add_fusion.1
  48.0 1.4 %collective-permute-start.18 = (bf16[432,256]{1,0:T(8,128)(2,1)S(1)}, bf16[432,256]{1,0:T(8,128)(2,1)S(1)}, u32[]{:S(2)}, u32[]{:S(2)}) collective-permute-start(bf16[432,256]{1,0:T(8,128)(2,1)S(1)} %fusion.12), channel_id=1, source_target_pairs={{0,2},{1,3},{2,0},{3,1},{4,6},{5,7},{6,4},{7,5},{8,10},{9,11},{10,... | collective-permute-start | bytes 663560 | tf_op jit(solution)/shard_map/ppermute | solution.py:354
  49.4 0.4 collective-permute-done.22
  49.8 0.1 add_convert_fusion
  50.0 1.1 %collective-permute-start.23 = (bf16[432,256]{1,0:T(8,128)(2,1)S(1)}, bf16[432,256]{1,0:T(8,128)(2,1)S(1)}, u32[]{:S(2)}, u32[]{:S(2)}) collective-permute-start(bf16[432,256]{1,0:T(8,128)(2,1)S(1)} %get-tuple-element.61), channel_id=1, source_target_pairs={{0,4},{1,5},{2,6},{3,7},{4,0},{5,1},{6,2},{7,3},{8,12},{9,13},{10,... | collective-permute-start | bytes 663560 | tf_op jit(solution)/shard_map/ppermute | solution.py:354
  51.2 0.1 convert_add_fusion
  51.4 4.2 %collective-permute-done.18 = bf16[432,256]{1,0:T(8,128)(2,1)S(1)} collective-permute-done((bf16[432,256]{1,0:T(8,128)(2,1)S(1)}, bf16[432,256]{1,0:T(8,128)(2,1)S(1)}, u32[]{:S(2)}, u32[]{:S(2)}) %collective-permute-start.18) | collective-permute-done | bytes 221216 | tf_op jit(solution)/shard_map/ppermute | solution.py:354
  55.6 1.1 %collective-permute-start.20 = (bf16[432,256]{1,0:T(8,128)(2,1)S(1)}, bf16[432,256]{1,0:T(8,128)(2,1)S(1)}, u32[]{:S(2)}, u32[]{:S(2)}) collective-permute-start(bf16[432,256]{1,0:T(8,128)(2,1)S(1)} %fusion.8), channel_id=1, source_target_pairs={{0,4},{1,5},{2,6},{3,7},{4,0},{5,1},{6,2},{7,3},{8,12},{9,13},{10,... | collective-permute-start | bytes 663560 | tf_op jit(solution)/shard_map/ppermute | solution.py:354
  56.7 1.5 %collective-permute-start.19 = (bf16[432,256]{1,0:T(8,128)(2,1)S(1)}, bf16[432,256]{1,0:T(8,128)(2,1)S(1)}, u32[]{:S(2)}, u32[]{:S(2)}) collective-permute-start(bf16[432,256]{1,0:T(8,128)(2,1)S(1)} %fusion.13), channel_id=1, source_target_pairs={{0,2},{1,3},{2,0},{3,1},{4,6},{5,7},{6,4},{7,5},{8,10},{9,11},{10,... | collective-permute-start | bytes 663560 | tf_op jit(solution)/shard_map/ppermute | solution.py:354
  58.3 4.7 %collective-permute-done.19 = bf16[432,256]{1,0:T(8,128)(2,1)S(1)} collective-permute-done((bf16[432,256]{1,0:T(8,128)(2,1)S(1)}, bf16[432,256]{1,0:T(8,128)(2,1)S(1)}, u32[]{:S(2)}, u32[]{:S(2)}) %collective-permute-start.19) | collective-permute-done | bytes 221216 | tf_op jit(solution)/shard_map/ppermute | solution.py:354
  63.1 1.9 %collective-permute-start.26 = (bf16[432,256]{1,0:T(8,128)(2,1)S(1)}, bf16[432,256]{1,0:T(8,128)(2,1)S(1)}, u32[]{:S(2)}, u32[]{:S(2)}) collective-permute-start(bf16[432,256]{1,0:T(8,128)(2,1)S(1)} %fusion.11), channel_id=1, source_target_pairs={{0,8},{1,9},{2,10},{3,11},{4,12},{5,13},{6,14},{7,15},{8,0},{9,1},... | collective-permute-start | bytes 663560 | tf_op jit(solution)/shard_map/ppermute | solution.py:354
  65.0 1.2 %collective-permute-start.25 = (bf16[432,256]{1,0:T(8,128)(2,1)S(1)}, bf16[432,256]{1,0:T(8,128)(2,1)S(1)}, u32[]{:S(2)}, u32[]{:S(2)}) collective-permute-start(bf16[432,256]{1,0:T(8,128)(2,1)S(1)} %get-tuple-element.60), channel_id=1, source_target_pairs={{0,4},{1,5},{2,6},{3,7},{4,0},{5,1},{6,2},{7,3},{8,12},{9,13},{10,... | collective-permute-start | bytes 663560 | tf_op jit(solution)/shard_map/ppermute | solution.py:354
  66.2 1.5 %collective-permute-start.24 = (bf16[432,256]{1,0:T(8,128)(2,1)S(1)}, bf16[432,256]{1,0:T(8,128)(2,1)S(1)}, u32[]{:S(2)}, u32[]{:S(2)}) collective-permute-start(bf16[432,256]{1,0:T(8,128)(2,1)S(1)} %fusion.1), channel_id=1, source_target_pairs={{0,2},{1,3},{2,0},{3,1},{4,6},{5,7},{6,4},{7,5},{8,10},{9,11},{10,... | collective-permute-start | bytes 663560 | tf_op jit(solution)/shard_map/ppermute | solution.py:354
  67.8 4.5 %shard_map.80 = (bf16[1,4,4,8,4,256]{5,4,3,2,1,0:T(4,128)(2,1)}, bf16[1,4,4,8,4,256]{5,4,3,2,1,0:T(4,128)(2,1)}) custom-call(s32[4]{0:T(128)S(1)} %bitcast.52, bf16[4,128,256]{2,1,0:T(8,128)(2,1)S(1)} %reshape.16.clips_ref.refs_1_, f32[1,256]{1,0:T(1,128)S(1)} %copy-done.2, bf16[512,256]{1,0:T(8,128)(2,1)S(1)} %get-tuple-element.41.hidden_ref, ...), custom_call_target="tpu_custom_call" | custom-call | flops 1811939328 | bytes 3538944 | tf_op jit(solution)/shard_map/pallas_call | solution.py:523
  72.3 2.0 %collective-permute-done.26 = bf16[432,256]{1,0:T(8,128)(2,1)S(1)} collective-permute-done((bf16[432,256]{1,0:T(8,128)(2,1)S(1)}, bf16[432,256]{1,0:T(8,128)(2,1)S(1)}, u32[]{:S(2)}, u32[]{:S(2)}) %collective-permute-start.26) | collective-permute-done | bytes 221216 | tf_op jit(solution)/shard_map/ppermute | solution.py:354
  74.3 0.1 collective-permute-done.25
  74.4 0.9 %fusion.6 = f32[1,432,256]{2,1,0:T(8,128)} fusion(f32[2,432,256]{2,1,0:T(8,128)S(1)} %convert_add_fusion, bf16[432,256]{1,0:T(8,128)(2,1)S(1)} %collective-permute-done.26, bf16[432,256]{1,0:T(8,128)(2,1)S(1)} %collective-permute-done.25, bf16[432,256]{1,0:T(8,128)(2,1)S(1)} %collective-permute-done.24), kind=kLoop, calls=%fused_computation.12 | loop fusion | flops 774144 | bytes 1548288 | tf_op jit(solution)/shard_map/broadcast_in_dim | solution.py:542
  (35 shorter events, 0.5 us)
Async XLA Ops:
  0.6 13.3 %collective-permute-start.3 = (bf16[432,256]{1,0:T(8,128)(2,1)}, bf16[432,256]{1,0:T(8,128)(2,1)S(1)}, u32[]{:S(2)}, u32[]{:S(2)}) collective-permute-start(bf16[432,256]{1,0:T(8,128)(2,1)} %bitcast.44), channel_id=1, source_target_pairs={{0,4},{1,5},{2,6},{3,7},{4,0},{5,1},{6,2},{7,3},{8,12},{9,13},{10,... | collective-permute-start | bytes 663560 | tf_op jit(solution)/shard_map/ppermute | solution.py:354
  3.7 12.8 %collective-permute-start = (bf16[432,256]{1,0:T(8,128)(2,1)}, bf16[432,256]{1,0:T(8,128)(2,1)S(1)}, u32[]{:S(2)}, u32[]{:S(2)}) collective-permute-start(bf16[432,256]{1,0:T(8,128)(2,1)} %bitcast.45), channel_id=1, source_target_pairs={{0,8},{1,9},{2,10},{3,11},{4,12},{5,13},{6,14},{7,15},{8,0},{9,1},... | collective-permute-start | bytes 663560 | tf_op jit(solution)/shard_map/ppermute | solution.py:354
  6.3 10.6 %collective-permute-start.5 = (bf16[432,256]{1,0:T(8,128)(2,1)}, bf16[432,256]{1,0:T(8,128)(2,1)S(1)}, u32[]{:S(2)}, u32[]{:S(2)}) collective-permute-start(bf16[432,256]{1,0:T(8,128)(2,1)} %bitcast.46), channel_id=1, source_target_pairs={{0,2},{1,3},{2,0},{3,1},{4,6},{5,7},{6,4},{7,5},{8,10},{9,11},{10,... | collective-permute-start | bytes 663560 | tf_op jit(solution)/shard_map/ppermute | solution.py:354
  7.8 10.7 %collective-permute-start.4 = (bf16[432,256]{1,0:T(8,128)(2,1)}, bf16[432,256]{1,0:T(8,128)(2,1)S(1)}, u32[]{:S(2)}, u32[]{:S(2)}) collective-permute-start(bf16[432,256]{1,0:T(8,128)(2,1)} %bitcast.47), channel_id=1, source_target_pairs={{0,1},{1,0},{2,3},{3,2},{4,5},{5,4},{6,7},{7,6},{8,9},{9,8},{10,11... | collective-permute-start | bytes 663560 | tf_op jit(solution)/shard_map/ppermute | solution.py:354
  8.8 22.7 %copy-start.2 = (f32[1,256]{1,0:T(1,128)S(1)}, f32[1,256]{1,0:T(1,128)}, u32[]{:S(2)}) copy-start(f32[1,256]{1,0:T(1,128)} %gain_ref.5) | copy-start | bytes 3076
  9.9 0.7 copy-start.1
  10.5 0.7 copy-start.3
  14.0 7.1 %collective-permute-start.8 = (bf16[432,256]{1,0:T(8,128)(2,1)S(1)}, bf16[432,256]{1,0:T(8,128)(2,1)S(1)}, u32[]{:S(2)}, u32[]{:S(2)}) collective-permute-start(bf16[432,256]{1,0:T(8,128)(2,1)S(1)} %collective-permute-done.3.refs_6_), channel_id=1, source_target_pairs={{0,2},{1,3},{2,0},{3,1},{4,6},{5,7},{6,4},{7,5},{8,10},{9,11},{10,... | collective-permute-start | bytes 663560 | tf_op jit(solution)/shard_map/ppermute | solution.py:354
  16.5 5.9 %collective-permute-start.1 = (bf16[432,256]{1,0:T(8,128)(2,1)S(1)}, bf16[432,256]{1,0:T(8,128)(2,1)S(1)}, u32[]{:S(2)}, u32[]{:S(2)}) collective-permute-start(bf16[432,256]{1,0:T(8,128)(2,1)S(1)} %collective-permute-done.refs_6_), channel_id=1, source_target_pairs={{0,4},{1,5},{2,6},{3,7},{4,0},{5,1},{6,2},{7,3},{8,12},{9,13},{10,... | collective-permute-start | bytes 663560 | tf_op jit(solution)/shard_map/ppermute | solution.py:354
  17.0 7.0 %collective-permute-start.6 = (bf16[432,256]{1,0:T(8,128)(2,1)S(1)}, bf16[432,256]{1,0:T(8,128)(2,1)S(1)}, u32[]{:S(2)}, u32[]{:S(2)}) collective-permute-start(bf16[432,256]{1,0:T(8,128)(2,1)S(1)} %collective-permute-done.5.refs_4_), channel_id=1, source_target_pairs={{0,1},{1,0},{2,3},{3,2},{4,5},{5,4},{6,7},{7,6},{8,9},{9,8},{10,11... | collective-permute-start | bytes 663560 | tf_op jit(solution)/shard_map/ppermute | solution.py:354
  17.0 8.8 %collective-permute-start.11 = (bf16[432,256]{1,0:T(8,128)(2,1)S(1)}, bf16[432,256]{1,0:T(8,128)(2,1)S(1)}, u32[]{:S(2)}, u32[]{:S(2)}) collective-permute-start(bf16[432,256]{1,0:T(8,128)(2,1)S(1)} %collective-permute-done.refs_6_), channel_id=1, source_target_pairs={{0,2},{1,3},{2,0},{3,1},{4,6},{5,7},{6,4},{7,5},{8,10},{9,11},{10,... | collective-permute-start | bytes 663560 | tf_op jit(solution)/shard_map/ppermute | solution.py:354
  18.5 7.3 %collective-permute-start.7 = (bf16[432,256]{1,0:T(8,128)(2,1)S(1)}, bf16[432,256]{1,0:T(8,128)(2,1)S(1)}, u32[]{:S(2)}, u32[]{:S(2)}) collective-permute-start(bf16[432,256]{1,0:T(8,128)(2,1)S(1)} %collective-permute-done.3.refs_6_), channel_id=1, source_target_pairs={{0,1},{1,0},{2,3},{3,2},{4,5},{5,4},{6,7},{7,6},{8,9},{9,8},{10,11... | collective-permute-start | bytes 663560 | tf_op jit(solution)/shard_map/ppermute | solution.py:354
  21.0 5.3 %collective-permute-start.9 = (bf16[432,256]{1,0:T(8,128)(2,1)S(1)}, bf16[432,256]{1,0:T(8,128)(2,1)S(1)}, u32[]{:S(2)}, u32[]{:S(2)}) collective-permute-start(bf16[432,256]{1,0:T(8,128)(2,1)S(1)} %collective-permute-done.8.refs_8_), channel_id=1, source_target_pairs={{0,1},{1,0},{2,3},{3,2},{4,5},{5,4},{6,7},{7,6},{8,9},{9,8},{10,11... | collective-permute-start | bytes 663560 | tf_op jit(solution)/shard_map/ppermute | solution.py:354
  22.5 7.6 %collective-permute-start.2 = (bf16[432,256]{1,0:T(8,128)(2,1)S(1)}, bf16[432,256]{1,0:T(8,128)(2,1)S(1)}, u32[]{:S(2)}, u32[]{:S(2)}) collective-permute-start(bf16[432,256]{1,0:T(8,128)(2,1)S(1)} %collective-permute-done.1.refs_10_), channel_id=1, source_target_pairs={{0,2},{1,3},{2,0},{3,1},{4,6},{5,7},{6,4},{7,5},{8,10},{9,11},{10,... | collective-permute-start | bytes 663560 | tf_op jit(solution)/shard_map/ppermute | solution.py:354
  23.9 6.1 %collective-permute-start.10 = (bf16[432,256]{1,0:T(8,128)(2,1)S(1)}, bf16[432,256]{1,0:T(8,128)(2,1)S(1)}, u32[]{:S(2)}, u32[]{:S(2)}) collective-permute-start(bf16[432,256]{1,0:T(8,128)(2,1)S(1)} %collective-permute-done.refs_6_), channel_id=1, source_target_pairs={{0,1},{1,0},{2,3},{3,2},{4,5},{5,4},{6,7},{7,6},{8,9},{9,8},{10,11... | collective-permute-start | bytes 663560 | tf_op jit(solution)/shard_map/ppermute | solution.py:354
  25.8 4.3 %collective-permute-start.13 = (bf16[432,256]{1,0:T(8,128)(2,1)S(1)}, bf16[432,256]{1,0:T(8,128)(2,1)S(1)}, u32[]{:S(2)}, u32[]{:S(2)}) collective-permute-start(bf16[432,256]{1,0:T(8,128)(2,1)S(1)} %collective-permute-done.1.refs_10_), channel_id=1, source_target_pairs={{0,1},{1,0},{2,3},{3,2},{4,5},{5,4},{6,7},{7,6},{8,9},{9,8},{10,11... | collective-permute-start | bytes 663560 | tf_op jit(solution)/shard_map/ppermute | solution.py:354
  25.8 4.3 %collective-permute-start.12 = (bf16[432,256]{1,0:T(8,128)(2,1)S(1)}, bf16[432,256]{1,0:T(8,128)(2,1)S(1)}, u32[]{:S(2)}, u32[]{:S(2)}) collective-permute-start(bf16[432,256]{1,0:T(8,128)(2,1)S(1)} %collective-permute-done.11.refs_8_), channel_id=1, source_target_pairs={{0,1},{1,0},{2,3},{3,2},{4,5},{5,4},{6,7},{7,6},{8,9},{9,8},{10,11... | collective-permute-start | bytes 663560 | tf_op jit(solution)/shard_map/ppermute | solution.py:354
  26.3 0.9 %copy-start = (bf16[1,432,256]{2,1,0:T(8,128)(2,1)S(1)}, bf16[1,432,256]{2,1,0:T(8,128)(2,1)}, u32[]{:S(2)}) copy-start(bf16[1,432,256]{2,1,0:T(8,128)(2,1)} %param.8) | copy-start | bytes 663556
  30.1 1.5 %collective-permute-start.14 = (bf16[432,256]{1,0:T(8,128)(2,1)S(1)}, bf16[432,256]{1,0:T(8,128)(2,1)S(1)}, u32[]{:S(2)}, u32[]{:S(2)}) collective-permute-start(bf16[432,256]{1,0:T(8,128)(2,1)S(1)} %collective-permute-done.2.refs_12_), channel_id=1, source_target_pairs={{0,1},{1,0},{2,3},{3,2},{4,5},{5,4},{6,7},{7,6},{8,9},{9,8},{10,11... | collective-permute-start | bytes 663560 | tf_op jit(solution)/shard_map/ppermute | solution.py:354
  33.8 8.6 %collective-permute-start.15 = (bf16[528,256]{1,0:T(8,128)(2,1)S(1)}, bf16[528,256]{1,0:T(8,128)(2,1)S(1)}, u32[]{:S(2)}, u32[]{:S(2)}) collective-permute-start(bf16[528,256]{1,0:T(8,128)(2,1)S(1)} %get-tuple-element.40.mine_ref), channel_id=1, source_target_pairs={{0,16},{16,0},{1,17},{17,1},{2,18},{18,2},{3,19},{19,3},{4,20},{20... | collective-permute-start | bytes 811016 | tf_op jit(solution)/shard_map/ppermute | solution.py:354
  45.5 2.4 %collective-permute-start.17 = (bf16[2,432,256]{2,1,0:T(8,128)(2,1)S(1)}, bf16[2,432,256]{2,1,0:T(8,128)(2,1)S(1)}, u32[]{:S(2)}, u32[]{:S(2)}) collective-permute-start(bf16[2,432,256]{2,1,0:T(8,128)(2,1)S(1)} %get-tuple-element.46), channel_id=1, source_target_pairs={{0,1},{1,0},{2,3},{3,2},{4,5},{5,4},{6,7},{7,6},{8,9},{9,8},{10,11... | collective-permute-start | bytes 1327112 | tf_op jit(solution)/shard_map/ppermute | solution.py:354
  45.6 5.5 %collective-permute-start.16 = (bf16[2,432,256]{2,1,0:T(8,128)(2,1)S(1)}, bf16[2,432,256]{2,1,0:T(8,128)(2,1)S(1)}, u32[]{:S(2)}, u32[]{:S(2)}) collective-permute-start(bf16[2,432,256]{2,1,0:T(8,128)(2,1)S(1)} %get-tuple-element.44), channel_id=1, source_target_pairs={{0,1},{1,0},{2,3},{3,2},{4,5},{5,4},{6,7},{7,6},{8,9},{9,8},{10,11... | collective-permute-start | bytes 1327112 | tf_op jit(solution)/shard_map/ppermute | solution.py:354
  47.3 3.9 %collective-permute-start.21 = (bf16[2,432,256]{2,1,0:T(8,128)(2,1)S(1)}, bf16[2,432,256]{2,1,0:T(8,128)(2,1)S(1)}, u32[]{:S(2)}, u32[]{:S(2)}) collective-permute-start(bf16[2,432,256]{2,1,0:T(8,128)(2,1)S(1)} %get-tuple-element.56), channel_id=1, source_target_pairs={{0,1},{1,0},{2,3},{3,2},{4,5},{5,4},{6,7},{7,6},{8,9},{9,8},{10,11... | collective-permute-start | bytes 1327112 | tf_op jit(solution)/shard_map/ppermute | solution.py:354
  47.5 2.3 %collective-permute-start.22 = (bf16[2,432,256]{2,1,0:T(8,128)(2,1)S(1)}, bf16[2,432,256]{2,1,0:T(8,128)(2,1)S(1)}, u32[]{:S(2)}, u32[]{:S(2)}) collective-permute-start(bf16[2,432,256]{2,1,0:T(8,128)(2,1)S(1)} %get-tuple-element.58), channel_id=1, source_target_pairs={{0,1},{1,0},{2,3},{3,2},{4,5},{5,4},{6,7},{7,6},{8,9},{9,8},{10,11... | collective-permute-start | bytes 1327112 | tf_op jit(solution)/shard_map/ppermute | solution.py:354
  48.0 7.5 %collective-permute-start.18 = (bf16[432,256]{1,0:T(8,128)(2,1)S(1)}, bf16[432,256]{1,0:T(8,128)(2,1)S(1)}, u32[]{:S(2)}, u32[]{:S(2)}) collective-permute-start(bf16[432,256]{1,0:T(8,128)(2,1)S(1)} %fusion.12), channel_id=1, source_target_pairs={{0,2},{1,3},{2,0},{3,1},{4,6},{5,7},{6,4},{7,5},{8,10},{9,11},{10,... | collective-permute-start | bytes 663560 | tf_op jit(solution)/shard_map/ppermute | solution.py:354
  50.0 17.8 %copy-start.4 = (s32[1,4]{1,0:T(1,128)S(1)}, s32[1,4]{1,0:T(1,128)}, u32[]{:S(2)}) copy-start(s32[1,4]{1,0:T(1,128)} %param.6) | copy-start | bytes 52
  50.0 8.2 %collective-permute-start.23 = (bf16[432,256]{1,0:T(8,128)(2,1)S(1)}, bf16[432,256]{1,0:T(8,128)(2,1)S(1)}, u32[]{:S(2)}, u32[]{:S(2)}) collective-permute-start(bf16[432,256]{1,0:T(8,128)(2,1)S(1)} %get-tuple-element.61), channel_id=1, source_target_pairs={{0,4},{1,5},{2,6},{3,7},{4,0},{5,1},{6,2},{7,3},{8,12},{9,13},{10,... | collective-permute-start | bytes 663560 | tf_op jit(solution)/shard_map/ppermute | solution.py:354
  55.6 7.4 %collective-permute-start.20 = (bf16[432,256]{1,0:T(8,128)(2,1)S(1)}, bf16[432,256]{1,0:T(8,128)(2,1)S(1)}, u32[]{:S(2)}, u32[]{:S(2)}) collective-permute-start(bf16[432,256]{1,0:T(8,128)(2,1)S(1)} %fusion.8), channel_id=1, source_target_pairs={{0,4},{1,5},{2,6},{3,7},{4,0},{5,1},{6,2},{7,3},{8,12},{9,13},{10,... | collective-permute-start | bytes 663560 | tf_op jit(solution)/shard_map/ppermute | solution.py:354
  56.7 6.3 %collective-permute-start.19 = (bf16[432,256]{1,0:T(8,128)(2,1)S(1)}, bf16[432,256]{1,0:T(8,128)(2,1)S(1)}, u32[]{:S(2)}, u32[]{:S(2)}) collective-permute-start(bf16[432,256]{1,0:T(8,128)(2,1)S(1)} %fusion.13), channel_id=1, source_target_pairs={{0,2},{1,3},{2,0},{3,1},{4,6},{5,7},{6,4},{7,5},{8,10},{9,11},{10,... | collective-permute-start | bytes 663560 | tf_op jit(solution)/shard_map/ppermute | solution.py:354
  63.1 11.2 %collective-permute-start.26 = (bf16[432,256]{1,0:T(8,128)(2,1)S(1)}, bf16[432,256]{1,0:T(8,128)(2,1)S(1)}, u32[]{:S(2)}, u32[]{:S(2)}) collective-permute-start(bf16[432,256]{1,0:T(8,128)(2,1)S(1)} %fusion.11), channel_id=1, source_target_pairs={{0,8},{1,9},{2,10},{3,11},{4,12},{5,13},{6,14},{7,15},{8,0},{9,1},... | collective-permute-start | bytes 663560 | tf_op jit(solution)/shard_map/ppermute | solution.py:354
  65.0 9.4 %collective-permute-start.25 = (bf16[432,256]{1,0:T(8,128)(2,1)S(1)}, bf16[432,256]{1,0:T(8,128)(2,1)S(1)}, u32[]{:S(2)}, u32[]{:S(2)}) collective-permute-start(bf16[432,256]{1,0:T(8,128)(2,1)S(1)} %get-tuple-element.60), channel_id=1, source_target_pairs={{0,4},{1,5},{2,6},{3,7},{4,0},{5,1},{6,2},{7,3},{8,12},{9,13},{10,... | collective-permute-start | bytes 663560 | tf_op jit(solution)/shard_map/ppermute | solution.py:354
  66.2 8.2 %collective-permute-start.24 = (bf16[432,256]{1,0:T(8,128)(2,1)S(1)}, bf16[432,256]{1,0:T(8,128)(2,1)S(1)}, u32[]{:S(2)}, u32[]{:S(2)}) collective-permute-start(bf16[432,256]{1,0:T(8,128)(2,1)S(1)} %fusion.1), channel_id=1, source_target_pairs={{0,2},{1,3},{2,0},{3,1},{4,6},{5,7},{6,4},{7,5},{8,10},{9,11},{10,... | collective-permute-start | bytes 663560 | tf_op jit(solution)/shard_map/ppermute | solution.py:354

commit v5 on v4

--- a/solution.py
+++ b/solution.py
@@ -483,8 +483,10 @@
             both = widen(kept) + widen(swap(sent, "fsdp", 1))
             return both[0], both[1]
 
+        cut = rows // (2 * ROW_TILE) * ROW_TILE
+        parts = slice(0, cut), slice(cut, rows)
         kept_12, send_12 = core_sum(*far_sums[:2])
-        send_12 = narrow(send_12)
+        send_12 = [narrow(send_12[part]) for part in parts]
 
     near_sums = call(
         rest_kernel,
@@ -499,23 +501,25 @@
         kept_8, send_8 = core_sum(*far_sums[2:])
         kept_4, send_4 = core_sum(*near_sums[:2])
         kept_0, send_0 = core_sum(*near_sums[2:])
-        send_8 = narrow(send_8)
+        send_8 = [narrow(send_8[part]) for part in parts]
         side_4 = swap(narrow(send_4), "fsdp", 4)
-        came_12 = swap(send_12, "fsdp", 2)
-        for_8 = narrow(kept_12 + widen(came_12))
-        from_4 = swap(for_8, "fsdp", 4)
-        for_8, send_8 = together(for_8, send_8)
-        came_8 = swap(send_8, "fsdp", 2)
-        ready = narrow(kept_8 + widen(came_8) + widen(from_4))
-        from_8 = swap(ready, "fsdp", 8)
-        send_0 = narrow(send_0 + widen(side_4))
-        came_8, send_0 = together(came_8, send_0)
-        came_0 = swap(send_0, "fsdp", 2)
+        came_12 = [swap(value, "fsdp", 2) for value in send_12]
+        came_8 = []
+        for at in (0, 1):
+            came_12[at], send_8[at] = together(came_12[at], send_8[at])
+            came_8.append(swap(send_8[at], "fsdp", 2))
+        for_8 = [narrow(kept_12[part] + widen(value)) for part, value in zip(parts, came_12)]
+        from_4 = [swap(value, "fsdp", 4) for value in for_8]
+        ready = [
+            narrow(kept_8[part] + widen(one) + widen(two)) for part, one, two in zip(parts, came_8, from_4)
+        ]
+        from_8 = jnp.concatenate([swap(value, "fsdp", 8) for value in ready], axis=0)
+        came_0 = swap(narrow(send_0 + widen(side_4)), "fsdp", 2)
         direct_4 = narrow(kept_4)
-        from_4, direct_4 = together(from_4, direct_4)
+        from_4[1], direct_4 = together(from_4[1], direct_4)
         late = swap(direct_4, "fsdp", 4)
         weight_grad = (kept_0 + widen(came_0) + widen(late) + widen(from_8)) * factor
-        grad, _ = together(grad, ready)
+        grad, _ = together(grad, ready[1])
     else:
         summed = widen(jnp.concatenate([near_sums[0], far_sums[0]], axis=0))
         weight_grad = lax.psum_scatter(summed, "fsdp", scatter_dimension=0, tiled=True) * factor

time: 75.6 us -> 74 us (0.979)
  waiting for transfers between devices: 29.3 us -> 24.4 us
  starting transfers between devices: 25.4 us -> 28.7 us
    ppermute x27 -> x31, waiting for transfers between devices: 29.3 us -> 24.4 us  [swap(): lax.ppermute(value, axis, [(i, i ^ by) for i in range(lax.axis_size(axis))])]
    ppermute x27 -> x31, starting transfers between devices: 25.4 us -> 28.7 us  [swap(): lax.ppermute(value, axis, [(i, i ^ by) for i in range(lax.axis_size(axis))])]
  transfers between devices with their start and end apart: 27 -> 31, of which waited for: 13 -> 12; matrix products, arithmetic and copies ran while one was open for 3% -> 4% of each run, Pallas kernels for 11% -> 12%
where the time goes in v5:
time: 74 us; the launch traced here: 73.8 us
  starting transfers between devices  28.7 us (39%)
  waiting for transfers between devices  24.4 us (33%)
  Pallas kernels  14 us (19%)
  local copies, waits for them, and re-layouts  4.38 us (6%)
  other arithmetic  1.48 us (2%)
  between operations  0.84 us (1%)
    ppermute x31, starting transfers between devices, swap(): lax.ppermute(value, axis, [(i, i ^ by) for i in range(lax.axis_size(axis))])  28.7 us
    ppermute x31, waiting for transfers between devices, swap(): lax.ppermute(value, axis, [(i, i ^ by) for i in range(lax.axis_size(axis))])  24.4 us
    pallas_call x1, Pallas kernels, on_device(): call(last_kernel, 1.0, limit=LAST_VMEM_LIMIT, out_shape=[jax.ShapeDtypeSt...  4.53 us
    pallas_call x1, Pallas kernels, on_device(): call(gradient_kernel, 0.5, out_shape=[volume, volume, turned_out, cols_ou...  3.14 us
    unnamed x10, local copies, waits for them, and re-layouts  2.28 us
    pallas_call x1, Pallas kernels, on_device(): call(lambda dims, split, *refs: far_kernel(dims, split, count, *refs), 0....  2.25 us
    pallas_call x1, Pallas kernels, on_device(): call(lambda dims, split, *refs: near_kernel(dims, split, count, *refs), 0...  1.7 us
  transfers between devices with their start and end apart: 31, of which 12 were waited for; matrix products, arithmetic and copies ran while one was open for 4% of the time, Pallas kernels for 12%

profile of v5, /device:TPU:0, one launch (start us, length us, event | category | flops | bytes accessed | tf_op | source)
XLA Modules:
  0.0 73.8 jit_solution(4200575410573521658)
XLA Ops:
  0.6 3.1 %collective-permute-start.3 = (bf16[432,256]{1,0:T(8,128)(2,1)}, bf16[432,256]{1,0:T(8,128)(2,1)S(1)}, u32[]{:S(2)}, u32[]{:S(2)}) collective-permute-start(bf16[432,256]{1,0:T(8,128)(2,1)} %bitcast.62), channel_id=1, source_target_pairs={{0,4},{1,5},{2,6},{3,7},{4,0},{5,1},{6,2},{7,3},{8,12},{9,13},{10,... | collective-permute-start | bytes 663560 | tf_op jit(solution)/shard_map/ppermute | solution.py:354
  3.7 2.6 %collective-permute-start = (bf16[432,256]{1,0:T(8,128)(2,1)}, bf16[432,256]{1,0:T(8,128)(2,1)S(1)}, u32[]{:S(2)}, u32[]{:S(2)}) collective-permute-start(bf16[432,256]{1,0:T(8,128)(2,1)} %bitcast.63), channel_id=1, source_target_pairs={{0,8},{1,9},{2,10},{3,11},{4,12},{5,13},{6,14},{7,15},{8,0},{9,1},... | collective-permute-start | bytes 663560 | tf_op jit(solution)/shard_map/ppermute | solution.py:354
  6.3 1.5 %collective-permute-start.5 = (bf16[432,256]{1,0:T(8,128)(2,1)}, bf16[432,256]{1,0:T(8,128)(2,1)S(1)}, u32[]{:S(2)}, u32[]{:S(2)}) collective-permute-start(bf16[432,256]{1,0:T(8,128)(2,1)} %bitcast.64), channel_id=1, source_target_pairs={{0,2},{1,3},{2,0},{3,1},{4,6},{5,7},{6,4},{7,5},{8,10},{9,11},{10,... | collective-permute-start | bytes 663560 | tf_op jit(solution)/shard_map/ppermute | solution.py:354
  7.8 1.0 %reshape.26.clips_ref.refs_1_ = bf16[4,128,256]{2,1,0:T(8,128)(2,1)S(1)} reshape(bf16[4,4,8,4,256]{4,3,2,1,0:T(4,128)(2,1)} %param.5) | data formatting | bytes 524288 | tf_op jit(solution)/shard_map/reshape | solution.py:380
  8.8 1.0 %reshape.27.cotangent_ref = bf16[4,128,256]{2,1,0:T(8,128)(2,1)S(1)} reshape(bf16[4,4,8,4,256]{4,3,2,1,0:T(4,128)(2,1)} %param.9) | data formatting | bytes 524288 | tf_op jit(solution)/shard_map/reshape | solution.py:381
  9.9 0.7 copy-done.1
  10.5 0.7 copy-done.3
  11.2 1.2 %shard_map.76 = (bf16[4,192,2304]{2,1,0:T(8,128)(2,1)S(1)}, f32[8,128]{1,0:T(8,128)S(1)}) custom-call(s32[4]{0:T(128)S(1)} %bitcast.67, bf16[4,128,256]{2,1,0:T(8,128)(2,1)S(1)} %reshape.26.clips_ref.refs_1_, bf16[4,128,256]{2,1,0:T(8,128)(2,1)S(1)} %reshape.27.cotangent_ref, f32[1,256]{1,0:T(1,128)S(1)} %copy-done.1, f32[1,256]{1,0:T(1,128)S(1)} %copy-done.1), custom_call_target="tpu_custom_call" | custom-call | flops 362387872 | bytes 3538944 | tf_op jit(solution)/shard_map/pallas_call | solution.py:416
  12.4 1.6 %collective-permute-done.3.refs_6_ = bf16[432,256]{1,0:T(8,128)(2,1)S(1)} collective-permute-done((bf16[432,256]{1,0:T(8,128)(2,1)}, bf16[432,256]{1,0:T(8,128)(2,1)S(1)}, u32[]{:S(2)}, u32[]{:S(2)}) %collective-permute-start.3) | collective-permute-done | bytes 221216 | tf_op jit(solution)/shard_map/ppermute | solution.py:354
  14.0 1.7 %collective-permute-start.8 = (bf16[432,256]{1,0:T(8,128)(2,1)S(1)}, bf16[432,256]{1,0:T(8,128)(2,1)S(1)}, u32[]{:S(2)}, u32[]{:S(2)}) collective-permute-start(bf16[432,256]{1,0:T(8,128)(2,1)S(1)} %collective-permute-done.3.refs_6_), channel_id=1, source_target_pairs={{0,2},{1,3},{2,0},{3,1},{4,6},{5,7},{6,4},{7,5},{8,10},{9,11},{10,... | collective-permute-start | bytes 663560 | tf_op jit(solution)/shard_map/ppermute | solution.py:354
  15.6 0.9 %collective-permute-done.refs_6_ = bf16[432,256]{1,0:T(8,128)(2,1)S(1)} collective-permute-done((bf16[432,256]{1,0:T(8,128)(2,1)}, bf16[432,256]{1,0:T(8,128)(2,1)S(1)}, u32[]{:S(2)}, u32[]{:S(2)}) %collective-permute-start) | collective-permute-done | bytes 221216 | tf_op jit(solution)/shard_map/ppermute | solution.py:354
  16.5 0.4 collective-permute-start.1
  17.0 1.5 %collective-permute-start.11 = (bf16[432,256]{1,0:T(8,128)(2,1)S(1)}, bf16[432,256]{1,0:T(8,128)(2,1)S(1)}, u32[]{:S(2)}, u32[]{:S(2)}) collective-permute-start(bf16[432,256]{1,0:T(8,128)(2,1)S(1)} %collective-permute-done.refs_6_), channel_id=1, source_target_pairs={{0,2},{1,3},{2,0},{3,1},{4,6},{5,7},{6,4},{7,5},{8,10},{9,11},{10,... | collective-permute-start | bytes 663560 | tf_op jit(solution)/shard_map/ppermute | solution.py:354
  18.5 0.2 collective-permute-start.7
  18.7 2.4 %collective-permute-done.8.refs_8_ = bf16[432,256]{1,0:T(8,128)(2,1)S(1)} collective-permute-done((bf16[432,256]{1,0:T(8,128)(2,1)S(1)}, bf16[432,256]{1,0:T(8,128)(2,1)S(1)}, u32[]{:S(2)}, u32[]{:S(2)}) %collective-permute-start.8) | collective-permute-done | bytes 221216 | tf_op jit(solution)/shard_map/ppermute | solution.py:354
  21.0 1.4 %collective-permute-done.1.refs_10_ = bf16[432,256]{1,0:T(8,128)(2,1)S(1)} collective-permute-done((bf16[432,256]{1,0:T(8,128)(2,1)S(1)}, bf16[432,256]{1,0:T(8,128)(2,1)S(1)}, u32[]{:S(2)}, u32[]{:S(2)}) %collective-permute-start.1) | collective-permute-done | bytes 221216 | tf_op jit(solution)/shard_map/ppermute | solution.py:354
  22.5 1.5 %collective-permute-start.2 = (bf16[432,256]{1,0:T(8,128)(2,1)S(1)}, bf16[432,256]{1,0:T(8,128)(2,1)S(1)}, u32[]{:S(2)}, u32[]{:S(2)}) collective-permute-start(bf16[432,256]{1,0:T(8,128)(2,1)S(1)} %collective-permute-done.1.refs_10_), channel_id=1, source_target_pairs={{0,2},{1,3},{2,0},{3,1},{4,6},{5,7},{6,4},{7,5},{8,10},{9,11},{10,... | collective-permute-start | bytes 663560 | tf_op jit(solution)/shard_map/ppermute | solution.py:354
  24.0 1.8 %collective-permute-done.11.refs_8_ = bf16[432,256]{1,0:T(8,128)(2,1)S(1)} collective-permute-done((bf16[432,256]{1,0:T(8,128)(2,1)S(1)}, bf16[432,256]{1,0:T(8,128)(2,1)S(1)}, u32[]{:S(2)}, u32[]{:S(2)}) %collective-permute-start.11) | collective-permute-done | bytes 221216 | tf_op jit(solution)/shard_map/ppermute | solution.py:354
  25.8 0.5 collective-permute-start.12
  26.3 0.9 %copy-done = bf16[1,432,256]{2,1,0:T(8,128)(2,1)S(1)} copy-done((bf16[1,432,256]{2,1,0:T(8,128)(2,1)S(1)}, bf16[1,432,256]{2,1,0:T(8,128)(2,1)}, u32[]{:S(2)}) %copy-start) | copy-done | bytes 221208
  27.2 1.7 %shard_map.77 = (f32[512,256]{1,0:T(8,128)S(1)}, f32[8,128]{1,0:T(8,128)S(1)}, bf16[3456,256]{1,0:T(8,128)(2,1)S(1)}) custom-call(bf16[4,192,2304]{2,1,0:T(8,128)(2,1)S(1)} %get-tuple-element.34.refs_0_.refs_4_.early_cols_ref, f32[8,128]{1,0:T(8,128)S(1)} %get-tuple-element.36.refs_1_, bf16[432,256]{1,0:T(8,128)(2,1)S(1)} %bitcast.66, ...), custom_call_target="tpu_custom_call" | custom-call | flops 905969664 | bytes 3538944 | tf_op jit(solution)/shard_map/pallas_call | solution.py:438
  28.9 1.1 %collective-permute-done.2.refs_12_ = bf16[432,256]{1,0:T(8,128)(2,1)S(1)} collective-permute-done((bf16[432,256]{1,0:T(8,128)(2,1)S(1)}, bf16[432,256]{1,0:T(8,128)(2,1)S(1)}, u32[]{:S(2)}, u32[]{:S(2)}) %collective-permute-start.2) | collective-permute-done | bytes 221216 | tf_op jit(solution)/shard_map/ppermute | solution.py:354
  30.1 1.5 %collective-permute-done.14.refs_13_ = bf16[432,256]{1,0:T(8,128)(2,1)S(1)} collective-permute-done((bf16[432,256]{1,0:T(8,128)(2,1)S(1)}, bf16[432,256]{1,0:T(8,128)(2,1)S(1)}, u32[]{:S(2)}, u32[]{:S(2)}) %collective-permute-start.14) | collective-permute-done | bytes 221216 | tf_op jit(solution)/shard_map/ppermute | solution.py:354
  31.5 2.2 %shard_map.78 = (bf16[528,256]{1,0:T(8,128)(2,1)S(1)}, bf16[3456,256]{1,0:T(8,128)(2,1)S(1)}) custom-call(s32[4]{0:T(128)S(1)} %bitcast.68, bf16[4,128,256]{2,1,0:T(8,128)(2,1)S(1)} %reshape.26.clips_ref.refs_1_, f32[1,256]{1,0:T(1,128)S(1)} %copy-done.2, f32[8,128]{1,0:T(8,128)S(1)} %get-tuple-element.39.refs_3_, ...), custom_call_target="tpu_custom_call" | custom-call | flops 905969664 | bytes 3538944 | tf_op jit(solution)/shard_map/pallas_call | solution.py:453
  33.8 1.4 %collective-permute-start.15 = (bf16[528,256]{1,0:T(8,128)(2,1)S(1)}, bf16[528,256]{1,0:T(8,128)(2,1)S(1)}, u32[]{:S(2)}, u32[]{:S(2)}) collective-permute-start(bf16[528,256]{1,0:T(8,128)(2,1)S(1)} %get-tuple-element.42.mine_ref), channel_id=1, source_target_pairs={{0,16},{16,0},{1,17},{17,1},{2,18},{18,2},{3,19},{19,3},{4,20},{20... | collective-permute-start | bytes 811016 | tf_op jit(solution)/shard_map/ppermute | solution.py:354
  35.2 7.2 %collective-permute-done.15.theirs_ref = bf16[528,256]{1,0:T(8,128)(2,1)S(1)} collective-permute-done((bf16[528,256]{1,0:T(8,128)(2,1)S(1)}, bf16[528,256]{1,0:T(8,128)(2,1)S(1)}, u32[]{:S(2)}, u32[]{:S(2)}) %collective-permute-start.15) | collective-permute-done | bytes 270368 | tf_op jit(solution)/shard_map/ppermute | solution.py:354
  42.4 3.1 %shard_map.79 = (bf16[512,256]{1,0:T(8,128)(2,1)S(1)}, bf16[512,256]{1,0:T(8,128)(2,1)S(1)}, bf16[256,512]{1,0:T(8,128)(2,1)S(1)}, bf16[4,192,2304]{2,1,0:T(8,12...) custom-call(s32[4]{0:T(128)S(1)} %bitcast.69, ...), custom_call_target="tpu_custom_call" | custom-call | flops 905969664 | bytes 3538944 | tf_op jit(solution)/shard_map/pallas_call | solution.py:465
  45.6 0.5 collective-permute-start.16
  46.1 1.2 %shard_map.81 = (bf16[2,432,256]{2,1,0:T(8,128)(2,1)S(1)}, bf16[2,432,256]{2,1,0:T(8,128)(2,1)S(1)}, bf16[2,432,256]{2,1,0:T(8,128)(2,1)S(1)}, bf16[2,432,256]{2,1,0:T(8,128)(2,1)S(1)}) custom-call(bf16[256,512]{1,0:T(8,128)(2,1)S(1)} %get-tuple-element.56.turned_ref, bf16[4,192,2304]{2,1,0:T(8,128)(2,1)S(1)} %get-tuple-element.57.cols_ref), custom_call_target="tpu_custom_call" | custom-call | flops 905969664 | bytes 3538944 | tf_op jit(solution)/shard_map/pallas_call | solution.py:491
  47.3 0.1 collective-permute-start.21
  47.5 0.4 collective-permute-start.22
  48.0 1.4 %collective-permute-start.26 = (bf16[208,256]{1,0:T(8,128)(2,1)S(1)}, bf16[208,256]{1,0:T(8,128)(2,1)S(1)}, u32[]{:S(2)}, u32[]{:S(2)}) collective-permute-start(bf16[208,256]{1,0:T(8,128)(2,1)S(1)} %slice_bitcast_fusion.11), channel_id=1, source_target_pairs={{0,2},{1,3},{2,0},{3,1},{4,6},{5,7},{6,4},{7,5},{8,10},{9,11},{10,... | collective-permute-start | bytes 319496 | tf_op jit(solution)/shard_map/ppermute | solution.py:354
  49.5 0.8 %collective-permute-start.18 = (bf16[224,256]{1,0:T(8,128)(2,1)S(1)}, bf16[224,256]{1,0:T(8,128)(2,1)S(1)}, u32[]{:S(2)}, u32[]{:S(2)}) collective-permute-start(bf16[224,256]{1,0:T(8,128)(2,1)S(1)} %slice_bitcast_fusion.9), channel_id=1, source_target_pairs={{0,2},{1,3},{2,0},{3,1},{4,6},{5,7},{6,4},{7,5},{8,10},{9,11},{10,... | collective-permute-start | bytes 344072 | tf_op jit(solution)/shard_map/ppermute | solution.py:354
  50.4 1.1 %collective-permute-start.23 = (bf16[432,256]{1,0:T(8,128)(2,1)S(1)}, bf16[432,256]{1,0:T(8,128)(2,1)S(1)}, u32[]{:S(2)}, u32[]{:S(2)}) collective-permute-start(bf16[432,256]{1,0:T(8,128)(2,1)S(1)} %get-tuple-element.69), channel_id=1, source_target_pairs={{0,4},{1,5},{2,6},{3,7},{4,0},{5,1},{6,2},{7,3},{8,12},{9,13},{10,... | collective-permute-start | bytes 663560 | tf_op jit(solution)/shard_map/ppermute | solution.py:354
  51.8 2.2 %collective-permute-done.26 = bf16[208,256]{1,0:T(8,128)(2,1)S(1)} collective-permute-done((bf16[208,256]{1,0:T(8,128)(2,1)S(1)}, bf16[208,256]{1,0:T(8,128)(2,1)S(1)}, u32[]{:S(2)}, u32[]{:S(2)}) %collective-permute-start.26) | collective-permute-done | bytes 106528 | tf_op jit(solution)/shard_map/ppermute | solution.py:354
  54.0 1.1 %collective-permute-start.28 = (bf16[208,256]{1,0:T(8,128)(2,1)S(1)}, bf16[208,256]{1,0:T(8,128)(2,1)S(1)}, u32[]{:S(2)}, u32[]{:S(2)}) collective-permute-start(bf16[208,256]{1,0:T(8,128)(2,1)S(1)} %fusion.13), channel_id=1, source_target_pairs={{0,4},{1,5},{2,6},{3,7},{4,0},{5,1},{6,2},{7,3},{8,12},{9,13},{10,... | collective-permute-start | bytes 319496 | tf_op jit(solution)/shard_map/ppermute | solution.py:354
  55.1 1.5 %collective-permute-start.27 = (bf16[208,256]{1,0:T(8,128)(2,1)S(1)}, bf16[208,256]{1,0:T(8,128)(2,1)S(1)}, u32[]{:S(2)}, u32[]{:S(2)}) collective-permute-start(bf16[208,256]{1,0:T(8,128)(2,1)S(1)} %slice_bitcast_fusion.10), channel_id=1, source_target_pairs={{0,2},{1,3},{2,0},{3,1},{4,6},{5,7},{6,4},{7,5},{8,10},{9,11},{10,... | collective-permute-start | bytes 319496 | tf_op jit(solution)/shard_map/ppermute | solution.py:354
  56.6 0.6 collective-permute-start.19
  57.2 1.0 %collective-permute-start.20 = (bf16[224,256]{1,0:T(8,128)(2,1)S(1)}, bf16[224,256]{1,0:T(8,128)(2,1)S(1)}, u32[]{:S(2)}, u32[]{:S(2)}) collective-permute-start(bf16[224,256]{1,0:T(8,128)(2,1)S(1)} %fusion.8), channel_id=1, source_target_pairs={{0,4},{1,5},{2,6},{3,7},{4,0},{5,1},{6,2},{7,3},{8,12},{9,13},{10,... | collective-permute-start | bytes 344072 | tf_op jit(solution)/shard_map/ppermute | solution.py:354
  58.2 2.9 %collective-permute-done.28 = bf16[208,256]{1,0:T(8,128)(2,1)S(1)} collective-permute-done((bf16[208,256]{1,0:T(8,128)(2,1)S(1)}, bf16[208,256]{1,0:T(8,128)(2,1)S(1)}, u32[]{:S(2)}, u32[]{:S(2)}) %collective-permute-start.28) | collective-permute-done | bytes 106528 | tf_op jit(solution)/shard_map/ppermute | solution.py:354
  61.1 2.0 %collective-permute-start.29 = (bf16[208,256]{1,0:T(8,128)(2,1)S(1)}, bf16[208,256]{1,0:T(8,128)(2,1)S(1)}, u32[]{:S(2)}, u32[]{:S(2)}) collective-permute-start(bf16[208,256]{1,0:T(8,128)(2,1)S(1)} %fusion.16), channel_id=1, source_target_pairs={{0,8},{1,9},{2,10},{3,11},{4,12},{5,13},{6,14},{7,15},{8,0},{9,1},... | collective-permute-start | bytes 319496 | tf_op jit(solution)/shard_map/ppermute | solution.py:354
  63.1 1.8 %collective-permute-start.24 = (bf16[432,256]{1,0:T(8,128)(2,1)S(1)}, bf16[432,256]{1,0:T(8,128)(2,1)S(1)}, u32[]{:S(2)}, u32[]{:S(2)}) collective-permute-start(bf16[432,256]{1,0:T(8,128)(2,1)S(1)} %fusion.1), channel_id=1, source_target_pairs={{0,2},{1,3},{2,0},{3,1},{4,6},{5,7},{6,4},{7,5},{8,10},{9,11},{10,... | collective-permute-start | bytes 663560 | tf_op jit(solution)/shard_map/ppermute | solution.py:354
  64.9 0.8 %collective-permute-start.25 = (bf16[432,256]{1,0:T(8,128)(2,1)S(1)}, bf16[432,256]{1,0:T(8,128)(2,1)S(1)}, u32[]{:S(2)}, u32[]{:S(2)}) collective-permute-start(bf16[432,256]{1,0:T(8,128)(2,1)S(1)} %get-tuple-element.62), channel_id=1, source_target_pairs={{0,4},{1,5},{2,6},{3,7},{4,0},{5,1},{6,2},{7,3},{8,12},{9,13},{10,... | collective-permute-start | bytes 663560 | tf_op jit(solution)/shard_map/ppermute | solution.py:354
  65.7 1.1 %collective-permute-start.30 = (bf16[224,256]{1,0:T(8,128)(2,1)S(1)}, bf16[224,256]{1,0:T(8,128)(2,1)S(1)}, u32[]{:S(2)}, u32[]{:S(2)}) collective-permute-start(bf16[224,256]{1,0:T(8,128)(2,1)S(1)} %fusion.11), channel_id=1, source_target_pairs={{0,8},{1,9},{2,10},{3,11},{4,12},{5,13},{6,14},{7,15},{8,0},{9,1},... | collective-permute-start | bytes 344072 | tf_op jit(solution)/shard_map/ppermute | solution.py:354
  66.9 4.5 %shard_map.80 = (bf16[1,4,4,8,4,256]{5,4,3,2,1,0:T(4,128)(2,1)}, bf16[1,4,4,8,4,256]{5,4,3,2,1,0:T(4,128)(2,1)}) custom-call(s32[4]{0:T(128)S(1)} %bitcast.70, bf16[4,128,256]{2,1,0:T(8,128)(2,1)S(1)} %reshape.26.clips_ref.refs_1_, f32[1,256]{1,0:T(1,128)S(1)} %copy-done.2, bf16[512,256]{1,0:T(8,128)(2,1)S(1)} %get-tuple-element.43.hidden_ref, ...), custom_call_target="tpu_custom_call" | custom-call | flops 1811939328 | bytes 3538944 | tf_op jit(solution)/shard_map/pallas_call | solution.py:527
  71.4 0.9 %collective-permute-done.30 = bf16[224,256]{1,0:T(8,128)(2,1)S(1)} collective-permute-done((bf16[224,256]{1,0:T(8,128)(2,1)S(1)}, bf16[224,256]{1,0:T(8,128)(2,1)S(1)}, u32[]{:S(2)}, u32[]{:S(2)}) %collective-permute-start.30) | collective-permute-done | bytes 114720 | tf_op jit(solution)/shard_map/ppermute | solution.py:354
  72.4 0.5 collective-permute-done.25
  72.9 0.9 %fusion.6 = f32[1,432,256]{2,1,0:T(8,128)} fusion(f32[2,432,256]{2,1,0:T(8,128)S(1)} %convert_add_fusion, bf16[432,256]{1,0:T(8,128)(2,1)S(1)} %collective-permute-done.25, bf16[432,256]{1,0:T(8,128)(2,1)S(1)} %collective-permute-done.24, bf16[224,256]{1,0:T(8,128)(2,1)S(1)} %collective-permute-done.30, bf16[208,256]{1,0:T(8,128)(2,1)S(1)} %collective-permute-done.29), kind=kLoop, calls=%fused_computation.12 | loop fusion | flops 1105920 | bytes 1548288 | tf_op jit(solution)/shard_map/broadcast_in_dim | solution.py:546
  (47 shorter events, 0.8 us)
Async XLA Ops:
  0.6 13.3 %collective-permute-start.3 = (bf16[432,256]{1,0:T(8,128)(2,1)}, bf16[432,256]{1,0:T(8,128)(2,1)S(1)}, u32[]{:S(2)}, u32[]{:S(2)}) collective-permute-start(bf16[432,256]{1,0:T(8,128)(2,1)} %bitcast.62), channel_id=1, source_target_pairs={{0,4},{1,5},{2,6},{3,7},{4,0},{5,1},{6,2},{7,3},{8,12},{9,13},{10,... | collective-permute-start | bytes 663560 | tf_op jit(solution)/shard_map/ppermute | solution.py:354
  3.7 12.8 %collective-permute-start = (bf16[432,256]{1,0:T(8,128)(2,1)}, bf16[432,256]{1,0:T(8,128)(2,1)S(1)}, u32[]{:S(2)}, u32[]{:S(2)}) collective-permute-start(bf16[432,256]{1,0:T(8,128)(2,1)} %bitcast.63), channel_id=1, source_target_pairs={{0,8},{1,9},{2,10},{3,11},{4,12},{5,13},{6,14},{7,15},{8,0},{9,1},... | collective-permute-start | bytes 663560 | tf_op jit(solution)/shard_map/ppermute | solution.py:354
  6.3 10.6 %collective-permute-start.5 = (bf16[432,256]{1,0:T(8,128)(2,1)}, bf16[432,256]{1,0:T(8,128)(2,1)S(1)}, u32[]{:S(2)}, u32[]{:S(2)}) collective-permute-start(bf16[432,256]{1,0:T(8,128)(2,1)} %bitcast.64), channel_id=1, source_target_pairs={{0,2},{1,3},{2,0},{3,1},{4,6},{5,7},{6,4},{7,5},{8,10},{9,11},{10,... | collective-permute-start | bytes 663560 | tf_op jit(solution)/shard_map/ppermute | solution.py:354
  7.8 10.7 %collective-permute-start.4 = (bf16[432,256]{1,0:T(8,128)(2,1)}, bf16[432,256]{1,0:T(8,128)(2,1)S(1)}, u32[]{:S(2)}, u32[]{:S(2)}) collective-permute-start(bf16[432,256]{1,0:T(8,128)(2,1)} %bitcast.65), channel_id=1, source_target_pairs={{0,1},{1,0},{2,3},{3,2},{4,5},{5,4},{6,7},{7,6},{8,9},{9,8},{10,11... | collective-permute-start | bytes 663560 | tf_op jit(solution)/shard_map/ppermute | solution.py:354
  8.8 22.7 %copy-start.2 = (f32[1,256]{1,0:T(1,128)S(1)}, f32[1,256]{1,0:T(1,128)}, u32[]{:S(2)}) copy-start(f32[1,256]{1,0:T(1,128)} %gain_ref.5) | copy-start | bytes 3076
  9.9 0.7 copy-start.1
  10.5 0.7 copy-start.3
  14.0 7.1 %collective-permute-start.8 = (bf16[432,256]{1,0:T(8,128)(2,1)S(1)}, bf16[432,256]{1,0:T(8,128)(2,1)S(1)}, u32[]{:S(2)}, u32[]{:S(2)}) collective-permute-start(bf16[432,256]{1,0:T(8,128)(2,1)S(1)} %collective-permute-done.3.refs_6_), channel_id=1, source_target_pairs={{0,2},{1,3},{2,0},{3,1},{4,6},{5,7},{6,4},{7,5},{8,10},{9,11},{10,... | collective-permute-start | bytes 663560 | tf_op jit(solution)/shard_map/ppermute | solution.py:354
  16.5 5.9 %collective-permute-start.1 = (bf16[432,256]{1,0:T(8,128)(2,1)S(1)}, bf16[432,256]{1,0:T(8,128)(2,1)S(1)}, u32[]{:S(2)}, u32[]{:S(2)}) collective-permute-start(bf16[432,256]{1,0:T(8,128)(2,1)S(1)} %collective-permute-done.refs_6_), channel_id=1, source_target_pairs={{0,4},{1,5},{2,6},{3,7},{4,0},{5,1},{6,2},{7,3},{8,12},{9,13},{10,... | collective-permute-start | bytes 663560 | tf_op jit(solution)/shard_map/ppermute | solution.py:354
  17.0 7.0 %collective-permute-start.6 = (bf16[432,256]{1,0:T(8,128)(2,1)S(1)}, bf16[432,256]{1,0:T(8,128)(2,1)S(1)}, u32[]{:S(2)}, u32[]{:S(2)}) collective-permute-start(bf16[432,256]{1,0:T(8,128)(2,1)S(1)} %collective-permute-done.5.refs_4_), channel_id=1, source_target_pairs={{0,1},{1,0},{2,3},{3,2},{4,5},{5,4},{6,7},{7,6},{8,9},{9,8},{10,11... | collective-permute-start | bytes 663560 | tf_op jit(solution)/shard_map/ppermute | solution.py:354
  17.0 8.8 %collective-permute-start.11 = (bf16[432,256]{1,0:T(8,128)(2,1)S(1)}, bf16[432,256]{1,0:T(8,128)(2,1)S(1)}, u32[]{:S(2)}, u32[]{:S(2)}) collective-permute-start(bf16[432,256]{1,0:T(8,128)(2,1)S(1)} %collective-permute-done.refs_6_), channel_id=1, source_target_pairs={{0,2},{1,3},{2,0},{3,1},{4,6},{5,7},{6,4},{7,5},{8,10},{9,11},{10,... | collective-permute-start | bytes 663560 | tf_op jit(solution)/shard_map/ppermute | solution.py:354
  18.5 7.3 %collective-permute-start.7 = (bf16[432,256]{1,0:T(8,128)(2,1)S(1)}, bf16[432,256]{1,0:T(8,128)(2,1)S(1)}, u32[]{:S(2)}, u32[]{:S(2)}) collective-permute-start(bf16[432,256]{1,0:T(8,128)(2,1)S(1)} %collective-permute-done.3.refs_6_), channel_id=1, source_target_pairs={{0,1},{1,0},{2,3},{3,2},{4,5},{5,4},{6,7},{7,6},{8,9},{9,8},{10,11... | collective-permute-start | bytes 663560 | tf_op jit(solution)/shard_map/ppermute | solution.py:354
  21.0 5.3 %collective-permute-start.9 = (bf16[432,256]{1,0:T(8,128)(2,1)S(1)}, bf16[432,256]{1,0:T(8,128)(2,1)S(1)}, u32[]{:S(2)}, u32[]{:S(2)}) collective-permute-start(bf16[432,256]{1,0:T(8,128)(2,1)S(1)} %collective-permute-done.8.refs_8_), channel_id=1, source_target_pairs={{0,1},{1,0},{2,3},{3,2},{4,5},{5,4},{6,7},{7,6},{8,9},{9,8},{10,11... | collective-permute-start | bytes 663560 | tf_op jit(solution)/shard_map/ppermute | solution.py:354
  22.5 7.6 %collective-permute-start.2 = (bf16[432,256]{1,0:T(8,128)(2,1)S(1)}, bf16[432,256]{1,0:T(8,128)(2,1)S(1)}, u32[]{:S(2)}, u32[]{:S(2)}) collective-permute-start(bf16[432,256]{1,0:T(8,128)(2,1)S(1)} %collective-permute-done.1.refs_10_), channel_id=1, source_target_pairs={{0,2},{1,3},{2,0},{3,1},{4,6},{5,7},{6,4},{7,5},{8,10},{9,11},{10,... | collective-permute-start | bytes 663560 | tf_op jit(solution)/shard_map/ppermute | solution.py:354
  23.9 6.1 %collective-permute-start.10 = (bf16[432,256]{1,0:T(8,128)(2,1)S(1)}, bf16[432,256]{1,0:T(8,128)(2,1)S(1)}, u32[]{:S(2)}, u32[]{:S(2)}) collective-permute-start(bf16[432,256]{1,0:T(8,128)(2,1)S(1)} %collective-permute-done.refs_6_), channel_id=1, source_target_pairs={{0,1},{1,0},{2,3},{3,2},{4,5},{5,4},{6,7},{7,6},{8,9},{9,8},{10,11... | collective-permute-start | bytes 663560 | tf_op jit(solution)/shard_map/ppermute | solution.py:354
  25.8 4.3 %collective-permute-start.13 = (bf16[432,256]{1,0:T(8,128)(2,1)S(1)}, bf16[432,256]{1,0:T(8,128)(2,1)S(1)}, u32[]{:S(2)}, u32[]{:S(2)}) collective-permute-start(bf16[432,256]{1,0:T(8,128)(2,1)S(1)} %collective-permute-done.1.refs_10_), channel_id=1, source_target_pairs={{0,1},{1,0},{2,3},{3,2},{4,5},{5,4},{6,7},{7,6},{8,9},{9,8},{10,11... | collective-permute-start | bytes 663560 | tf_op jit(solution)/shard_map/ppermute | solution.py:354
  25.8 4.3 %collective-permute-start.12 = (bf16[432,256]{1,0:T(8,128)(2,1)S(1)}, bf16[432,256]{1,0:T(8,128)(2,1)S(1)}, u32[]{:S(2)}, u32[]{:S(2)}) collective-permute-start(bf16[432,256]{1,0:T(8,128)(2,1)S(1)} %collective-permute-done.11.refs_8_), channel_id=1, source_target_pairs={{0,1},{1,0},{2,3},{3,2},{4,5},{5,4},{6,7},{7,6},{8,9},{9,8},{10,11... | collective-permute-start | bytes 663560 | tf_op jit(solution)/shard_map/ppermute | solution.py:354
  26.3 0.9 %copy-start = (bf16[1,432,256]{2,1,0:T(8,128)(2,1)S(1)}, bf16[1,432,256]{2,1,0:T(8,128)(2,1)}, u32[]{:S(2)}) copy-start(bf16[1,432,256]{2,1,0:T(8,128)(2,1)} %param.8) | copy-start | bytes 663556
  30.1 1.5 %collective-permute-start.14 = (bf16[432,256]{1,0:T(8,128)(2,1)S(1)}, bf16[432,256]{1,0:T(8,128)(2,1)S(1)}, u32[]{:S(2)}, u32[]{:S(2)}) collective-permute-start(bf16[432,256]{1,0:T(8,128)(2,1)S(1)} %collective-permute-done.2.refs_12_), channel_id=1, source_target_pairs={{0,1},{1,0},{2,3},{3,2},{4,5},{5,4},{6,7},{7,6},{8,9},{9,8},{10,11... | collective-permute-start | bytes 663560 | tf_op jit(solution)/shard_map/ppermute | solution.py:354
  33.8 8.6 %collective-permute-start.15 = (bf16[528,256]{1,0:T(8,128)(2,1)S(1)}, bf16[528,256]{1,0:T(8,128)(2,1)S(1)}, u32[]{:S(2)}, u32[]{:S(2)}) collective-permute-start(bf16[528,256]{1,0:T(8,128)(2,1)S(1)} %get-tuple-element.42.mine_ref), channel_id=1, source_target_pairs={{0,16},{16,0},{1,17},{17,1},{2,18},{18,2},{3,19},{19,3},{4,20},{20... | collective-permute-start | bytes 811016 | tf_op jit(solution)/shard_map/ppermute | solution.py:354
  45.5 2.4 %collective-permute-start.17 = (bf16[2,432,256]{2,1,0:T(8,128)(2,1)S(1)}, bf16[2,432,256]{2,1,0:T(8,128)(2,1)S(1)}, u32[]{:S(2)}, u32[]{:S(2)}) collective-permute-start(bf16[2,432,256]{2,1,0:T(8,128)(2,1)S(1)} %get-tuple-element.48), channel_id=1, source_target_pairs={{0,1},{1,0},{2,3},{3,2},{4,5},{5,4},{6,7},{7,6},{8,9},{9,8},{10,11... | collective-permute-start | bytes 1327112 | tf_op jit(solution)/shard_map/ppermute | solution.py:354
  45.6 5.9 %collective-permute-start.16 = (bf16[2,432,256]{2,1,0:T(8,128)(2,1)S(1)}, bf16[2,432,256]{2,1,0:T(8,128)(2,1)S(1)}, u32[]{:S(2)}, u32[]{:S(2)}) collective-permute-start(bf16[2,432,256]{2,1,0:T(8,128)(2,1)S(1)} %get-tuple-element.46), channel_id=1, source_target_pairs={{0,1},{1,0},{2,3},{3,2},{4,5},{5,4},{6,7},{7,6},{8,9},{9,8},{10,11... | collective-permute-start | bytes 1327112 | tf_op jit(solution)/shard_map/ppermute | solution.py:354
  47.3 4.3 %collective-permute-start.21 = (bf16[2,432,256]{2,1,0:T(8,128)(2,1)S(1)}, bf16[2,432,256]{2,1,0:T(8,128)(2,1)S(1)}, u32[]{:S(2)}, u32[]{:S(2)}) collective-permute-start(bf16[2,432,256]{2,1,0:T(8,128)(2,1)S(1)} %get-tuple-element.59), channel_id=1, source_target_pairs={{0,1},{1,0},{2,3},{3,2},{4,5},{5,4},{6,7},{7,6},{8,9},{9,8},{10,11... | collective-permute-start | bytes 1327112 | tf_op jit(solution)/shard_map/ppermute | solution.py:354
  47.5 2.7 %collective-permute-start.22 = (bf16[2,432,256]{2,1,0:T(8,128)(2,1)S(1)}, bf16[2,432,256]{2,1,0:T(8,128)(2,1)S(1)}, u32[]{:S(2)}, u32[]{:S(2)}) collective-permute-start(bf16[2,432,256]{2,1,0:T(8,128)(2,1)S(1)} %get-tuple-element.61), channel_id=1, source_target_pairs={{0,1},{1,0},{2,3},{3,2},{4,5},{5,4},{6,7},{7,6},{8,9},{9,8},{10,11... | collective-permute-start | bytes 1327112 | tf_op jit(solution)/shard_map/ppermute | solution.py:354
  48.0 5.9 %collective-permute-start.26 = (bf16[208,256]{1,0:T(8,128)(2,1)S(1)}, bf16[208,256]{1,0:T(8,128)(2,1)S(1)}, u32[]{:S(2)}, u32[]{:S(2)}) collective-permute-start(bf16[208,256]{1,0:T(8,128)(2,1)S(1)} %slice_bitcast_fusion.11), channel_id=1, source_target_pairs={{0,2},{1,3},{2,0},{3,1},{4,6},{5,7},{6,4},{7,5},{8,10},{9,11},{10,... | collective-permute-start | bytes 319496 | tf_op jit(solution)/shard_map/ppermute | solution.py:354
  49.5 7.1 %collective-permute-start.18 = (bf16[224,256]{1,0:T(8,128)(2,1)S(1)}, bf16[224,256]{1,0:T(8,128)(2,1)S(1)}, u32[]{:S(2)}, u32[]{:S(2)}) collective-permute-start(bf16[224,256]{1,0:T(8,128)(2,1)S(1)} %slice_bitcast_fusion.9), channel_id=1, source_target_pairs={{0,2},{1,3},{2,0},{3,1},{4,6},{5,7},{6,4},{7,5},{8,10},{9,11},{10,... | collective-permute-start | bytes 344072 | tf_op jit(solution)/shard_map/ppermute | solution.py:354
  50.4 12.7 %collective-permute-start.23 = (bf16[432,256]{1,0:T(8,128)(2,1)S(1)}, bf16[432,256]{1,0:T(8,128)(2,1)S(1)}, u32[]{:S(2)}, u32[]{:S(2)}) collective-permute-start(bf16[432,256]{1,0:T(8,128)(2,1)S(1)} %get-tuple-element.69), channel_id=1, source_target_pairs={{0,4},{1,5},{2,6},{3,7},{4,0},{5,1},{6,2},{7,3},{8,12},{9,13},{10,... | collective-permute-start | bytes 663560 | tf_op jit(solution)/shard_map/ppermute | solution.py:354
  51.5 15.4 %copy-start.4 = (s32[1,4]{1,0:T(1,128)S(1)}, s32[1,4]{1,0:T(1,128)}, u32[]{:S(2)}) copy-start(s32[1,4]{1,0:T(1,128)} %param.6) | copy-start | bytes 52
  54.0 7.1 %collective-permute-start.28 = (bf16[208,256]{1,0:T(8,128)(2,1)S(1)}, bf16[208,256]{1,0:T(8,128)(2,1)S(1)}, u32[]{:S(2)}, u32[]{:S(2)}) collective-permute-start(bf16[208,256]{1,0:T(8,128)(2,1)S(1)} %fusion.13), channel_id=1, source_target_pairs={{0,4},{1,5},{2,6},{3,7},{4,0},{5,1},{6,2},{7,3},{8,12},{9,13},{10,... | collective-permute-start | bytes 319496 | tf_op jit(solution)/shard_map/ppermute | solution.py:354
  55.1 5.9 %collective-permute-start.27 = (bf16[208,256]{1,0:T(8,128)(2,1)S(1)}, bf16[208,256]{1,0:T(8,128)(2,1)S(1)}, u32[]{:S(2)}, u32[]{:S(2)}) collective-permute-start(bf16[208,256]{1,0:T(8,128)(2,1)S(1)} %slice_bitcast_fusion.10), channel_id=1, source_target_pairs={{0,2},{1,3},{2,0},{3,1},{4,6},{5,7},{6,4},{7,5},{8,10},{9,11},{10,... | collective-permute-start | bytes 319496 | tf_op jit(solution)/shard_map/ppermute | solution.py:354
  56.6 9.1 %collective-permute-start.19 = (bf16[224,256]{1,0:T(8,128)(2,1)S(1)}, bf16[224,256]{1,0:T(8,128)(2,1)S(1)}, u32[]{:S(2)}, u32[]{:S(2)}) collective-permute-start(bf16[224,256]{1,0:T(8,128)(2,1)S(1)} %slice_bitcast_fusion.8), channel_id=1, source_target_pairs={{0,2},{1,3},{2,0},{3,1},{4,6},{5,7},{6,4},{7,5},{8,10},{9,11},{10,... | collective-permute-start | bytes 344072 | tf_op jit(solution)/shard_map/ppermute | solution.py:354
  57.2 7.7 %collective-permute-start.20 = (bf16[224,256]{1,0:T(8,128)(2,1)S(1)}, bf16[224,256]{1,0:T(8,128)(2,1)S(1)}, u32[]{:S(2)}, u32[]{:S(2)}) collective-permute-start(bf16[224,256]{1,0:T(8,128)(2,1)S(1)} %fusion.8), channel_id=1, source_target_pairs={{0,4},{1,5},{2,6},{3,7},{4,0},{5,1},{6,2},{7,3},{8,12},{9,13},{10,... | collective-permute-start | bytes 344072 | tf_op jit(solution)/shard_map/ppermute | solution.py:354
  61.1 10.3 %collective-permute-start.29 = (bf16[208,256]{1,0:T(8,128)(2,1)S(1)}, bf16[208,256]{1,0:T(8,128)(2,1)S(1)}, u32[]{:S(2)}, u32[]{:S(2)}) collective-permute-start(bf16[208,256]{1,0:T(8,128)(2,1)S(1)} %fusion.16), channel_id=1, source_target_pairs={{0,8},{1,9},{2,10},{3,11},{4,12},{5,13},{6,14},{7,15},{8,0},{9,1},... | collective-permute-start | bytes 319496 | tf_op jit(solution)/shard_map/ppermute | solution.py:354
  63.1 9.2 %collective-permute-start.24 = (bf16[432,256]{1,0:T(8,128)(2,1)S(1)}, bf16[432,256]{1,0:T(8,128)(2,1)S(1)}, u32[]{:S(2)}, u32[]{:S(2)}) collective-permute-start(bf16[432,256]{1,0:T(8,128)(2,1)S(1)} %fusion.1), channel_id=1, source_target_pairs={{0,2},{1,3},{2,0},{3,1},{4,6},{5,7},{6,4},{7,5},{8,10},{9,11},{10,... | collective-permute-start | bytes 663560 | tf_op jit(solution)/shard_map/ppermute | solution.py:354
  64.9 8.0 %collective-permute-start.25 = (bf16[432,256]{1,0:T(8,128)(2,1)S(1)}, bf16[432,256]{1,0:T(8,128)(2,1)S(1)}, u32[]{:S(2)}, u32[]{:S(2)}) collective-permute-start(bf16[432,256]{1,0:T(8,128)(2,1)S(1)} %get-tuple-element.62), channel_id=1, source_target_pairs={{0,4},{1,5},{2,6},{3,7},{4,0},{5,1},{6,2},{7,3},{8,12},{9,13},{10,... | collective-permute-start | bytes 663560 | tf_op jit(solution)/shard_map/ppermute | solution.py:354
  65.7 6.6 %collective-permute-start.30 = (bf16[224,256]{1,0:T(8,128)(2,1)S(1)}, bf16[224,256]{1,0:T(8,128)(2,1)S(1)}, u32[]{:S(2)}, u32[]{:S(2)}) collective-permute-start(bf16[224,256]{1,0:T(8,128)(2,1)S(1)} %fusion.11), channel_id=1, source_target_pairs={{0,8},{1,9},{2,10},{3,11},{4,12},{5,13},{6,14},{7,15},{8,0},{9,1},... | collective-permute-start | bytes 344072 | tf_op jit(solution)/shard_map/ppermute | solution.py:354

commit v6 on v5

--- a/solution.py
+++ b/solution.py
@@ -516,7 +516,7 @@
         from_8 = jnp.concatenate([swap(value, "fsdp", 8) for value in ready], axis=0)
         came_0 = swap(narrow(send_0 + widen(side_4)), "fsdp", 2)
         direct_4 = narrow(kept_4)
-        from_4[1], direct_4 = together(from_4[1], direct_4)
+        from_4[0], direct_4 = together(from_4[0], direct_4)
         late = swap(direct_4, "fsdp", 4)
         weight_grad = (kept_0 + widen(came_0) + widen(late) + widen(from_8)) * factor
         grad, _ = together(grad, ready[1])

time: 74 us -> 73.1 us (0.988)
  waiting for transfers between devices: 24.4 us -> 23.4 us
    ppermute x31, waiting for transfers between devices: 24.4 us -> 23.4 us  [swap(): lax.ppermute(value, axis, [(i, i ^ by) for i in range(lax.axis_size(axis))])]
  transfers between devices with their start and end apart: 31 -> 31, of which waited for: 12 -> 11; matrix products, arithmetic and copies ran while one was open for 4% -> 4% of each run, Pallas kernels for 12% -> 12%
where the time goes in v6:
time: 73.1 us; the launch traced here: 72.8 us
  starting transfers between devices  28.7 us (39%)
  waiting for transfers between devices  23.4 us (32%)
  Pallas kernels  14 us (19%)
  local copies, waits for them, and re-layouts  4.38 us (6%)
  other arithmetic  1.49 us (2%)
  between operations  0.84 us (1%)
    ppermute x31, starting transfers between devices, swap(): lax.ppermute(value, axis, [(i, i ^ by) for i in range(lax.axis_size(axis))])  28.7 us
    ppermute x31, waiting for transfers between devices, swap(): lax.ppermute(value, axis, [(i, i ^ by) for i in range(lax.axis_size(axis))])  23.4 us
    pallas_call x1, Pallas kernels, on_device(): call(last_kernel, 1.0, limit=LAST_VMEM_LIMIT, out_shape=[jax.ShapeDtypeSt...  4.53 us
    pallas_call x1, Pallas kernels, on_device(): call(gradient_kernel, 0.5, out_shape=[volume, volume, turned_out, cols_ou...  3.14 us
    unnamed x10, local copies, waits for them, and re-layouts  2.28 us
    pallas_call x1, Pallas kernels, on_device(): call(lambda dims, split, *refs: far_kernel(dims, split, count, *refs), 0....  2.25 us
    pallas_call x1, Pallas kernels, on_device(): call(lambda dims, split, *refs: near_kernel(dims, split, count, *refs), 0...  1.7 us
  transfers between devices with their start and end apart: 31, of which 11 were waited for; matrix products, arithmetic and copies ran while one was open for 4% of the time, Pallas kernels for 12%

profile of v6, /device:TPU:0, one launch (start us, length us, event | category | flops | bytes accessed | tf_op | source)
XLA Modules:
  0.0 72.8 jit_solution(7676781646047318593)
XLA Ops:
  0.6 3.1 %collective-permute-start.3 = (bf16[432,256]{1,0:T(8,128)(2,1)}, bf16[432,256]{1,0:T(8,128)(2,1)S(1)}, u32[]{:S(2)}, u32[]{:S(2)}) collective-permute-start(bf16[432,256]{1,0:T(8,128)(2,1)} %bitcast.62), channel_id=1, source_target_pairs={{0,4},{1,5},{2,6},{3,7},{4,0},{5,1},{6,2},{7,3},{8,12},{9,13},{10,... | collective-permute-start | bytes 663560 | tf_op jit(solution)/shard_map/ppermute | solution.py:354
  3.7 2.6 %collective-permute-start = (bf16[432,256]{1,0:T(8,128)(2,1)}, bf16[432,256]{1,0:T(8,128)(2,1)S(1)}, u32[]{:S(2)}, u32[]{:S(2)}) collective-permute-start(bf16[432,256]{1,0:T(8,128)(2,1)} %bitcast.63), channel_id=1, source_target_pairs={{0,8},{1,9},{2,10},{3,11},{4,12},{5,13},{6,14},{7,15},{8,0},{9,1},... | collective-permute-start | bytes 663560 | tf_op jit(solution)/shard_map/ppermute | solution.py:354
  6.3 1.5 %collective-permute-start.5 = (bf16[432,256]{1,0:T(8,128)(2,1)}, bf16[432,256]{1,0:T(8,128)(2,1)S(1)}, u32[]{:S(2)}, u32[]{:S(2)}) collective-permute-start(bf16[432,256]{1,0:T(8,128)(2,1)} %bitcast.64), channel_id=1, source_target_pairs={{0,2},{1,3},{2,0},{3,1},{4,6},{5,7},{6,4},{7,5},{8,10},{9,11},{10,... | collective-permute-start | bytes 663560 | tf_op jit(solution)/shard_map/ppermute | solution.py:354
  7.8 1.0 %reshape.26.clips_ref.refs_1_ = bf16[4,128,256]{2,1,0:T(8,128)(2,1)S(1)} reshape(bf16[4,4,8,4,256]{4,3,2,1,0:T(4,128)(2,1)} %param.5) | data formatting | bytes 524288 | tf_op jit(solution)/shard_map/reshape | solution.py:380
  8.8 1.0 %reshape.27.cotangent_ref = bf16[4,128,256]{2,1,0:T(8,128)(2,1)S(1)} reshape(bf16[4,4,8,4,256]{4,3,2,1,0:T(4,128)(2,1)} %param.9) | data formatting | bytes 524288 | tf_op jit(solution)/shard_map/reshape | solution.py:381
  9.9 0.7 copy-done.1
  10.5 0.7 copy-done.3
  11.2 1.2 %shard_map.76 = (bf16[4,192,2304]{2,1,0:T(8,128)(2,1)S(1)}, f32[8,128]{1,0:T(8,128)S(1)}) custom-call(s32[4]{0:T(128)S(1)} %bitcast.67, bf16[4,128,256]{2,1,0:T(8,128)(2,1)S(1)} %reshape.26.clips_ref.refs_1_, bf16[4,128,256]{2,1,0:T(8,128)(2,1)S(1)} %reshape.27.cotangent_ref, f32[1,256]{1,0:T(1,128)S(1)} %copy-done.1, f32[1,256]{1,0:T(1,128)S(1)} %copy-done.1), custom_call_target="tpu_custom_call" | custom-call | flops 362387872 | bytes 3538944 | tf_op jit(solution)/shard_map/pallas_call | solution.py:416
  12.4 1.6 %collective-permute-done.3.refs_6_ = bf16[432,256]{1,0:T(8,128)(2,1)S(1)} collective-permute-done((bf16[432,256]{1,0:T(8,128)(2,1)}, bf16[432,256]{1,0:T(8,128)(2,1)S(1)}, u32[]{:S(2)}, u32[]{:S(2)}) %collective-permute-start.3) | collective-permute-done | bytes 221216 | tf_op jit(solution)/shard_map/ppermute | solution.py:354
  14.0 1.7 %collective-permute-start.8 = (bf16[432,256]{1,0:T(8,128)(2,1)S(1)}, bf16[432,256]{1,0:T(8,128)(2,1)S(1)}, u32[]{:S(2)}, u32[]{:S(2)}) collective-permute-start(bf16[432,256]{1,0:T(8,128)(2,1)S(1)} %collective-permute-done.3.refs_6_), channel_id=1, source_target_pairs={{0,2},{1,3},{2,0},{3,1},{4,6},{5,7},{6,4},{7,5},{8,10},{9,11},{10,... | collective-permute-start | bytes 663560 | tf_op jit(solution)/shard_map/ppermute | solution.py:354
  15.6 0.9 %collective-permute-done.refs_6_ = bf16[432,256]{1,0:T(8,128)(2,1)S(1)} collective-permute-done((bf16[432,256]{1,0:T(8,128)(2,1)}, bf16[432,256]{1,0:T(8,128)(2,1)S(1)}, u32[]{:S(2)}, u32[]{:S(2)}) %collective-permute-start) | collective-permute-done | bytes 221216 | tf_op jit(solution)/shard_map/ppermute | solution.py:354
  16.5 0.4 collective-permute-start.1
  17.0 1.5 %collective-permute-start.11 = (bf16[432,256]{1,0:T(8,128)(2,1)S(1)}, bf16[432,256]{1,0:T(8,128)(2,1)S(1)}, u32[]{:S(2)}, u32[]{:S(2)}) collective-permute-start(bf16[432,256]{1,0:T(8,128)(2,1)S(1)} %collective-permute-done.refs_6_), channel_id=1, source_target_pairs={{0,2},{1,3},{2,0},{3,1},{4,6},{5,7},{6,4},{7,5},{8,10},{9,11},{10,... | collective-permute-start | bytes 663560 | tf_op jit(solution)/shard_map/ppermute | solution.py:354
  18.5 0.2 collective-permute-start.7
  18.7 2.4 %collective-permute-done.8.refs_8_ = bf16[432,256]{1,0:T(8,128)(2,1)S(1)} collective-permute-done((bf16[432,256]{1,0:T(8,128)(2,1)S(1)}, bf16[432,256]{1,0:T(8,128)(2,1)S(1)}, u32[]{:S(2)}, u32[]{:S(2)}) %collective-permute-start.8) | collective-permute-done | bytes 221216 | tf_op jit(solution)/shard_map/ppermute | solution.py:354
  21.0 1.4 %collective-permute-done.1.refs_10_ = bf16[432,256]{1,0:T(8,128)(2,1)S(1)} collective-permute-done((bf16[432,256]{1,0:T(8,128)(2,1)S(1)}, bf16[432,256]{1,0:T(8,128)(2,1)S(1)}, u32[]{:S(2)}, u32[]{:S(2)}) %collective-permute-start.1) | collective-permute-done | bytes 221216 | tf_op jit(solution)/shard_map/ppermute | solution.py:354
  22.5 1.5 %collective-permute-start.2 = (bf16[432,256]{1,0:T(8,128)(2,1)S(1)}, bf16[432,256]{1,0:T(8,128)(2,1)S(1)}, u32[]{:S(2)}, u32[]{:S(2)}) collective-permute-start(bf16[432,256]{1,0:T(8,128)(2,1)S(1)} %collective-permute-done.1.refs_10_), channel_id=1, source_target_pairs={{0,2},{1,3},{2,0},{3,1},{4,6},{5,7},{6,4},{7,5},{8,10},{9,11},{10,... | collective-permute-start | bytes 663560 | tf_op jit(solution)/shard_map/ppermute | solution.py:354
  24.0 1.8 %collective-permute-done.11.refs_8_ = bf16[432,256]{1,0:T(8,128)(2,1)S(1)} collective-permute-done((bf16[432,256]{1,0:T(8,128)(2,1)S(1)}, bf16[432,256]{1,0:T(8,128)(2,1)S(1)}, u32[]{:S(2)}, u32[]{:S(2)}) %collective-permute-start.11) | collective-permute-done | bytes 221216 | tf_op jit(solution)/shard_map/ppermute | solution.py:354
  25.8 0.5 collective-permute-start.12
  26.3 0.9 %copy-done = bf16[1,432,256]{2,1,0:T(8,128)(2,1)S(1)} copy-done((bf16[1,432,256]{2,1,0:T(8,128)(2,1)S(1)}, bf16[1,432,256]{2,1,0:T(8,128)(2,1)}, u32[]{:S(2)}) %copy-start) | copy-done | bytes 221208
  27.2 1.7 %shard_map.77 = (f32[512,256]{1,0:T(8,128)S(1)}, f32[8,128]{1,0:T(8,128)S(1)}, bf16[3456,256]{1,0:T(8,128)(2,1)S(1)}) custom-call(bf16[4,192,2304]{2,1,0:T(8,128)(2,1)S(1)} %get-tuple-element.34.refs_0_.refs_4_.early_cols_ref, f32[8,128]{1,0:T(8,128)S(1)} %get-tuple-element.36.refs_1_, bf16[432,256]{1,0:T(8,128)(2,1)S(1)} %bitcast.66, ...), custom_call_target="tpu_custom_call" | custom-call | flops 905969664 | bytes 3538944 | tf_op jit(solution)/shard_map/pallas_call | solution.py:438
  28.9 1.1 %collective-permute-done.2.refs_12_ = bf16[432,256]{1,0:T(8,128)(2,1)S(1)} collective-permute-done((bf16[432,256]{1,0:T(8,128)(2,1)S(1)}, bf16[432,256]{1,0:T(8,128)(2,1)S(1)}, u32[]{:S(2)}, u32[]{:S(2)}) %collective-permute-start.2) | collective-permute-done | bytes 221216 | tf_op jit(solution)/shard_map/ppermute | solution.py:354
  30.1 1.5 %collective-permute-done.14.refs_13_ = bf16[432,256]{1,0:T(8,128)(2,1)S(1)} collective-permute-done((bf16[432,256]{1,0:T(8,128)(2,1)S(1)}, bf16[432,256]{1,0:T(8,128)(2,1)S(1)}, u32[]{:S(2)}, u32[]{:S(2)}) %collective-permute-start.14) | collective-permute-done | bytes 221216 | tf_op jit(solution)/shard_map/ppermute | solution.py:354
  31.5 2.2 %shard_map.78 = (bf16[528,256]{1,0:T(8,128)(2,1)S(1)}, bf16[3456,256]{1,0:T(8,128)(2,1)S(1)}) custom-call(s32[4]{0:T(128)S(1)} %bitcast.68, bf16[4,128,256]{2,1,0:T(8,128)(2,1)S(1)} %reshape.26.clips_ref.refs_1_, f32[1,256]{1,0:T(1,128)S(1)} %copy-done.2, f32[8,128]{1,0:T(8,128)S(1)} %get-tuple-element.39.refs_3_, ...), custom_call_target="tpu_custom_call" | custom-call | flops 905969664 | bytes 3538944 | tf_op jit(solution)/shard_map/pallas_call | solution.py:453
  33.8 1.4 %collective-permute-start.15 = (bf16[528,256]{1,0:T(8,128)(2,1)S(1)}, bf16[528,256]{1,0:T(8,128)(2,1)S(1)}, u32[]{:S(2)}, u32[]{:S(2)}) collective-permute-start(bf16[528,256]{1,0:T(8,128)(2,1)S(1)} %get-tuple-element.42.mine_ref), channel_id=1, source_target_pairs={{0,16},{16,0},{1,17},{17,1},{2,18},{18,2},{3,19},{19,3},{4,20},{20... | collective-permute-start | bytes 811016 | tf_op jit(solution)/shard_map/ppermute | solution.py:354
  35.2 7.2 %collective-permute-done.15.theirs_ref = bf16[528,256]{1,0:T(8,128)(2,1)S(1)} collective-permute-done((bf16[528,256]{1,0:T(8,128)(2,1)S(1)}, bf16[528,256]{1,0:T(8,128)(2,1)S(1)}, u32[]{:S(2)}, u32[]{:S(2)}) %collective-permute-start.15) | collective-permute-done | bytes 270368 | tf_op jit(solution)/shard_map/ppermute | solution.py:354
  42.4 3.1 %shard_map.79 = (bf16[512,256]{1,0:T(8,128)(2,1)S(1)}, bf16[512,256]{1,0:T(8,128)(2,1)S(1)}, bf16[256,512]{1,0:T(8,128)(2,1)S(1)}, bf16[4,192,2304]{2,1,0:T(8,12...) custom-call(s32[4]{0:T(128)S(1)} %bitcast.69, ...), custom_call_target="tpu_custom_call" | custom-call | flops 905969664 | bytes 3538944 | tf_op jit(solution)/shard_map/pallas_call | solution.py:465
  45.6 0.5 collective-permute-start.16
  46.1 1.2 %shard_map.81 = (bf16[2,432,256]{2,1,0:T(8,128)(2,1)S(1)}, bf16[2,432,256]{2,1,0:T(8,128)(2,1)S(1)}, bf16[2,432,256]{2,1,0:T(8,128)(2,1)S(1)}, bf16[2,432,256]{2,1,0:T(8,128)(2,1)S(1)}) custom-call(bf16[256,512]{1,0:T(8,128)(2,1)S(1)} %get-tuple-element.56.turned_ref, bf16[4,192,2304]{2,1,0:T(8,128)(2,1)S(1)} %get-tuple-element.57.cols_ref), custom_call_target="tpu_custom_call" | custom-call | flops 905969664 | bytes 3538944 | tf_op jit(solution)/shard_map/pallas_call | solution.py:491
  47.3 0.1 collective-permute-start.21
  47.5 0.4 collective-permute-start.22
  48.0 1.4 %collective-permute-start.25 = (bf16[208,256]{1,0:T(8,128)(2,1)S(1)}, bf16[208,256]{1,0:T(8,128)(2,1)S(1)}, u32[]{:S(2)}, u32[]{:S(2)}) collective-permute-start(bf16[208,256]{1,0:T(8,128)(2,1)S(1)} %slice_bitcast_fusion.11), channel_id=1, source_target_pairs={{0,2},{1,3},{2,0},{3,1},{4,6},{5,7},{6,4},{7,5},{8,10},{9,11},{10,... | collective-permute-start | bytes 319496 | tf_op jit(solution)/shard_map/ppermute | solution.py:354
  49.5 0.8 %collective-permute-start.18 = (bf16[224,256]{1,0:T(8,128)(2,1)S(1)}, bf16[224,256]{1,0:T(8,128)(2,1)S(1)}, u32[]{:S(2)}, u32[]{:S(2)}) collective-permute-start(bf16[224,256]{1,0:T(8,128)(2,1)S(1)} %slice_bitcast_fusion.9), channel_id=1, source_target_pairs={{0,2},{1,3},{2,0},{3,1},{4,6},{5,7},{6,4},{7,5},{8,10},{9,11},{10,... | collective-permute-start | bytes 344072 | tf_op jit(solution)/shard_map/ppermute | solution.py:354
  50.2 0.1 add_convert_fusion
  50.4 1.1 %collective-permute-start.23 = (bf16[432,256]{1,0:T(8,128)(2,1)S(1)}, bf16[432,256]{1,0:T(8,128)(2,1)S(1)}, u32[]{:S(2)}, u32[]{:S(2)}) collective-permute-start(bf16[432,256]{1,0:T(8,128)(2,1)S(1)} %get-tuple-element.69), channel_id=1, source_target_pairs={{0,4},{1,5},{2,6},{3,7},{4,0},{5,1},{6,2},{7,3},{8,12},{9,13},{10,... | collective-permute-start | bytes 663560 | tf_op jit(solution)/shard_map/ppermute | solution.py:354
  51.8 2.2 %collective-permute-done.25 = bf16[208,256]{1,0:T(8,128)(2,1)S(1)} collective-permute-done((bf16[208,256]{1,0:T(8,128)(2,1)S(1)}, bf16[208,256]{1,0:T(8,128)(2,1)S(1)}, u32[]{:S(2)}, u32[]{:S(2)}) %collective-permute-start.25) | collective-permute-done | bytes 106528 | tf_op jit(solution)/shard_map/ppermute | solution.py:354
  54.0 1.1 %collective-permute-start.26 = (bf16[208,256]{1,0:T(8,128)(2,1)S(1)}, bf16[208,256]{1,0:T(8,128)(2,1)S(1)}, u32[]{:S(2)}, u32[]{:S(2)}) collective-permute-start(bf16[208,256]{1,0:T(8,128)(2,1)S(1)} %fusion.16), channel_id=1, source_target_pairs={{0,4},{1,5},{2,6},{3,7},{4,0},{5,1},{6,2},{7,3},{8,12},{9,13},{10,... | collective-permute-start | bytes 319496 | tf_op jit(solution)/shard_map/ppermute | solution.py:354
  55.1 1.5 %collective-permute-start.28 = (bf16[208,256]{1,0:T(8,128)(2,1)S(1)}, bf16[208,256]{1,0:T(8,128)(2,1)S(1)}, u32[]{:S(2)}, u32[]{:S(2)}) collective-permute-start(bf16[208,256]{1,0:T(8,128)(2,1)S(1)} %slice_bitcast_fusion.10), channel_id=1, source_target_pairs={{0,2},{1,3},{2,0},{3,1},{4,6},{5,7},{6,4},{7,5},{8,10},{9,11},{10,... | collective-permute-start | bytes 319496 | tf_op jit(solution)/shard_map/ppermute | solution.py:354
  56.6 0.6 collective-permute-start.19
  57.2 1.0 %collective-permute-start.20 = (bf16[224,256]{1,0:T(8,128)(2,1)S(1)}, bf16[224,256]{1,0:T(8,128)(2,1)S(1)}, u32[]{:S(2)}, u32[]{:S(2)}) collective-permute-start(bf16[224,256]{1,0:T(8,128)(2,1)S(1)} %fusion.8), channel_id=1, source_target_pairs={{0,4},{1,5},{2,6},{3,7},{4,0},{5,1},{6,2},{7,3},{8,12},{9,13},{10,... | collective-permute-start | bytes 344072 | tf_op jit(solution)/shard_map/ppermute | solution.py:354
  58.2 2.9 %collective-permute-done.26 = bf16[208,256]{1,0:T(8,128)(2,1)S(1)} collective-permute-done((bf16[208,256]{1,0:T(8,128)(2,1)S(1)}, bf16[208,256]{1,0:T(8,128)(2,1)S(1)}, u32[]{:S(2)}, u32[]{:S(2)}) %collective-permute-start.26) | collective-permute-done | bytes 106528 | tf_op jit(solution)/shard_map/ppermute | solution.py:354
  61.1 2.0 %collective-permute-start.29 = (bf16[208,256]{1,0:T(8,128)(2,1)S(1)}, bf16[208,256]{1,0:T(8,128)(2,1)S(1)}, u32[]{:S(2)}, u32[]{:S(2)}) collective-permute-start(bf16[208,256]{1,0:T(8,128)(2,1)S(1)} %fusion.14), channel_id=1, source_target_pairs={{0,8},{1,9},{2,10},{3,11},{4,12},{5,13},{6,14},{7,15},{8,0},{9,1},... | collective-permute-start | bytes 319496 | tf_op jit(solution)/shard_map/ppermute | solution.py:354
  63.0 0.9 %collective-permute-start.27 = (bf16[432,256]{1,0:T(8,128)(2,1)S(1)}, bf16[432,256]{1,0:T(8,128)(2,1)S(1)}, u32[]{:S(2)}, u32[]{:S(2)}) collective-permute-start(bf16[432,256]{1,0:T(8,128)(2,1)S(1)} %get-tuple-element.63), channel_id=1, source_target_pairs={{0,4},{1,5},{2,6},{3,7},{4,0},{5,1},{6,2},{7,3},{8,12},{9,13},{10,... | collective-permute-start | bytes 663560 | tf_op jit(solution)/shard_map/ppermute | solution.py:354
  64.0 1.7 %collective-permute-start.24 = (bf16[432,256]{1,0:T(8,128)(2,1)S(1)}, bf16[432,256]{1,0:T(8,128)(2,1)S(1)}, u32[]{:S(2)}, u32[]{:S(2)}) collective-permute-start(bf16[432,256]{1,0:T(8,128)(2,1)S(1)} %fusion.1), channel_id=1, source_target_pairs={{0,2},{1,3},{2,0},{3,1},{4,6},{5,7},{6,4},{7,5},{8,10},{9,11},{10,... | collective-permute-start | bytes 663560 | tf_op jit(solution)/shard_map/ppermute | solution.py:354
  65.7 1.1 %collective-permute-start.30 = (bf16[224,256]{1,0:T(8,128)(2,1)S(1)}, bf16[224,256]{1,0:T(8,128)(2,1)S(1)}, u32[]{:S(2)}, u32[]{:S(2)}) collective-permute-start(bf16[224,256]{1,0:T(8,128)(2,1)S(1)} %fusion.11), channel_id=1, source_target_pairs={{0,8},{1,9},{2,10},{3,11},{4,12},{5,13},{6,14},{7,15},{8,0},{9,1},... | collective-permute-start | bytes 344072 | tf_op jit(solution)/shard_map/ppermute | solution.py:354
  66.9 4.5 %shard_map.80 = (bf16[1,4,4,8,4,256]{5,4,3,2,1,0:T(4,128)(2,1)}, bf16[1,4,4,8,4,256]{5,4,3,2,1,0:T(4,128)(2,1)}) custom-call(s32[4]{0:T(128)S(1)} %bitcast.70, bf16[4,128,256]{2,1,0:T(8,128)(2,1)S(1)} %reshape.26.clips_ref.refs_1_, f32[1,256]{1,0:T(1,128)S(1)} %copy-done.2, bf16[512,256]{1,0:T(8,128)(2,1)S(1)} %get-tuple-element.43.hidden_ref, ...), custom_call_target="tpu_custom_call" | custom-call | flops 1811939328 | bytes 3538944 | tf_op jit(solution)/shard_map/pallas_call | solution.py:527
  71.4 0.5 collective-permute-done.30
  71.9 0.9 %fusion.6 = f32[1,432,256]{2,1,0:T(8,128)} fusion(f32[2,432,256]{2,1,0:T(8,128)S(1)} %convert_add_fusion, bf16[432,256]{1,0:T(8,128)(2,1)S(1)} %collective-permute-done.27, bf16[432,256]{1,0:T(8,128)(2,1)S(1)} %collective-permute-done.24, bf16[224,256]{1,0:T(8,128)(2,1)S(1)} %collective-permute-done.30, bf16[208,256]{1,0:T(8,128)(2,1)S(1)} %collective-permute-done.29), kind=kLoop, calls=%fused_computation.12 | loop fusion | flops 1105920 | bytes 1548288 | tf_op jit(solution)/shard_map/broadcast_in_dim | solution.py:546
  (47 shorter events, 0.7 us)
Async XLA Ops:
  0.6 13.3 %collective-permute-start.3 = (bf16[432,256]{1,0:T(8,128)(2,1)}, bf16[432,256]{1,0:T(8,128)(2,1)S(1)}, u32[]{:S(2)}, u32[]{:S(2)}) collective-permute-start(bf16[432,256]{1,0:T(8,128)(2,1)} %bitcast.62), channel_id=1, source_target_pairs={{0,4},{1,5},{2,6},{3,7},{4,0},{5,1},{6,2},{7,3},{8,12},{9,13},{10,... | collective-permute-start | bytes 663560 | tf_op jit(solution)/shard_map/ppermute | solution.py:354
  3.7 12.8 %collective-permute-start = (bf16[432,256]{1,0:T(8,128)(2,1)}, bf16[432,256]{1,0:T(8,128)(2,1)S(1)}, u32[]{:S(2)}, u32[]{:S(2)}) collective-permute-start(bf16[432,256]{1,0:T(8,128)(2,1)} %bitcast.63), channel_id=1, source_target_pairs={{0,8},{1,9},{2,10},{3,11},{4,12},{5,13},{6,14},{7,15},{8,0},{9,1},... | collective-permute-start | bytes 663560 | tf_op jit(solution)/shard_map/ppermute | solution.py:354
  6.3 10.6 %collective-permute-start.5 = (bf16[432,256]{1,0:T(8,128)(2,1)}, bf16[432,256]{1,0:T(8,128)(2,1)S(1)}, u32[]{:S(2)}, u32[]{:S(2)}) collective-permute-start(bf16[432,256]{1,0:T(8,128)(2,1)} %bitcast.64), channel_id=1, source_target_pairs={{0,2},{1,3},{2,0},{3,1},{4,6},{5,7},{6,4},{7,5},{8,10},{9,11},{10,... | collective-permute-start | bytes 663560 | tf_op jit(solution)/shard_map/ppermute | solution.py:354
  7.8 10.7 %collective-permute-start.4 = (bf16[432,256]{1,0:T(8,128)(2,1)}, bf16[432,256]{1,0:T(8,128)(2,1)S(1)}, u32[]{:S(2)}, u32[]{:S(2)}) collective-permute-start(bf16[432,256]{1,0:T(8,128)(2,1)} %bitcast.65), channel_id=1, source_target_pairs={{0,1},{1,0},{2,3},{3,2},{4,5},{5,4},{6,7},{7,6},{8,9},{9,8},{10,11... | collective-permute-start | bytes 663560 | tf_op jit(solution)/shard_map/ppermute | solution.py:354
  8.8 22.7 %copy-start.2 = (f32[1,256]{1,0:T(1,128)S(1)}, f32[1,256]{1,0:T(1,128)}, u32[]{:S(2)}) copy-start(f32[1,256]{1,0:T(1,128)} %gain_ref.5) | copy-start | bytes 3076
  9.9 0.7 copy-start.1
  10.5 0.7 copy-start.3
  14.0 7.1 %collective-permute-start.8 = (bf16[432,256]{1,0:T(8,128)(2,1)S(1)}, bf16[432,256]{1,0:T(8,128)(2,1)S(1)}, u32[]{:S(2)}, u32[]{:S(2)}) collective-permute-start(bf16[432,256]{1,0:T(8,128)(2,1)S(1)} %collective-permute-done.3.refs_6_), channel_id=1, source_target_pairs={{0,2},{1,3},{2,0},{3,1},{4,6},{5,7},{6,4},{7,5},{8,10},{9,11},{10,... | collective-permute-start | bytes 663560 | tf_op jit(solution)/shard_map/ppermute | solution.py:354
  16.5 5.9 %collective-permute-start.1 = (bf16[432,256]{1,0:T(8,128)(2,1)S(1)}, bf16[432,256]{1,0:T(8,128)(2,1)S(1)}, u32[]{:S(2)}, u32[]{:S(2)}) collective-permute-start(bf16[432,256]{1,0:T(8,128)(2,1)S(1)} %collective-permute-done.refs_6_), channel_id=1, source_target_pairs={{0,4},{1,5},{2,6},{3,7},{4,0},{5,1},{6,2},{7,3},{8,12},{9,13},{10,... | collective-permute-start | bytes 663560 | tf_op jit(solution)/shard_map/ppermute | solution.py:354
  17.0 7.0 %collective-permute-start.6 = (bf16[432,256]{1,0:T(8,128)(2,1)S(1)}, bf16[432,256]{1,0:T(8,128)(2,1)S(1)}, u32[]{:S(2)}, u32[]{:S(2)}) collective-permute-start(bf16[432,256]{1,0:T(8,128)(2,1)S(1)} %collective-permute-done.5.refs_4_), channel_id=1, source_target_pairs={{0,1},{1,0},{2,3},{3,2},{4,5},{5,4},{6,7},{7,6},{8,9},{9,8},{10,11... | collective-permute-start | bytes 663560 | tf_op jit(solution)/shard_map/ppermute | solution.py:354
  17.0 8.8 %collective-permute-start.11 = (bf16[432,256]{1,0:T(8,128)(2,1)S(1)}, bf16[432,256]{1,0:T(8,128)(2,1)S(1)}, u32[]{:S(2)}, u32[]{:S(2)}) collective-permute-start(bf16[432,256]{1,0:T(8,128)(2,1)S(1)} %collective-permute-done.refs_6_), channel_id=1, source_target_pairs={{0,2},{1,3},{2,0},{3,1},{4,6},{5,7},{6,4},{7,5},{8,10},{9,11},{10,... | collective-permute-start | bytes 663560 | tf_op jit(solution)/shard_map/ppermute | solution.py:354
  18.5 7.3 %collective-permute-start.7 = (bf16[432,256]{1,0:T(8,128)(2,1)S(1)}, bf16[432,256]{1,0:T(8,128)(2,1)S(1)}, u32[]{:S(2)}, u32[]{:S(2)}) collective-permute-start(bf16[432,256]{1,0:T(8,128)(2,1)S(1)} %collective-permute-done.3.refs_6_), channel_id=1, source_target_pairs={{0,1},{1,0},{2,3},{3,2},{4,5},{5,4},{6,7},{7,6},{8,9},{9,8},{10,11... | collective-permute-start | bytes 663560 | tf_op jit(solution)/shard_map/ppermute | solution.py:354
  21.0 5.3 %collective-permute-start.9 = (bf16[432,256]{1,0:T(8,128)(2,1)S(1)}, bf16[432,256]{1,0:T(8,128)(2,1)S(1)}, u32[]{:S(2)}, u32[]{:S(2)}) collective-permute-start(bf16[432,256]{1,0:T(8,128)(2,1)S(1)} %collective-permute-done.8.refs_8_), channel_id=1, source_target_pairs={{0,1},{1,0},{2,3},{3,2},{4,5},{5,4},{6,7},{7,6},{8,9},{9,8},{10,11... | collective-permute-start | bytes 663560 | tf_op jit(solution)/shard_map/ppermute | solution.py:354
  22.5 7.6 %collective-permute-start.2 = (bf16[432,256]{1,0:T(8,128)(2,1)S(1)}, bf16[432,256]{1,0:T(8,128)(2,1)S(1)}, u32[]{:S(2)}, u32[]{:S(2)}) collective-permute-start(bf16[432,256]{1,0:T(8,128)(2,1)S(1)} %collective-permute-done.1.refs_10_), channel_id=1, source_target_pairs={{0,2},{1,3},{2,0},{3,1},{4,6},{5,7},{6,4},{7,5},{8,10},{9,11},{10,... | collective-permute-start | bytes 663560 | tf_op jit(solution)/shard_map/ppermute | solution.py:354
  23.9 6.1 %collective-permute-start.10 = (bf16[432,256]{1,0:T(8,128)(2,1)S(1)}, bf16[432,256]{1,0:T(8,128)(2,1)S(1)}, u32[]{:S(2)}, u32[]{:S(2)}) collective-permute-start(bf16[432,256]{1,0:T(8,128)(2,1)S(1)} %collective-permute-done.refs_6_), channel_id=1, source_target_pairs={{0,1},{1,0},{2,3},{3,2},{4,5},{5,4},{6,7},{7,6},{8,9},{9,8},{10,11... | collective-permute-start | bytes 663560 | tf_op jit(solution)/shard_map/ppermute | solution.py:354
  25.8 4.3 %collective-permute-start.13 = (bf16[432,256]{1,0:T(8,128)(2,1)S(1)}, bf16[432,256]{1,0:T(8,128)(2,1)S(1)}, u32[]{:S(2)}, u32[]{:S(2)}) collective-permute-start(bf16[432,256]{1,0:T(8,128)(2,1)S(1)} %collective-permute-done.1.refs_10_), channel_id=1, source_target_pairs={{0,1},{1,0},{2,3},{3,2},{4,5},{5,4},{6,7},{7,6},{8,9},{9,8},{10,11... | collective-permute-start | bytes 663560 | tf_op jit(solution)/shard_map/ppermute | solution.py:354
  25.8 4.3 %collective-permute-start.12 = (bf16[432,256]{1,0:T(8,128)(2,1)S(1)}, bf16[432,256]{1,0:T(8,128)(2,1)S(1)}, u32[]{:S(2)}, u32[]{:S(2)}) collective-permute-start(bf16[432,256]{1,0:T(8,128)(2,1)S(1)} %collective-permute-done.11.refs_8_), channel_id=1, source_target_pairs={{0,1},{1,0},{2,3},{3,2},{4,5},{5,4},{6,7},{7,6},{8,9},{9,8},{10,11... | collective-permute-start | bytes 663560 | tf_op jit(solution)/shard_map/ppermute | solution.py:354
  26.3 0.9 %copy-start = (bf16[1,432,256]{2,1,0:T(8,128)(2,1)S(1)}, bf16[1,432,256]{2,1,0:T(8,128)(2,1)}, u32[]{:S(2)}) copy-start(bf16[1,432,256]{2,1,0:T(8,128)(2,1)} %param.8) | copy-start | bytes 663556
  30.1 1.5 %collective-permute-start.14 = (bf16[432,256]{1,0:T(8,128)(2,1)S(1)}, bf16[432,256]{1,0:T(8,128)(2,1)S(1)}, u32[]{:S(2)}, u32[]{:S(2)}) collective-permute-start(bf16[432,256]{1,0:T(8,128)(2,1)S(1)} %collective-permute-done.2.refs_12_), channel_id=1, source_target_pairs={{0,1},{1,0},{2,3},{3,2},{4,5},{5,4},{6,7},{7,6},{8,9},{9,8},{10,11... | collective-permute-start | bytes 663560 | tf_op jit(solution)/shard_map/ppermute | solution.py:354
  33.8 8.6 %collective-permute-start.15 = (bf16[528,256]{1,0:T(8,128)(2,1)S(1)}, bf16[528,256]{1,0:T(8,128)(2,1)S(1)}, u32[]{:S(2)}, u32[]{:S(2)}) collective-permute-start(bf16[528,256]{1,0:T(8,128)(2,1)S(1)} %get-tuple-element.42.mine_ref), channel_id=1, source_target_pairs={{0,16},{16,0},{1,17},{17,1},{2,18},{18,2},{3,19},{19,3},{4,20},{20... | collective-permute-start | bytes 811016 | tf_op jit(solution)/shard_map/ppermute | solution.py:354
  45.5 2.4 %collective-permute-start.17 = (bf16[2,432,256]{2,1,0:T(8,128)(2,1)S(1)}, bf16[2,432,256]{2,1,0:T(8,128)(2,1)S(1)}, u32[]{:S(2)}, u32[]{:S(2)}) collective-permute-start(bf16[2,432,256]{2,1,0:T(8,128)(2,1)S(1)} %get-tuple-element.48), channel_id=1, source_target_pairs={{0,1},{1,0},{2,3},{3,2},{4,5},{5,4},{6,7},{7,6},{8,9},{9,8},{10,11... | collective-permute-start | bytes 1327112 | tf_op jit(solution)/shard_map/ppermute | solution.py:354
  45.6 5.9 %collective-permute-start.16 = (bf16[2,432,256]{2,1,0:T(8,128)(2,1)S(1)}, bf16[2,432,256]{2,1,0:T(8,128)(2,1)S(1)}, u32[]{:S(2)}, u32[]{:S(2)}) collective-permute-start(bf16[2,432,256]{2,1,0:T(8,128)(2,1)S(1)} %get-tuple-element.46), channel_id=1, source_target_pairs={{0,1},{1,0},{2,3},{3,2},{4,5},{5,4},{6,7},{7,6},{8,9},{9,8},{10,11... | collective-permute-start | bytes 1327112 | tf_op jit(solution)/shard_map/ppermute | solution.py:354
  47.3 4.3 %collective-permute-start.21 = (bf16[2,432,256]{2,1,0:T(8,128)(2,1)S(1)}, bf16[2,432,256]{2,1,0:T(8,128)(2,1)S(1)}, u32[]{:S(2)}, u32[]{:S(2)}) collective-permute-start(bf16[2,432,256]{2,1,0:T(8,128)(2,1)S(1)} %get-tuple-element.59), channel_id=1, source_target_pairs={{0,1},{1,0},{2,3},{3,2},{4,5},{5,4},{6,7},{7,6},{8,9},{9,8},{10,11... | collective-permute-start | bytes 1327112 | tf_op jit(solution)/shard_map/ppermute | solution.py:354
  47.5 2.7 %collective-permute-start.22 = (bf16[2,432,256]{2,1,0:T(8,128)(2,1)S(1)}, bf16[2,432,256]{2,1,0:T(8,128)(2,1)S(1)}, u32[]{:S(2)}, u32[]{:S(2)}) collective-permute-start(bf16[2,432,256]{2,1,0:T(8,128)(2,1)S(1)} %get-tuple-element.61), channel_id=1, source_target_pairs={{0,1},{1,0},{2,3},{3,2},{4,5},{5,4},{6,7},{7,6},{8,9},{9,8},{10,11... | collective-permute-start | bytes 1327112 | tf_op jit(solution)/shard_map/ppermute | solution.py:354
  48.0 5.9 %collective-permute-start.25 = (bf16[208,256]{1,0:T(8,128)(2,1)S(1)}, bf16[208,256]{1,0:T(8,128)(2,1)S(1)}, u32[]{:S(2)}, u32[]{:S(2)}) collective-permute-start(bf16[208,256]{1,0:T(8,128)(2,1)S(1)} %slice_bitcast_fusion.11), channel_id=1, source_target_pairs={{0,2},{1,3},{2,0},{3,1},{4,6},{5,7},{6,4},{7,5},{8,10},{9,11},{10,... | collective-permute-start | bytes 319496 | tf_op jit(solution)/shard_map/ppermute | solution.py:354
  49.5 7.1 %collective-permute-start.18 = (bf16[224,256]{1,0:T(8,128)(2,1)S(1)}, bf16[224,256]{1,0:T(8,128)(2,1)S(1)}, u32[]{:S(2)}, u32[]{:S(2)}) collective-permute-start(bf16[224,256]{1,0:T(8,128)(2,1)S(1)} %slice_bitcast_fusion.9), channel_id=1, source_target_pairs={{0,2},{1,3},{2,0},{3,1},{4,6},{5,7},{6,4},{7,5},{8,10},{9,11},{10,... | collective-permute-start | bytes 344072 | tf_op jit(solution)/shard_map/ppermute | solution.py:354
  50.4 13.6 %collective-permute-start.23 = (bf16[432,256]{1,0:T(8,128)(2,1)S(1)}, bf16[432,256]{1,0:T(8,128)(2,1)S(1)}, u32[]{:S(2)}, u32[]{:S(2)}) collective-permute-start(bf16[432,256]{1,0:T(8,128)(2,1)S(1)} %get-tuple-element.69), channel_id=1, source_target_pairs={{0,4},{1,5},{2,6},{3,7},{4,0},{5,1},{6,2},{7,3},{8,12},{9,13},{10,... | collective-permute-start | bytes 663560 | tf_op jit(solution)/shard_map/ppermute | solution.py:354
  51.5 15.4 %copy-start.4 = (s32[1,4]{1,0:T(1,128)S(1)}, s32[1,4]{1,0:T(1,128)}, u32[]{:S(2)}) copy-start(s32[1,4]{1,0:T(1,128)} %param.6) | copy-start | bytes 52
  54.0 7.1 %collective-permute-start.26 = (bf16[208,256]{1,0:T(8,128)(2,1)S(1)}, bf16[208,256]{1,0:T(8,128)(2,1)S(1)}, u32[]{:S(2)}, u32[]{:S(2)}) collective-permute-start(bf16[208,256]{1,0:T(8,128)(2,1)S(1)} %fusion.16), channel_id=1, source_target_pairs={{0,4},{1,5},{2,6},{3,7},{4,0},{5,1},{6,2},{7,3},{8,12},{9,13},{10,... | collective-permute-start | bytes 319496 | tf_op jit(solution)/shard_map/ppermute | solution.py:354
  55.1 5.9 %collective-permute-start.28 = (bf16[208,256]{1,0:T(8,128)(2,1)S(1)}, bf16[208,256]{1,0:T(8,128)(2,1)S(1)}, u32[]{:S(2)}, u32[]{:S(2)}) collective-permute-start(bf16[208,256]{1,0:T(8,128)(2,1)S(1)} %slice_bitcast_fusion.10), channel_id=1, source_target_pairs={{0,2},{1,3},{2,0},{3,1},{4,6},{5,7},{6,4},{7,5},{8,10},{9,11},{10,... | collective-permute-start | bytes 319496 | tf_op jit(solution)/shard_map/ppermute | solution.py:354
  56.6 9.1 %collective-permute-start.19 = (bf16[224,256]{1,0:T(8,128)(2,1)S(1)}, bf16[224,256]{1,0:T(8,128)(2,1)S(1)}, u32[]{:S(2)}, u32[]{:S(2)}) collective-permute-start(bf16[224,256]{1,0:T(8,128)(2,1)S(1)} %slice_bitcast_fusion.8), channel_id=1, source_target_pairs={{0,2},{1,3},{2,0},{3,1},{4,6},{5,7},{6,4},{7,5},{8,10},{9,11},{10,... | collective-permute-start | bytes 344072 | tf_op jit(solution)/shard_map/ppermute | solution.py:354
  57.2 8.5 %collective-permute-start.20 = (bf16[224,256]{1,0:T(8,128)(2,1)S(1)}, bf16[224,256]{1,0:T(8,128)(2,1)S(1)}, u32[]{:S(2)}, u32[]{:S(2)}) collective-permute-start(bf16[224,256]{1,0:T(8,128)(2,1)S(1)} %fusion.8), channel_id=1, source_target_pairs={{0,4},{1,5},{2,6},{3,7},{4,0},{5,1},{6,2},{7,3},{8,12},{9,13},{10,... | collective-permute-start | bytes 344072 | tf_op jit(solution)/shard_map/ppermute | solution.py:354
  61.1 10.3 %collective-permute-start.29 = (bf16[208,256]{1,0:T(8,128)(2,1)S(1)}, bf16[208,256]{1,0:T(8,128)(2,1)S(1)}, u32[]{:S(2)}, u32[]{:S(2)}) collective-permute-start(bf16[208,256]{1,0:T(8,128)(2,1)S(1)} %fusion.14), channel_id=1, source_target_pairs={{0,8},{1,9},{2,10},{3,11},{4,12},{5,13},{6,14},{7,15},{8,0},{9,1},... | collective-permute-start | bytes 319496 | tf_op jit(solution)/shard_map/ppermute | solution.py:354
  63.0 8.9 %collective-permute-start.27 = (bf16[432,256]{1,0:T(8,128)(2,1)S(1)}, bf16[432,256]{1,0:T(8,128)(2,1)S(1)}, u32[]{:S(2)}, u32[]{:S(2)}) collective-permute-start(bf16[432,256]{1,0:T(8,128)(2,1)S(1)} %get-tuple-element.63), channel_id=1, source_target_pairs={{0,4},{1,5},{2,6},{3,7},{4,0},{5,1},{6,2},{7,3},{8,12},{9,13},{10,... | collective-permute-start | bytes 663560 | tf_op jit(solution)/shard_map/ppermute | solution.py:354
  64.0 7.9 %collective-permute-start.24 = (bf16[432,256]{1,0:T(8,128)(2,1)S(1)}, bf16[432,256]{1,0:T(8,128)(2,1)S(1)}, u32[]{:S(2)}, u32[]{:S(2)}) collective-permute-start(bf16[432,256]{1,0:T(8,128)(2,1)S(1)} %fusion.1), channel_id=1, source_target_pairs={{0,2},{1,3},{2,0},{3,1},{4,6},{5,7},{6,4},{7,5},{8,10},{9,11},{10,... | collective-permute-start | bytes 663560 | tf_op jit(solution)/shard_map/ppermute | solution.py:354
  65.7 6.2 %collective-permute-start.30 = (bf16[224,256]{1,0:T(8,128)(2,1)S(1)}, bf16[224,256]{1,0:T(8,128)(2,1)S(1)}, u32[]{:S(2)}, u32[]{:S(2)}) collective-permute-start(bf16[224,256]{1,0:T(8,128)(2,1)S(1)} %fusion.11), channel_id=1, source_target_pairs={{0,8},{1,9},{2,10},{3,11},{4,12},{5,13},{6,14},{7,15},{8,0},{9,1},... | collective-permute-start | bytes 344072 | tf_op jit(solution)/shard_map/ppermute | solution.py:354

commit v7 on v6

--- a/solution.py
+++ b/solution.py
@@ -126,15 +126,20 @@
     return jnp.concatenate([total[:, :middle], total[:, middle:] + partial], axis=1)
 
 
-def half_gradient(turned_ref, cols_ref, sums_ref, dims, half):
+def half_gradient(turned_refs, cols_refs, sums_ref, dims, half):
     channels = dims[4]
     for k, low, high, at in half_pieces(half, dims):
         by_t, j = (26 - k) // 9 - 1, (26 - k) % 9
-        sums_ref[at : at + high - low, :] = jnp.dot(
-            turned_ref[low:high, :],
-            frame_columns(cols_ref, by_t, dims, j * channels, (j + 1) * channels),
-            preferred_element_type=jnp.float32,
-        ).astype(jnp.bfloat16)
+        total = None
+        for turned_ref, cols_ref in zip(turned_refs, cols_refs):
+            some = (cols_ref.shape[0], *dims[1:])
+            term = jnp.dot(
+                turned_ref[low:high, :],
+                frame_columns(cols_ref, by_t, some, j * channels, (j + 1) * channels),
+                preferred_element_type=jnp.float32,
+            )
+            total = term if total is None else total + term
+        sums_ref[at : at + high - low, :] = total.astype(jnp.bfloat16)
 
 
 def where_am_i(split):
@@ -218,25 +223,36 @@
 
 
 def far_kernel(dims, split, count, plan_ref, clips_ref, gain_ref, early_ref, cols_ref, base_ref, *rest):
-    pieces, (out_ref, kept_ref, weight_ref, held_ref, held_gain, sems) = rest[:count], rest[count:]
-    total = base_ref.shape[0]
+    pieces, (out_ref, weight_ref, held_ref, held_gain, sems) = rest[:count], rest[count:]
+    arriving = fetch([(clips_ref, held_ref), (gain_ref, held_gain)], sems)
+    lay_pieces(lax.axis_index("fsdp"), pieces, weight_ref)
+    wait_all(arriving)
+    rows = out_ref.shape[0] - ROW_TILE
+    out_ref[rows:, :] = split_gain(held_gain[...])
+    finish_clips(dims, split, 0, plan_ref, held_ref, cols_ref, base_ref, weight_ref, out_ref)
+
+
+def other_kernel(dims, split, plan_ref, clips_ref, cols_ref, base_ref, weight_ref, out_ref, held_ref, sems):
+    wait_all(fetch([(clips_ref, held_ref)], sems))
+    finish_clips(dims, split, dims[0] // 2, plan_ref, held_ref, cols_ref, base_ref, weight_ref, out_ref)
+
+
+def finish_clips(dims, split, first, plan_ref, clips_ref, cols_ref, base_ref, weight_ref, out_ref):
     section, place, near = where_am_i(split)
-    arriving = fetch([(clips_ref, held_ref), (gain_ref, held_gain)], sems)
-    lay_pieces(place, pieces, weight_ref)
-    leaving = pltpu.make_async_copy(weight_ref, kept_ref, sems.at[2])
-    leaving.start()
-    wait_all(arriving)
-    out_ref[total:, :] = split_gain(held_gain[...])
+    voxels = dims[1] * dims[2] * dims[3]
+    last = dims[0] // 2 if first == 0 else dims[0]
+    rows = (last - first) * voxels
+    some = (last - first, *dims[1:])
 
     def run(at, part):
         conv = half_forward if at == 0 else half_spread
-        value = base_ref[...] + conv(cols_ref, weight_ref, dims, part)
+        value = base_ref[first * voxels : last * voxels, :] + conv(cols_ref.at[first:last], weight_ref, some, part)
         if at == 0:
-            value = value + take_clips(plan_ref, held_ref, dims)
-        out_ref[:total, :] = value.astype(jnp.bfloat16)
+            picked = [clips_ref[plan_ref[m]].astype(jnp.float32) for m in range(first, last)]
+            value = value + jnp.concatenate(picked, axis=0)
+        out_ref[:rows, :] = value.astype(jnp.bfloat16)
 
     on_half(section, 1 - near, run)
-    leaving.wait()
 
 
 def hand_out(place, ways, sums_ref, outs):
@@ -250,103 +266,116 @@
             out[inner] = sums_ref[pl.ds(pl.multiple_of(owner * rows, ROW_TILE), rows), :]
 
 
-def gradient_kernel(dims, split, plan_ref, clips_ref, cotangent_ref, gain_ref, mine_ref, theirs_ref,
-                    early_cols_ref, grad_ref, hidden_ref, turned_ref, cols_ref, *rest):
+def prelude(dims, split, first, plan_ref, clips_ref, cotangent_ref, gain_row, gains_refs, mine, theirs,
+            early_cols_ref, grad_ref, hidden_ref, turned_ref, cols_ref):
+    section, place, near = where_am_i(split)
+    leading = section == 0
+    last = dims[0] // 2 if first == 0 else dims[0]
+    mine, theirs = mine.astype(jnp.float32), theirs.astype(jnp.float32)
+    hidden = jnp.where(leading, mine, theirs)
+    spread = jnp.where(leading, theirs, mine)
+    last_gain = jnp.where(leading, join_gain(gains_refs[1][...]), join_gain(gains_refs[0][...]))
+    cotangent = cotangent_ref[first:last].reshape(hidden.shape).astype(jnp.float32)
+    upstream = back(hidden, cotangent, spread, last_gain).astype(jnp.bfloat16)
+    grad_ref[...] = upstream
+    hidden_ref[...] = hidden.astype(jnp.bfloat16)
+    picked = jnp.concatenate([clips_ref[plan_ref[m]] for m in range(first, last)], axis=0).astype(jnp.float32)
+    turned_ref[...] = activate(jnp.where(leading, picked, hidden), gain_row).T
+
+    @pl.when(leading)
+    def _():
+        fill_columns(cols_ref, upstream.astype(jnp.float32), (last - first, *dims[1:]))
+
+    @pl.when(jnp.logical_not(leading))
+    def _():
+        cols_ref[...] = early_cols_ref[first:last]
+
+
+def begin_kernel(dims, split, plan_ref, clips_ref, cotangent_ref, gain_ref, mine_ref, theirs_ref, early_cols_ref,
+                 grad_ref, hidden_ref, turned_ref, cols_ref, held_clips, held_cotangent, held_gain, sems):
+    wait_all(fetch([(cotangent_ref, held_cotangent), (clips_ref, held_clips), (gain_ref, held_gain)], sems))
+    rows = grad_ref.shape[0]
+    gains_refs = mine_ref.at[rows : rows + ROW_TILE], theirs_ref.at[rows : rows + ROW_TILE]
+    prelude(dims, split, 0, plan_ref, held_clips, held_cotangent, held_gain[...], gains_refs, mine_ref[:rows, :],
+            theirs_ref[:rows, :], early_cols_ref, grad_ref, hidden_ref, turned_ref, cols_ref)
+
+
+def gradient_kernel(dims, split, plan_ref, clips_ref, cotangent_ref, gain_ref, mine_ref, theirs_ref, other_mine_ref,
+                    other_theirs_ref, early_cols_ref, first_turned_ref, first_cols_ref, grad_ref, hidden_ref,
+                    turned_ref, cols_ref, *rest):
     outs = rest[:-5]
     sums_ref, held_clips, held_cotangent, held_gain, sems = rest[-5:]
+    wait_all(fetch([(cotangent_ref, held_cotangent), (clips_ref, held_clips), (gain_ref, held_gain)], sems))
     section, place, near = where_am_i(split)
-    channels = dims[4]
-    total = dims[0] * dims[1] * dims[2] * dims[3]
-    arriving = fetch(
-        [
-            (cotangent_ref, held_cotangent),
-            (clips_ref, held_clips),
-            (gain_ref, held_gain),
-        ],
-        sems,
-    )
-    leading = section == 0
-    mine = mine_ref[:total, :].astype(jnp.float32)
-    theirs = theirs_ref[:total, :].astype(jnp.float32)
-    last_gain = join_gain(jnp.where(leading, theirs_ref[total:, :].astype(jnp.float32), mine_ref[total:, :].astype(jnp.float32)))
-    hidden = jnp.where(leading, mine, theirs)
-    spread = jnp.where(leading, theirs, mine)
-    hidden_ref[...] = hidden.astype(jnp.bfloat16)
-    wait_all(arriving)
-    cotangent = held_cotangent[...].reshape(total, channels).astype(jnp.float32)
-    upstream = back(hidden, cotangent, spread, last_gain).astype(jnp.bfloat16)
-    grad_ref[...] = upstream
-    unit = jnp.where(leading, take_clips(plan_ref, held_clips, dims), hidden)
-    turned_ref[...] = activate(unit, held_gain[...]).T
-
-    @pl.when(leading)
-    def _():
-        fill_columns(cols_ref, upstream.astype(jnp.float32), dims)
-
-    @pl.when(jnp.logical_not(leading))
-    def _():
-        cols_ref[...] = early_cols_ref[...]
-
+    rows = mine_ref.shape[0] - ROW_TILE
+    gains_refs = mine_ref.at[rows : rows + ROW_TILE], theirs_ref.at[rows : rows + ROW_TILE]
+    prelude(dims, split, dims[0] // 2, plan_ref, held_clips, held_cotangent, held_gain[...], gains_refs,
+            other_mine_ref[...], other_theirs_ref[...], early_cols_ref, grad_ref, hidden_ref, turned_ref, cols_ref)
     for part in (0, 1):
 
         @pl.when(near != part)
         def _(part=part):
-            half_gradient(turned_ref, cols_ref, sums_ref, dims, part)
+            half_gradient((first_turned_ref, turned_ref), (first_cols_ref, cols_ref), sums_ref, dims, part)
 
     hand_out(place, (12, 8) if split else (), sums_ref, outs)
 
 
-def rest_kernel(dims, split, turned_ref, cols_ref, *rest):
+def rest_kernel(dims, split, first_turned_ref, first_cols_ref, turned_ref, cols_ref, *rest):
     outs, sums_ref = rest[:-1], rest[-1]
     section, place, near = where_am_i(split)
     for part in (0, 1):
 
         @pl.when(near == part)
         def _(part=part):
-            half_gradient(turned_ref, cols_ref, sums_ref, dims, part)
+            half_gradient((first_turned_ref, turned_ref), (first_cols_ref, cols_ref), sums_ref, dims, part)
 
     hand_out(place, (4, 0) if split else (), sums_ref, outs)
 
 
-def last_kernel(dims, split, plan_ref, clips_ref, gain_ref, hidden_ref, grad_ref, near_ref, far_ref, acts_ref,
-                grads_ref, weight_ref, cols_ref, held_clips, held_gain, held_hidden, held_grad, made_acts, made_grads, sems):
+def last_kernel(dims, split, plan_ref, clips_ref, gain_ref, hidden_ref, grad_ref, other_hidden_ref, other_grad_ref,
+                near_ref, far_ref, acts_ref, grads_ref, cols_ref, held_clips, held_gain, held_hidden, held_grad,
+                made_acts, made_grads, sems):
     section, place, near = where_am_i(split)
-    half_rows = weight_ref.shape[0] // 2
-    first = pl.multiple_of(near * half_rows, ROW_TILE) if split else 0
-    second = pl.multiple_of((1 - near) * half_rows, ROW_TILE) if split else half_rows
+    first, second = hidden_ref.shape[0], other_hidden_ref.shape[0]
     arriving = fetch(
         [
-            (near_ref, weight_ref.at[pl.ds(first, half_rows)]),
-            (far_ref, weight_ref.at[pl.ds(second, half_rows)]),
-            (hidden_ref, held_hidden),
-            (grad_ref, held_grad),
+            (hidden_ref, held_hidden.at[pl.ds(0, first)]),
+            (grad_ref, held_grad.at[pl.ds(0, first)]),
+            (other_hidden_ref, held_hidden.at[pl.ds(first, second)]),
+            (other_grad_ref, held_grad.at[pl.ds(first, second)]),
             (gain_ref, held_gain),
             (clips_ref, held_clips),
         ],
         sems,
     )
     wait_all(arriving)
-    halves = weight_ref.at[pl.ds(0, half_rows)], weight_ref.at[pl.ds(half_rows, half_rows)]
     gain_row = held_gain[...]
-
-    @pl.when(section == 0)
+    leading = section == 0
+
+    @pl.when(leading)
     def _():
-        upstream = held_grad[...].astype(jnp.float32)
-        fill_columns(cols_ref, upstream, dims)
-        spread = half_spread(cols_ref, halves[0], dims, 0) + half_spread(cols_ref, halves[1], dims, 1)
-        ordered = take_clips(plan_ref, held_clips, dims)
-        back_out = back(ordered, upstream, spread, gain_row).astype(jnp.bfloat16)
-        made_grads[...] = back_out.reshape(made_grads.shape)
         made_acts[...] = held_hidden[...].reshape(made_acts.shape)
-
-    @pl.when(section != 0)
+        fill_columns(cols_ref, held_grad[...].astype(jnp.float32), dims)
+
+    @pl.when(jnp.logical_not(leading))
     def _():
-        hidden = held_hidden[...].astype(jnp.float32)
-        fill_columns(cols_ref, activate(hidden, gain_row).astype(jnp.float32), dims)
-        branch = half_forward(cols_ref, halves[0], dims, 0) + half_forward(cols_ref, halves[1], dims, 1)
-        made_acts[...] = (hidden + branch).astype(jnp.bfloat16).reshape(made_acts.shape)
         made_grads[...] = held_grad[...].reshape(made_grads.shape)
-
+        fill_columns(cols_ref, activate(held_hidden[...].astype(jnp.float32), gain_row).astype(jnp.float32), dims)
+
+    def run(at, part):
+        halves = (near_ref, far_ref) if part == 0 else (far_ref, near_ref)
+        conv = half_spread if at == 0 else half_forward
+        total = conv(cols_ref, halves[0], dims, 0) + conv(cols_ref, halves[1], dims, 1)
+        if at == 0:
+            ordered = take_clips(plan_ref, held_clips, dims)
+            upstream = held_grad[...].astype(jnp.float32)
+            back_out = back(ordered, upstream, total, gain_row).astype(jnp.bfloat16)
+            made_grads[...] = back_out.reshape(made_grads.shape)
+        else:
+            hidden = held_hidden[...].astype(jnp.float32)
+            made_acts[...] = (hidden + total).astype(jnp.bfloat16).reshape(made_acts.shape)
+
+    on_half(section, near, run)
     wait_all(fetch([(made_acts, acts_ref), (made_grads, grads_ref)], sems))
 
 
@@ -390,7 +419,6 @@
     gain_scratch = pltpu.VMEM((1, channels), jnp.float32)
     cols_shape = (micro, voxels + 2 * height * width, 9 * channels)
     volume = jax.ShapeDtypeStruct((total, channels), jnp.bfloat16)
-    turned_out = jax.ShapeDtypeStruct((channels, total), jnp.bfloat16)
     cols_out = jax.ShapeDtypeStruct(cols_shape, jnp.bfloat16)
     half_out = jax.ShapeDtypeStruct((half_rows, channels), jnp.bfloat16)
     token_out = jax.ShapeDtypeStruct((8, 128), jnp.float32)
@@ -450,32 +478,54 @@
             held[by + 1] = swap(held[by], "fsdp", 1)
         far = [held[by] for by in range(8, 16)]
 
+    first_rows = micro // 2 * voxels
     mine, far_weight = call(
         lambda dims, split, *refs: far_kernel(dims, split, count, *refs),
-        0.5,
-        out_shape=[jax.ShapeDtypeStruct((total + ROW_TILE, channels), jnp.bfloat16), half_out],
+        0.25,
+        out_shape=[jax.ShapeDtypeStruct((first_rows + ROW_TILE, channels), jnp.bfloat16), half_out],
         in_specs=[smem] + [anywhere] * 3 + [vmem] * (2 + count),
-        out_specs=[vmem, anywhere],
-        scratch_shapes=[half_weight, clips_scratch, gain_scratch, pltpu.SemaphoreType.DMA((3,))],
+        out_specs=[vmem] * 2,
+        scratch_shapes=[clips_scratch, gain_scratch, pltpu.SemaphoreType.DMA((2,))],
     )(order, flat_clips, gains, token, early_cols, base, *far)
-
     theirs = swap(mine, "section", 1)
 
+    other_mine = call(
+        other_kernel,
+        0.25,
+        out_shape=jax.ShapeDtypeStruct((total - first_rows, channels), jnp.bfloat16),
+        in_specs=[smem] + [anywhere] + [vmem] * 3,
+        out_specs=vmem,
+        scratch_shapes=[clips_scratch, pltpu.SemaphoreType.DMA((1,))],
+    )(order, flat_clips, early_cols, base, far_weight)
+    other_theirs = swap(other_mine, "section", 1)
+
     shapes = [jax.ShapeDtypeStruct((2, rows, channels), jnp.bfloat16)] * 4 if split else [half_out]
-    grad, hidden, turned, late_cols, *far_sums = call(
+    fetched = [clips_scratch, clips_scratch, gain_scratch, pltpu.SemaphoreType.DMA((3,))]
+
+    def operand_shapes(clip_count):
+        part_rows = clip_count * voxels
+        part = jax.ShapeDtypeStruct((part_rows, channels), jnp.bfloat16)
+        turned_part = jax.ShapeDtypeStruct((channels, part_rows), jnp.bfloat16)
+        return [part, part, turned_part, jax.ShapeDtypeStruct((clip_count, *cols_shape[1:]), jnp.bfloat16)]
+
+    grad, hidden, first_turned, first_cols = call(
+        begin_kernel,
+        0.1,
+        out_shape=operand_shapes(micro // 2),
+        in_specs=[smem] + [anywhere] * 3 + [vmem] * 3,
+        out_specs=[vmem] * 4,
+        scratch_shapes=fetched,
+    )(order, flat_clips, flat_cotangent, gains, mine, theirs, early_cols)
+
+    other_grad, other_hidden, turned, late_cols, *far_sums = call(
         gradient_kernel,
         0.5,
-        out_shape=[volume, volume, turned_out, cols_out] + shapes,
-        in_specs=[smem] + [anywhere] * 3 + [vmem] * 3,
+        out_shape=operand_shapes(micro - micro // 2) + shapes,
+        in_specs=[smem] + [anywhere] * 3 + [vmem] * 7,
         out_specs=[vmem] * (4 + len(shapes)),
-        scratch_shapes=[
-            half_weight,
-            clips_scratch,
-            clips_scratch,
-            gain_scratch,
-            pltpu.SemaphoreType.DMA((3,)),
-        ],
-    )(order, flat_clips, flat_cotangent, gains, mine, theirs, early_cols)
+        scratch_shapes=[half_weight] + fetched,
+    )(order, flat_clips, flat_cotangent, gains, mine, theirs, other_mine, other_theirs, early_cols, first_turned,
+      first_cols)
 
     if split:
 
@@ -492,10 +542,10 @@
         rest_kernel,
         0.5,
         out_shape=shapes,
-        in_specs=[vmem] * 2,
+        in_specs=[vmem] * 4,
         out_specs=[vmem] * len(shapes),
         scratch_shapes=[half_weight],
-    )(turned, late_cols)
+    )(first_turned, first_cols, turned, late_cols)
 
     if split:
         kept_8, send_8 = core_sum(*far_sums[2:])
@@ -529,10 +579,9 @@
         1.0,
         limit=LAST_VMEM_LIMIT,
         out_shape=[jax.ShapeDtypeStruct((1, *dims), jnp.bfloat16)] * 2,
-        in_specs=[smem] + [anywhere] * 6,
+        in_specs=[smem] + [anywhere] * 6 + [vmem] * 2,
         out_specs=[anywhere, anywhere],
         scratch_shapes=[
-            pltpu.VMEM((all_rows, channels), jnp.bfloat16),
             pltpu.VMEM(cols_shape, jnp.bfloat16),
             clips_scratch,
             gain_scratch,
@@ -542,7 +591,7 @@
             pltpu.VMEM((1, *dims), jnp.bfloat16),
             pltpu.SemaphoreType.DMA((6,)),
         ],
-    )(order, flat_clips, gains, hidden, grad, near_weight, far_weight)
+    )(order, flat_clips, gains, hidden, grad, other_hidden, other_grad, near_weight, far_weight)
     return (acts, grads, weight_grad[None])
 
 

time: 73.1 us -> 71.6 us (0.979)
  waiting for transfers between devices: 23.4 us -> 20.8 us
  Pallas kernels: 14 us -> 15.3 us
  local copies, waits for them, and re-layouts: 4.38 us -> 3.44 us
  starting transfers between devices: 28.7 us -> 29.5 us
    ppermute x31 -> x32, waiting for transfers between devices: 23.4 us -> 20.8 us  [swap(): lax.ppermute(value, axis, [(i, i ^ by) for i in range(lax.axis_size(axis))])]
    pallas_call x2 -> x4, Pallas kernels: 4.36 us -> 6.13 us  [the longest x1 2.54 us: on_device(): call(gradient_kernel, 0.5, out_shape=operand_shapes(micro - micro // 2) +...]
    unnamed x10, local copies, waits for them, and re-layouts: 2.28 us -> 1.34 us
    pallas_call x1, Pallas kernels: 2.25 us -> 1.42 us  [on_device(): call(lambda dims, split, *refs: far_kernel(dims, split, count, *refs), 0....]
    ppermute x31 -> x32, starting transfers between devices: 28.7 us -> 29.5 us  [swap(): lax.ppermute(value, axis, [(i, i ^ by) for i in range(lax.axis_size(axis))])]
  transfers between devices with their start and end apart: 31 -> 32, of which waited for: 11 -> 12; matrix products, arithmetic and copies ran while one was open for 4% -> 4% of each run, Pallas kernels for 12% -> 16%
where the time goes in v7:
time: 71.6 us; the launch traced here: 71.4 us
  starting transfers between devices  29.5 us (41%)
  waiting for transfers between devices  20.8 us (29%)
  Pallas kernels  15.3 us (21%)
  local copies, waits for them, and re-layouts  3.44 us (5%)
  other arithmetic  1.51 us (2%)
  between operations  0.87 us (1%)
    ppermute x32, starting transfers between devices, swap(): lax.ppermute(value, axis, [(i, i ^ by) for i in range(lax.axis_size(axis))])  29.5 us
    ppermute x32, waiting for transfers between devices, swap(): lax.ppermute(value, axis, [(i, i ^ by) for i in range(lax.axis_size(axis))])  20.8 us
    pallas_call x1, Pallas kernels, on_device(): call(last_kernel, 1.0, limit=LAST_VMEM_LIMIT, out_shape=[jax.ShapeDtypeSt...  4.86 us
    pallas_call x1, Pallas kernels, on_device(): call(gradient_kernel, 0.5, out_shape=operand_shapes(micro - micro // 2) +...  2.54 us
    pallas_call x1, Pallas kernels, on_device(): call(lambda dims, split, *refs: near_kernel(dims, split, count, *refs), 0...  1.7 us
  transfers between devices with their start and end apart: 32, of which 12 were waited for; matrix products, arithmetic and copies ran while one was open for 4% of the time, Pallas kernels for 16%

profile of v7, /device:TPU:0, one launch (start us, length us, event | category | flops | bytes accessed | tf_op | source)
XLA Modules:
  0.0 71.4 jit_solution(6007716543270256542)
XLA Ops:
  0.6 3.1 %collective-permute-start.3 = (bf16[432,256]{1,0:T(8,128)(2,1)}, bf16[432,256]{1,0:T(8,128)(2,1)S(1)}, u32[]{:S(2)}, u32[]{:S(2)}) collective-permute-start(bf16[432,256]{1,0:T(8,128)(2,1)} %bitcast.62), channel_id=1, source_target_pairs={{0,4},{1,5},{2,6},{3,7},{4,0},{5,1},{6,2},{7,3},{8,12},{9,13},{10,... | collective-permute-start | bytes 663560 | tf_op jit(solution)/shard_map/ppermute | solution.py:383
  3.7 2.6 %collective-permute-start = (bf16[432,256]{1,0:T(8,128)(2,1)}, bf16[432,256]{1,0:T(8,128)(2,1)S(1)}, u32[]{:S(2)}, u32[]{:S(2)}) collective-permute-start(bf16[432,256]{1,0:T(8,128)(2,1)} %bitcast.63), channel_id=1, source_target_pairs={{0,8},{1,9},{2,10},{3,11},{4,12},{5,13},{6,14},{7,15},{8,0},{9,1},... | collective-permute-start | bytes 663560 | tf_op jit(solution)/shard_map/ppermute | solution.py:383
  6.3 1.5 %collective-permute-start.5 = (bf16[432,256]{1,0:T(8,128)(2,1)}, bf16[432,256]{1,0:T(8,128)(2,1)S(1)}, u32[]{:S(2)}, u32[]{:S(2)}) collective-permute-start(bf16[432,256]{1,0:T(8,128)(2,1)} %bitcast.64), channel_id=1, source_target_pairs={{0,2},{1,3},{2,0},{3,1},{4,6},{5,7},{6,4},{7,5},{8,10},{9,11},{10,... | collective-permute-start | bytes 663560 | tf_op jit(solution)/shard_map/ppermute | solution.py:383
  7.8 1.0 %reshape.26.clips_ref.refs_1_ = bf16[4,128,256]{2,1,0:T(8,128)(2,1)S(1)} reshape(bf16[4,4,8,4,256]{4,3,2,1,0:T(4,128)(2,1)} %param.5) | data formatting | bytes 524288 | tf_op jit(solution)/shard_map/reshape | solution.py:409
  8.8 1.0 %reshape.27.cotangent_ref = bf16[4,128,256]{2,1,0:T(8,128)(2,1)S(1)} reshape(bf16[4,4,8,4,256]{4,3,2,1,0:T(4,128)(2,1)} %param.9) | data formatting | bytes 524288 | tf_op jit(solution)/shard_map/reshape | solution.py:410
  9.9 0.7 copy-done.1
  10.5 0.7 copy-done.3
  11.2 1.2 %shard_map.76 = (bf16[4,192,2304]{2,1,0:T(8,128)(2,1)S(1)}, f32[8,128]{1,0:T(8,128)S(1)}) custom-call(s32[4]{0:T(128)S(1)} %bitcast.67, bf16[4,128,256]{2,1,0:T(8,128)(2,1)S(1)} %reshape.26.clips_ref.refs_1_, bf16[4,128,256]{2,1,0:T(8,128)(2,1)S(1)} %reshape.27.cotangent_ref, f32[1,256]{1,0:T(1,128)S(1)} %copy-done.1, f32[1,256]{1,0:T(1,128)S(1)} %copy-done.1), custom_call_target="tpu_custom_call" | custom-call | flops 362387872 | bytes 3538944 | tf_op jit(solution)/shard_map/pallas_call | solution.py:444
  12.4 1.6 %collective-permute-done.3.refs_6_ = bf16[432,256]{1,0:T(8,128)(2,1)S(1)} collective-permute-done((bf16[432,256]{1,0:T(8,128)(2,1)}, bf16[432,256]{1,0:T(8,128)(2,1)S(1)}, u32[]{:S(2)}, u32[]{:S(2)}) %collective-permute-start.3) | collective-permute-done | bytes 221216 | tf_op jit(solution)/shard_map/ppermute | solution.py:383
  14.0 1.7 %collective-permute-start.8 = (bf16[432,256]{1,0:T(8,128)(2,1)S(1)}, bf16[432,256]{1,0:T(8,128)(2,1)S(1)}, u32[]{:S(2)}, u32[]{:S(2)}) collective-permute-start(bf16[432,256]{1,0:T(8,128)(2,1)S(1)} %collective-permute-done.3.refs_6_), channel_id=1, source_target_pairs={{0,2},{1,3},{2,0},{3,1},{4,6},{5,7},{6,4},{7,5},{8,10},{9,11},{10,... | collective-permute-start | bytes 663560 | tf_op jit(solution)/shard_map/ppermute | solution.py:383
  15.6 0.9 %collective-permute-done.refs_6_ = bf16[432,256]{1,0:T(8,128)(2,1)S(1)} collective-permute-done((bf16[432,256]{1,0:T(8,128)(2,1)}, bf16[432,256]{1,0:T(8,128)(2,1)S(1)}, u32[]{:S(2)}, u32[]{:S(2)}) %collective-permute-start) | collective-permute-done | bytes 221216 | tf_op jit(solution)/shard_map/ppermute | solution.py:383
  16.5 0.4 collective-permute-start.1
  17.0 1.5 %collective-permute-start.11 = (bf16[432,256]{1,0:T(8,128)(2,1)S(1)}, bf16[432,256]{1,0:T(8,128)(2,1)S(1)}, u32[]{:S(2)}, u32[]{:S(2)}) collective-permute-start(bf16[432,256]{1,0:T(8,128)(2,1)S(1)} %collective-permute-done.refs_6_), channel_id=1, source_target_pairs={{0,2},{1,3},{2,0},{3,1},{4,6},{5,7},{6,4},{7,5},{8,10},{9,11},{10,... | collective-permute-start | bytes 663560 | tf_op jit(solution)/shard_map/ppermute | solution.py:383
  18.5 0.2 collective-permute-start.7
  18.7 2.3 %collective-permute-done.8.refs_8_ = bf16[432,256]{1,0:T(8,128)(2,1)S(1)} collective-permute-done((bf16[432,256]{1,0:T(8,128)(2,1)S(1)}, bf16[432,256]{1,0:T(8,128)(2,1)S(1)}, u32[]{:S(2)}, u32[]{:S(2)}) %collective-permute-start.8) | collective-permute-done | bytes 221216 | tf_op jit(solution)/shard_map/ppermute | solution.py:383
  21.0 1.4 %collective-permute-done.1.refs_10_ = bf16[432,256]{1,0:T(8,128)(2,1)S(1)} collective-permute-done((bf16[432,256]{1,0:T(8,128)(2,1)S(1)}, bf16[432,256]{1,0:T(8,128)(2,1)S(1)}, u32[]{:S(2)}, u32[]{:S(2)}) %collective-permute-start.1) | collective-permute-done | bytes 221216 | tf_op jit(solution)/shard_map/ppermute | solution.py:383
  22.5 1.5 %collective-permute-start.2 = (bf16[432,256]{1,0:T(8,128)(2,1)S(1)}, bf16[432,256]{1,0:T(8,128)(2,1)S(1)}, u32[]{:S(2)}, u32[]{:S(2)}) collective-permute-start(bf16[432,256]{1,0:T(8,128)(2,1)S(1)} %collective-permute-done.1.refs_10_), channel_id=1, source_target_pairs={{0,2},{1,3},{2,0},{3,1},{4,6},{5,7},{6,4},{7,5},{8,10},{9,11},{10,... | collective-permute-start | bytes 663560 | tf_op jit(solution)/shard_map/ppermute | solution.py:383
  24.0 1.8 %collective-permute-done.11.refs_8_ = bf16[432,256]{1,0:T(8,128)(2,1)S(1)} collective-permute-done((bf16[432,256]{1,0:T(8,128)(2,1)S(1)}, bf16[432,256]{1,0:T(8,128)(2,1)S(1)}, u32[]{:S(2)}, u32[]{:S(2)}) %collective-permute-start.11) | collective-permute-done | bytes 221216 | tf_op jit(solution)/shard_map/ppermute | solution.py:383
  25.8 0.5 collective-permute-start.12
  26.3 1.7 %shard_map.77 = (f32[512,256]{1,0:T(8,128)S(1)}, f32[8,128]{1,0:T(8,128)S(1)}, bf16[3456,256]{1,0:T(8,128)(2,1)S(1)}) custom-call(bf16[4,192,2304]{2,1,0:T(8,128)(2,1)S(1)} %get-tuple-element.38.refs_0_.refs_4_.early_cols_ref.cols_ref, f32[8,128]{1,0:T(8,128)S(1)} %get-tuple-element.40.refs_1_, bf16[432,256]{1,0:T(8,128)(2,1)S(1)} %bitcast.66, ...), custom_call_target="tpu_custom_call" | custom-call | flops 905969664 | bytes 3538944 | tf_op jit(solution)/shard_map/pallas_call | solution.py:466
  28.0 2.1 %collective-permute-done.2.refs_12_ = bf16[432,256]{1,0:T(8,128)(2,1)S(1)} collective-permute-done((bf16[432,256]{1,0:T(8,128)(2,1)S(1)}, bf16[432,256]{1,0:T(8,128)(2,1)S(1)}, u32[]{:S(2)}, u32[]{:S(2)}) %collective-permute-start.2) | collective-permute-done | bytes 221216 | tf_op jit(solution)/shard_map/ppermute | solution.py:383
  30.1 1.5 %collective-permute-done.14.refs_13_ = bf16[432,256]{1,0:T(8,128)(2,1)S(1)} collective-permute-done((bf16[432,256]{1,0:T(8,128)(2,1)S(1)}, bf16[432,256]{1,0:T(8,128)(2,1)S(1)}, u32[]{:S(2)}, u32[]{:S(2)}) %collective-permute-start.14) | collective-permute-done | bytes 221216 | tf_op jit(solution)/shard_map/ppermute | solution.py:383
  31.6 1.4 %shard_map.78 = (bf16[272,256]{1,0:T(8,128)(2,1)S(1)}, bf16[3456,256]{1,0:T(8,128)(2,1)S(1)}) custom-call(s32[4]{0:T(128)S(1)} %bitcast.68, bf16[4,128,256]{2,1,0:T(8,128)(2,1)S(1)} %reshape.26.clips_ref.refs_1_, f32[1,256]{1,0:T(1,128)S(1)} %copy-done.2, f32[8,128]{1,0:T(8,128)S(1)} %get-tuple-element.43.refs_3_, ...), custom_call_target="tpu_custom_call" | custom-call | flops 452984832 | bytes 3538944 | tf_op jit(solution)/shard_map/pallas_call | solution.py:482
  33.0 1.4 %collective-permute-start.15 = (bf16[272,256]{1,0:T(8,128)(2,1)S(1)}, bf16[272,256]{1,0:T(8,128)(2,1)S(1)}, u32[]{:S(2)}, u32[]{:S(2)}) collective-permute-start(bf16[272,256]{1,0:T(8,128)(2,1)S(1)} %get-tuple-element.46.mine_ref), channel_id=1, source_target_pairs={{0,16},{16,0},{1,17},{17,1},{2,18},{18,2},{3,19},{19,3},{4,20},{20... | collective-permute-start | bytes 417800 | tf_op jit(solution)/shard_map/ppermute | solution.py:383
  34.4 1.2 %shard_map.80.other_mine_ref = bf16[256,256]{1,0:T(8,128)(2,1)S(1)} custom-call(s32[4]{0:T(128)S(1)} %bitcast.69, bf16[4,128,256]{2,1,0:T(8,128)(2,1)S(1)} %reshape.26.clips_ref.refs_1_, bf16[4,192,2304]{2,1,0:T(8,128)(2,1)S(1)} %get-tuple-element.38.refs_0_.refs_4_.early_cols_ref.cols_ref, f32[512,256]{1,0:T(8,128)S(1)} %get-tuple-element.44.refs_5_.base_ref, ...), custom_call_target="tpu_custom_call" | custom-call | flops 452984832 | bytes 3538944 | tf_op jit(solution)/shard_map/pallas_call | solution.py:492
  35.7 0.7 %collective-permute-start.16 = (bf16[256,256]{1,0:T(8,128)(2,1)S(1)}, bf16[256,256]{1,0:T(8,128)(2,1)S(1)}, u32[]{:S(2)}, u32[]{:S(2)}) collective-permute-start(bf16[256,256]{1,0:T(8,128)(2,1)S(1)} %shard_map.80.other_mine_ref), channel_id=1, source_target_pairs={{0,16},{16,0},{1,17},{17,1},{2,18},{18,2},{3,19},{19,3},{4,20},{20... | collective-permute-start | bytes 393224 | tf_op jit(solution)/shard_map/ppermute | solution.py:383
  36.4 2.9 %collective-permute-done.15.theirs_ref = bf16[272,256]{1,0:T(8,128)(2,1)S(1)} collective-permute-done((bf16[272,256]{1,0:T(8,128)(2,1)S(1)}, bf16[272,256]{1,0:T(8,128)(2,1)S(1)}, u32[]{:S(2)}, u32[]{:S(2)}) %collective-permute-start.15) | collective-permute-done | bytes 139296 | tf_op jit(solution)/shard_map/ppermute | solution.py:383
  39.3 1.1 %shard_map.79 = (bf16[256,256]{1,0:T(8,128)(2,1)S(1)}, bf16[256,256]{1,0:T(8,128)(2,1)S(1)}, bf16[256,256]{1,0:T(8,128)(2,1)S(1)}, bf16[2,192,2304]{2,1,0:T(8,128)(2,1)S(1)}) custom-call(s32[4]{0:T(128)S(1)} %bitcast.70, bf16[4,128,256]{2,1,0:T(8,128)(2,1)S(1)} %reshape.26.clips_ref.refs_1_, bf16[4,128,256]{2,1,0:T(8,128)(2,1)S(1)} %reshape.27.cotangent_ref, ...), custom_call_target="tpu_custom_call" | custom-call | flops 181193936 | bytes 3538944 | tf_op jit(solution)/shard_map/pallas_call | solution.py:511
  40.4 1.2 %collective-permute-done.16.other_theirs_ref = bf16[256,256]{1,0:T(8,128)(2,1)S(1)} collective-permute-done((bf16[256,256]{1,0:T(8,128)(2,1)S(1)}, bf16[256,256]{1,0:T(8,128)(2,1)S(1)}, u32[]{:S(2)}, u32[]{:S(2)}) %collective-permute-start.16) | collective-permute-done | bytes 131104 | tf_op jit(solution)/shard_map/ppermute | solution.py:383
  41.6 2.5 %shard_map.81 = (bf16[256,256]{1,0:T(8,128)(2,1)S(1)}, bf16[256,256]{1,0:T(8,128)(2,1)S(1)}, bf16[256,256]{1,0:T(8,128)(2,1)S(1)}, bf16[2,192,2304]{2,1,0:T(8,12...) custom-call(s32[4]{0:T(128)S(1)} %bitcast.71, ...), custom_call_target="tpu_custom_call" | custom-call | flops 905969664 | bytes 3538944 | tf_op jit(solution)/shard_map/pallas_call | solution.py:520
  44.2 0.5 collective-permute-start.17
  44.7 1.2 %shard_map.83 = (bf16[2,432,256]{2,1,0:T(8,128)(2,1)S(1)}, bf16[2,432,256]{2,1,0:T(8,128)(2,1)S(1)}, bf16[2,432,256]{2,1,0:T(8,128)(2,1)S(1)}, bf16[2,432,256]{2,1,0:T(8,128)(2,1)S(1)}) custom-call(bf16[256,256]{1,0:T(8,128)(2,1)S(1)} %get-tuple-element.50.first_turned_ref, bf16[2,192,2304]{2,1,0:T(8,128)(2,1)S(1)} %get-tuple-element.51.first_cols_ref, ...), custom_call_target="tpu_custom_call" | custom-call | flops 905969664 | bytes 3538944 | tf_op jit(solution)/shard_map/pallas_call | solution.py:541
  46.1 0.4 collective-permute-start.23
  46.6 1.4 %collective-permute-start.26 = (bf16[208,256]{1,0:T(8,128)(2,1)S(1)}, bf16[208,256]{1,0:T(8,128)(2,1)S(1)}, u32[]{:S(2)}, u32[]{:S(2)}) collective-permute-start(bf16[208,256]{1,0:T(8,128)(2,1)S(1)} %slice_bitcast_fusion.11), channel_id=1, source_target_pairs={{0,2},{1,3},{2,0},{3,1},{4,6},{5,7},{6,4},{7,5},{8,10},{9,11},{10,... | collective-permute-start | bytes 319496 | tf_op jit(solution)/shard_map/ppermute | solution.py:383
  48.0 0.8 %collective-permute-start.19 = (bf16[224,256]{1,0:T(8,128)(2,1)S(1)}, bf16[224,256]{1,0:T(8,128)(2,1)S(1)}, u32[]{:S(2)}, u32[]{:S(2)}) collective-permute-start(bf16[224,256]{1,0:T(8,128)(2,1)S(1)} %slice_bitcast_fusion.9), channel_id=1, source_target_pairs={{0,2},{1,3},{2,0},{3,1},{4,6},{5,7},{6,4},{7,5},{8,10},{9,11},{10,... | collective-permute-start | bytes 344072 | tf_op jit(solution)/shard_map/ppermute | solution.py:383
  49.0 1.1 %collective-permute-start.24 = (bf16[432,256]{1,0:T(8,128)(2,1)S(1)}, bf16[432,256]{1,0:T(8,128)(2,1)S(1)}, u32[]{:S(2)}, u32[]{:S(2)}) collective-permute-start(bf16[432,256]{1,0:T(8,128)(2,1)S(1)} %get-tuple-element.77), channel_id=1, source_target_pairs={{0,4},{1,5},{2,6},{3,7},{4,0},{5,1},{6,2},{7,3},{8,12},{9,13},{10,... | collective-permute-start | bytes 663560 | tf_op jit(solution)/shard_map/ppermute | solution.py:383
  50.4 2.2 %collective-permute-done.26 = bf16[208,256]{1,0:T(8,128)(2,1)S(1)} collective-permute-done((bf16[208,256]{1,0:T(8,128)(2,1)S(1)}, bf16[208,256]{1,0:T(8,128)(2,1)S(1)}, u32[]{:S(2)}, u32[]{:S(2)}) %collective-permute-start.26) | collective-permute-done | bytes 106528 | tf_op jit(solution)/shard_map/ppermute | solution.py:383
  52.5 1.1 %collective-permute-start.27 = (bf16[208,256]{1,0:T(8,128)(2,1)S(1)}, bf16[208,256]{1,0:T(8,128)(2,1)S(1)}, u32[]{:S(2)}, u32[]{:S(2)}) collective-permute-start(bf16[208,256]{1,0:T(8,128)(2,1)S(1)} %fusion.16), channel_id=1, source_target_pairs={{0,4},{1,5},{2,6},{3,7},{4,0},{5,1},{6,2},{7,3},{8,12},{9,13},{10,... | collective-permute-start | bytes 319496 | tf_op jit(solution)/shard_map/ppermute | solution.py:383
  53.7 1.5 %collective-permute-start.29 = (bf16[208,256]{1,0:T(8,128)(2,1)S(1)}, bf16[208,256]{1,0:T(8,128)(2,1)S(1)}, u32[]{:S(2)}, u32[]{:S(2)}) collective-permute-start(bf16[208,256]{1,0:T(8,128)(2,1)S(1)} %slice_bitcast_fusion.10), channel_id=1, source_target_pairs={{0,2},{1,3},{2,0},{3,1},{4,6},{5,7},{6,4},{7,5},{8,10},{9,11},{10,... | collective-permute-start | bytes 319496 | tf_op jit(solution)/shard_map/ppermute | solution.py:383
  55.2 0.6 collective-permute-start.20
  55.8 1.0 %collective-permute-start.21 = (bf16[224,256]{1,0:T(8,128)(2,1)S(1)}, bf16[224,256]{1,0:T(8,128)(2,1)S(1)}, u32[]{:S(2)}, u32[]{:S(2)}) collective-permute-start(bf16[224,256]{1,0:T(8,128)(2,1)S(1)} %fusion.8), channel_id=1, source_target_pairs={{0,4},{1,5},{2,6},{3,7},{4,0},{5,1},{6,2},{7,3},{8,12},{9,13},{10,... | collective-permute-start | bytes 344072 | tf_op jit(solution)/shard_map/ppermute | solution.py:383
  56.8 2.8 %collective-permute-done.27 = bf16[208,256]{1,0:T(8,128)(2,1)S(1)} collective-permute-done((bf16[208,256]{1,0:T(8,128)(2,1)S(1)}, bf16[208,256]{1,0:T(8,128)(2,1)S(1)}, u32[]{:S(2)}, u32[]{:S(2)}) %collective-permute-start.27) | collective-permute-done | bytes 106528 | tf_op jit(solution)/shard_map/ppermute | solution.py:383
  59.7 1.9 %collective-permute-start.30 = (bf16[208,256]{1,0:T(8,128)(2,1)S(1)}, bf16[208,256]{1,0:T(8,128)(2,1)S(1)}, u32[]{:S(2)}, u32[]{:S(2)}) collective-permute-start(bf16[208,256]{1,0:T(8,128)(2,1)S(1)} %fusion.14), channel_id=1, source_target_pairs={{0,8},{1,9},{2,10},{3,11},{4,12},{5,13},{6,14},{7,15},{8,0},{9,1},... | collective-permute-start | bytes 319496 | tf_op jit(solution)/shard_map/ppermute | solution.py:383
  61.6 0.9 %collective-permute-start.28 = (bf16[432,256]{1,0:T(8,128)(2,1)S(1)}, bf16[432,256]{1,0:T(8,128)(2,1)S(1)}, u32[]{:S(2)}, u32[]{:S(2)}) collective-permute-start(bf16[432,256]{1,0:T(8,128)(2,1)S(1)} %get-tuple-element.71), channel_id=1, source_target_pairs={{0,4},{1,5},{2,6},{3,7},{4,0},{5,1},{6,2},{7,3},{8,12},{9,13},{10,... | collective-permute-start | bytes 663560 | tf_op jit(solution)/shard_map/ppermute | solution.py:383
  62.5 1.7 %collective-permute-start.25 = (bf16[432,256]{1,0:T(8,128)(2,1)S(1)}, bf16[432,256]{1,0:T(8,128)(2,1)S(1)}, u32[]{:S(2)}, u32[]{:S(2)}) collective-permute-start(bf16[432,256]{1,0:T(8,128)(2,1)S(1)} %fusion.1), channel_id=1, source_target_pairs={{0,2},{1,3},{2,0},{3,1},{4,6},{5,7},{6,4},{7,5},{8,10},{9,11},{10,... | collective-permute-start | bytes 663560 | tf_op jit(solution)/shard_map/ppermute | solution.py:383
  64.3 1.2 %collective-permute-start.31 = (bf16[224,256]{1,0:T(8,128)(2,1)S(1)}, bf16[224,256]{1,0:T(8,128)(2,1)S(1)}, u32[]{:S(2)}, u32[]{:S(2)}) collective-permute-start(bf16[224,256]{1,0:T(8,128)(2,1)S(1)} %fusion.11), channel_id=1, source_target_pairs={{0,8},{1,9},{2,10},{3,11},{4,12},{5,13},{6,14},{7,15},{8,0},{9,1},... | collective-permute-start | bytes 344072 | tf_op jit(solution)/shard_map/ppermute | solution.py:383
  65.5 4.9 %shard_map.82 = (bf16[1,4,4,8,4,256]{5,4,3,2,1,0:T(4,128)(2,1)}, bf16[1,4,4,8,4,256]{5,4,3,2,1,0:T(4,128)(2,1)}) custom-call(s32[4]{0:T(128)S(1)} %bitcast.72, bf16[4,128,256]{2,1,0:T(8,128)(2,1)S(1)} %reshape.26.clips_ref.refs_1_, f32[1,256]{1,0:T(1,128)S(1)} %copy-done.2, bf16[256,256]{1,0:T(8,128)(2,1)S(1)} %get-tuple-element.47.hidden_ref, ...), custom_call_target="tpu_custom_call" | custom-call | flops 1811939328 | bytes 3538944 | tf_op jit(solution)/shard_map/pallas_call | solution.py:577
  70.5 0.9 %fusion.6 = f32[1,432,256]{2,1,0:T(8,128)} fusion(f32[2,432,256]{2,1,0:T(8,128)S(1)} %convert_add_fusion, bf16[432,256]{1,0:T(8,128)(2,1)S(1)} %collective-permute-done.28, bf16[432,256]{1,0:T(8,128)(2,1)S(1)} %collective-permute-done.25, bf16[224,256]{1,0:T(8,128)(2,1)S(1)} %collective-permute-done.31, bf16[208,256]{1,0:T(8,128)(2,1)S(1)} %collective-permute-done.30), kind=kLoop, calls=%fused_computation.12 | loop fusion | flops 1105920 | bytes 1548288 | tf_op jit(solution)/shard_map/broadcast_in_dim | solution.py:595
  (51 shorter events, 1.1 us)
Async XLA Ops:
  0.6 25.7 %copy-start = (bf16[1,432,256]{2,1,0:T(8,128)(2,1)S(1)}, bf16[1,432,256]{2,1,0:T(8,128)(2,1)}, u32[]{:S(2)}) copy-start(bf16[1,432,256]{2,1,0:T(8,128)(2,1)} %param.8) | copy-start | bytes 663556
  0.6 13.3 %collective-permute-start.3 = (bf16[432,256]{1,0:T(8,128)(2,1)}, bf16[432,256]{1,0:T(8,128)(2,1)S(1)}, u32[]{:S(2)}, u32[]{:S(2)}) collective-permute-start(bf16[432,256]{1,0:T(8,128)(2,1)} %bitcast.62), channel_id=1, source_target_pairs={{0,4},{1,5},{2,6},{3,7},{4,0},{5,1},{6,2},{7,3},{8,12},{9,13},{10,... | collective-permute-start | bytes 663560 | tf_op jit(solution)/shard_map/ppermute | solution.py:383
  3.7 12.8 %collective-permute-start = (bf16[432,256]{1,0:T(8,128)(2,1)}, bf16[432,256]{1,0:T(8,128)(2,1)S(1)}, u32[]{:S(2)}, u32[]{:S(2)}) collective-permute-start(bf16[432,256]{1,0:T(8,128)(2,1)} %bitcast.63), channel_id=1, source_target_pairs={{0,8},{1,9},{2,10},{3,11},{4,12},{5,13},{6,14},{7,15},{8,0},{9,1},... | collective-permute-start | bytes 663560 | tf_op jit(solution)/shard_map/ppermute | solution.py:383
  6.3 10.6 %collective-permute-start.5 = (bf16[432,256]{1,0:T(8,128)(2,1)}, bf16[432,256]{1,0:T(8,128)(2,1)S(1)}, u32[]{:S(2)}, u32[]{:S(2)}) collective-permute-start(bf16[432,256]{1,0:T(8,128)(2,1)} %bitcast.64), channel_id=1, source_target_pairs={{0,2},{1,3},{2,0},{3,1},{4,6},{5,7},{6,4},{7,5},{8,10},{9,11},{10,... | collective-permute-start | bytes 663560 | tf_op jit(solution)/shard_map/ppermute | solution.py:383
  7.8 10.7 %collective-permute-start.4 = (bf16[432,256]{1,0:T(8,128)(2,1)}, bf16[432,256]{1,0:T(8,128)(2,1)S(1)}, u32[]{:S(2)}, u32[]{:S(2)}) collective-permute-start(bf16[432,256]{1,0:T(8,128)(2,1)} %bitcast.65), channel_id=1, source_target_pairs={{0,1},{1,0},{2,3},{3,2},{4,5},{5,4},{6,7},{7,6},{8,9},{9,8},{10,11... | collective-permute-start | bytes 663560 | tf_op jit(solution)/shard_map/ppermute | solution.py:383
  9.9 0.7 copy-start.1
  10.5 0.7 copy-start.3
  14.0 7.1 %collective-permute-start.8 = (bf16[432,256]{1,0:T(8,128)(2,1)S(1)}, bf16[432,256]{1,0:T(8,128)(2,1)S(1)}, u32[]{:S(2)}, u32[]{:S(2)}) collective-permute-start(bf16[432,256]{1,0:T(8,128)(2,1)S(1)} %collective-permute-done.3.refs_6_), channel_id=1, source_target_pairs={{0,2},{1,3},{2,0},{3,1},{4,6},{5,7},{6,4},{7,5},{8,10},{9,11},{10,... | collective-permute-start | bytes 663560 | tf_op jit(solution)/shard_map/ppermute | solution.py:383
  16.5 5.9 %collective-permute-start.1 = (bf16[432,256]{1,0:T(8,128)(2,1)S(1)}, bf16[432,256]{1,0:T(8,128)(2,1)S(1)}, u32[]{:S(2)}, u32[]{:S(2)}) collective-permute-start(bf16[432,256]{1,0:T(8,128)(2,1)S(1)} %collective-permute-done.refs_6_), channel_id=1, source_target_pairs={{0,4},{1,5},{2,6},{3,7},{4,0},{5,1},{6,2},{7,3},{8,12},{9,13},{10,... | collective-permute-start | bytes 663560 | tf_op jit(solution)/shard_map/ppermute | solution.py:383
  17.0 7.0 %collective-permute-start.6 = (bf16[432,256]{1,0:T(8,128)(2,1)S(1)}, bf16[432,256]{1,0:T(8,128)(2,1)S(1)}, u32[]{:S(2)}, u32[]{:S(2)}) collective-permute-start(bf16[432,256]{1,0:T(8,128)(2,1)S(1)} %collective-permute-done.5.refs_4_), channel_id=1, source_target_pairs={{0,1},{1,0},{2,3},{3,2},{4,5},{5,4},{6,7},{7,6},{8,9},{9,8},{10,11... | collective-permute-start | bytes 663560 | tf_op jit(solution)/shard_map/ppermute | solution.py:383
  17.0 8.8 %collective-permute-start.11 = (bf16[432,256]{1,0:T(8,128)(2,1)S(1)}, bf16[432,256]{1,0:T(8,128)(2,1)S(1)}, u32[]{:S(2)}, u32[]{:S(2)}) collective-permute-start(bf16[432,256]{1,0:T(8,128)(2,1)S(1)} %collective-permute-done.refs_6_), channel_id=1, source_target_pairs={{0,2},{1,3},{2,0},{3,1},{4,6},{5,7},{6,4},{7,5},{8,10},{9,11},{10,... | collective-permute-start | bytes 663560 | tf_op jit(solution)/shard_map/ppermute | solution.py:383
  18.5 7.3 %collective-permute-start.7 = (bf16[432,256]{1,0:T(8,128)(2,1)S(1)}, bf16[432,256]{1,0:T(8,128)(2,1)S(1)}, u32[]{:S(2)}, u32[]{:S(2)}) collective-permute-start(bf16[432,256]{1,0:T(8,128)(2,1)S(1)} %collective-permute-done.3.refs_6_), channel_id=1, source_target_pairs={{0,1},{1,0},{2,3},{3,2},{4,5},{5,4},{6,7},{7,6},{8,9},{9,8},{10,11... | collective-permute-start | bytes 663560 | tf_op jit(solution)/shard_map/ppermute | solution.py:383
  21.0 5.3 %collective-permute-start.9 = (bf16[432,256]{1,0:T(8,128)(2,1)S(1)}, bf16[432,256]{1,0:T(8,128)(2,1)S(1)}, u32[]{:S(2)}, u32[]{:S(2)}) collective-permute-start(bf16[432,256]{1,0:T(8,128)(2,1)S(1)} %collective-permute-done.8.refs_8_), channel_id=1, source_target_pairs={{0,1},{1,0},{2,3},{3,2},{4,5},{5,4},{6,7},{7,6},{8,9},{9,8},{10,11... | collective-permute-start | bytes 663560 | tf_op jit(solution)/shard_map/ppermute | solution.py:383
  22.5 7.6 %collective-permute-start.2 = (bf16[432,256]{1,0:T(8,128)(2,1)S(1)}, bf16[432,256]{1,0:T(8,128)(2,1)S(1)}, u32[]{:S(2)}, u32[]{:S(2)}) collective-permute-start(bf16[432,256]{1,0:T(8,128)(2,1)S(1)} %collective-permute-done.1.refs_10_), channel_id=1, source_target_pairs={{0,2},{1,3},{2,0},{3,1},{4,6},{5,7},{6,4},{7,5},{8,10},{9,11},{10,... | collective-permute-start | bytes 663560 | tf_op jit(solution)/shard_map/ppermute | solution.py:383
  24.0 6.1 %collective-permute-start.10 = (bf16[432,256]{1,0:T(8,128)(2,1)S(1)}, bf16[432,256]{1,0:T(8,128)(2,1)S(1)}, u32[]{:S(2)}, u32[]{:S(2)}) collective-permute-start(bf16[432,256]{1,0:T(8,128)(2,1)S(1)} %collective-permute-done.refs_6_), channel_id=1, source_target_pairs={{0,1},{1,0},{2,3},{3,2},{4,5},{5,4},{6,7},{7,6},{8,9},{9,8},{10,11... | collective-permute-start | bytes 663560 | tf_op jit(solution)/shard_map/ppermute | solution.py:383
  25.8 4.3 %collective-permute-start.13 = (bf16[432,256]{1,0:T(8,128)(2,1)S(1)}, bf16[432,256]{1,0:T(8,128)(2,1)S(1)}, u32[]{:S(2)}, u32[]{:S(2)}) collective-permute-start(bf16[432,256]{1,0:T(8,128)(2,1)S(1)} %collective-permute-done.1.refs_10_), channel_id=1, source_target_pairs={{0,1},{1,0},{2,3},{3,2},{4,5},{5,4},{6,7},{7,6},{8,9},{9,8},{10,11... | collective-permute-start | bytes 663560 | tf_op jit(solution)/shard_map/ppermute | solution.py:383
  25.8 4.3 %collective-permute-start.12 = (bf16[432,256]{1,0:T(8,128)(2,1)S(1)}, bf16[432,256]{1,0:T(8,128)(2,1)S(1)}, u32[]{:S(2)}, u32[]{:S(2)}) collective-permute-start(bf16[432,256]{1,0:T(8,128)(2,1)S(1)} %collective-permute-done.11.refs_8_), channel_id=1, source_target_pairs={{0,1},{1,0},{2,3},{3,2},{4,5},{5,4},{6,7},{7,6},{8,9},{9,8},{10,11... | collective-permute-start | bytes 663560 | tf_op jit(solution)/shard_map/ppermute | solution.py:383
  26.3 5.2 %copy-start.2 = (f32[1,256]{1,0:T(1,128)S(1)}, f32[1,256]{1,0:T(1,128)}, u32[]{:S(2)}) copy-start(f32[1,256]{1,0:T(1,128)} %gain_ref.7) | copy-start | bytes 3076
  30.1 1.5 %collective-permute-start.14 = (bf16[432,256]{1,0:T(8,128)(2,1)S(1)}, bf16[432,256]{1,0:T(8,128)(2,1)S(1)}, u32[]{:S(2)}, u32[]{:S(2)}) collective-permute-start(bf16[432,256]{1,0:T(8,128)(2,1)S(1)} %collective-permute-done.2.refs_12_), channel_id=1, source_target_pairs={{0,1},{1,0},{2,3},{3,2},{4,5},{5,4},{6,7},{7,6},{8,9},{9,8},{10,11... | collective-permute-start | bytes 663560 | tf_op jit(solution)/shard_map/ppermute | solution.py:383
  33.0 6.3 %collective-permute-start.15 = (bf16[272,256]{1,0:T(8,128)(2,1)S(1)}, bf16[272,256]{1,0:T(8,128)(2,1)S(1)}, u32[]{:S(2)}, u32[]{:S(2)}) collective-permute-start(bf16[272,256]{1,0:T(8,128)(2,1)S(1)} %get-tuple-element.46.mine_ref), channel_id=1, source_target_pairs={{0,16},{16,0},{1,17},{17,1},{2,18},{18,2},{3,19},{19,3},{4,20},{20... | collective-permute-start | bytes 417800 | tf_op jit(solution)/shard_map/ppermute | solution.py:383
  35.7 5.9 %collective-permute-start.16 = (bf16[256,256]{1,0:T(8,128)(2,1)S(1)}, bf16[256,256]{1,0:T(8,128)(2,1)S(1)}, u32[]{:S(2)}, u32[]{:S(2)}) collective-permute-start(bf16[256,256]{1,0:T(8,128)(2,1)S(1)} %shard_map.80.other_mine_ref), channel_id=1, source_target_pairs={{0,16},{16,0},{1,17},{17,1},{2,18},{18,2},{3,19},{19,3},{4,20},{20... | collective-permute-start | bytes 393224 | tf_op jit(solution)/shard_map/ppermute | solution.py:383
  44.1 2.4 %collective-permute-start.18 = (bf16[2,432,256]{2,1,0:T(8,128)(2,1)S(1)}, bf16[2,432,256]{2,1,0:T(8,128)(2,1)S(1)}, u32[]{:S(2)}, u32[]{:S(2)}) collective-permute-start(bf16[2,432,256]{2,1,0:T(8,128)(2,1)S(1)} %get-tuple-element.55), channel_id=1, source_target_pairs={{0,1},{1,0},{2,3},{3,2},{4,5},{5,4},{6,7},{7,6},{8,9},{9,8},{10,11... | collective-permute-start | bytes 1327112 | tf_op jit(solution)/shard_map/ppermute | solution.py:383
  44.2 5.9 %collective-permute-start.17 = (bf16[2,432,256]{2,1,0:T(8,128)(2,1)S(1)}, bf16[2,432,256]{2,1,0:T(8,128)(2,1)S(1)}, u32[]{:S(2)}, u32[]{:S(2)}) collective-permute-start(bf16[2,432,256]{2,1,0:T(8,128)(2,1)S(1)} %get-tuple-element.53), channel_id=1, source_target_pairs={{0,1},{1,0},{2,3},{3,2},{4,5},{5,4},{6,7},{7,6},{8,9},{9,8},{10,11... | collective-permute-start | bytes 1327112 | tf_op jit(solution)/shard_map/ppermute | solution.py:383
  45.9 4.3 %collective-permute-start.22 = (bf16[2,432,256]{2,1,0:T(8,128)(2,1)S(1)}, bf16[2,432,256]{2,1,0:T(8,128)(2,1)S(1)}, u32[]{:S(2)}, u32[]{:S(2)}) collective-permute-start(bf16[2,432,256]{2,1,0:T(8,128)(2,1)S(1)} %get-tuple-element.67), channel_id=1, source_target_pairs={{0,1},{1,0},{2,3},{3,2},{4,5},{5,4},{6,7},{7,6},{8,9},{9,8},{10,11... | collective-permute-start | bytes 1327112 | tf_op jit(solution)/shard_map/ppermute | solution.py:383
  46.1 2.7 %collective-permute-start.23 = (bf16[2,432,256]{2,1,0:T(8,128)(2,1)S(1)}, bf16[2,432,256]{2,1,0:T(8,128)(2,1)S(1)}, u32[]{:S(2)}, u32[]{:S(2)}) collective-permute-start(bf16[2,432,256]{2,1,0:T(8,128)(2,1)S(1)} %get-tuple-element.69), channel_id=1, source_target_pairs={{0,1},{1,0},{2,3},{3,2},{4,5},{5,4},{6,7},{7,6},{8,9},{9,8},{10,11... | collective-permute-start | bytes 1327112 | tf_op jit(solution)/shard_map/ppermute | solution.py:383
  46.6 5.9 %collective-permute-start.26 = (bf16[208,256]{1,0:T(8,128)(2,1)S(1)}, bf16[208,256]{1,0:T(8,128)(2,1)S(1)}, u32[]{:S(2)}, u32[]{:S(2)}) collective-permute-start(bf16[208,256]{1,0:T(8,128)(2,1)S(1)} %slice_bitcast_fusion.11), channel_id=1, source_target_pairs={{0,2},{1,3},{2,0},{3,1},{4,6},{5,7},{6,4},{7,5},{8,10},{9,11},{10,... | collective-permute-start | bytes 319496 | tf_op jit(solution)/shard_map/ppermute | solution.py:383
  48.0 7.1 %collective-permute-start.19 = (bf16[224,256]{1,0:T(8,128)(2,1)S(1)}, bf16[224,256]{1,0:T(8,128)(2,1)S(1)}, u32[]{:S(2)}, u32[]{:S(2)}) collective-permute-start(bf16[224,256]{1,0:T(8,128)(2,1)S(1)} %slice_bitcast_fusion.9), channel_id=1, source_target_pairs={{0,2},{1,3},{2,0},{3,1},{4,6},{5,7},{6,4},{7,5},{8,10},{9,11},{10,... | collective-permute-start | bytes 344072 | tf_op jit(solution)/shard_map/ppermute | solution.py:383
  49.0 13.5 %collective-permute-start.24 = (bf16[432,256]{1,0:T(8,128)(2,1)S(1)}, bf16[432,256]{1,0:T(8,128)(2,1)S(1)}, u32[]{:S(2)}, u32[]{:S(2)}) collective-permute-start(bf16[432,256]{1,0:T(8,128)(2,1)S(1)} %get-tuple-element.77), channel_id=1, source_target_pairs={{0,4},{1,5},{2,6},{3,7},{4,0},{5,1},{6,2},{7,3},{8,12},{9,13},{10,... | collective-permute-start | bytes 663560 | tf_op jit(solution)/shard_map/ppermute | solution.py:383
  50.3 15.1 %copy-start.4 = (s32[1,4]{1,0:T(1,128)S(1)}, s32[1,4]{1,0:T(1,128)}, u32[]{:S(2)}) copy-start(s32[1,4]{1,0:T(1,128)} %param.6) | copy-start | bytes 52
  52.5 7.1 %collective-permute-start.27 = (bf16[208,256]{1,0:T(8,128)(2,1)S(1)}, bf16[208,256]{1,0:T(8,128)(2,1)S(1)}, u32[]{:S(2)}, u32[]{:S(2)}) collective-permute-start(bf16[208,256]{1,0:T(8,128)(2,1)S(1)} %fusion.16), channel_id=1, source_target_pairs={{0,4},{1,5},{2,6},{3,7},{4,0},{5,1},{6,2},{7,3},{8,12},{9,13},{10,... | collective-permute-start | bytes 319496 | tf_op jit(solution)/shard_map/ppermute | solution.py:383
  53.7 5.9 %collective-permute-start.29 = (bf16[208,256]{1,0:T(8,128)(2,1)S(1)}, bf16[208,256]{1,0:T(8,128)(2,1)S(1)}, u32[]{:S(2)}, u32[]{:S(2)}) collective-permute-start(bf16[208,256]{1,0:T(8,128)(2,1)S(1)} %slice_bitcast_fusion.10), channel_id=1, source_target_pairs={{0,2},{1,3},{2,0},{3,1},{4,6},{5,7},{6,4},{7,5},{8,10},{9,11},{10,... | collective-permute-start | bytes 319496 | tf_op jit(solution)/shard_map/ppermute | solution.py:383
  55.2 9.0 %collective-permute-start.20 = (bf16[224,256]{1,0:T(8,128)(2,1)S(1)}, bf16[224,256]{1,0:T(8,128)(2,1)S(1)}, u32[]{:S(2)}, u32[]{:S(2)}) collective-permute-start(bf16[224,256]{1,0:T(8,128)(2,1)S(1)} %slice_bitcast_fusion.8), channel_id=1, source_target_pairs={{0,2},{1,3},{2,0},{3,1},{4,6},{5,7},{6,4},{7,5},{8,10},{9,11},{10,... | collective-permute-start | bytes 344072 | tf_op jit(solution)/shard_map/ppermute | solution.py:383
  55.8 8.4 %collective-permute-start.21 = (bf16[224,256]{1,0:T(8,128)(2,1)S(1)}, bf16[224,256]{1,0:T(8,128)(2,1)S(1)}, u32[]{:S(2)}, u32[]{:S(2)}) collective-permute-start(bf16[224,256]{1,0:T(8,128)(2,1)S(1)} %fusion.8), channel_id=1, source_target_pairs={{0,4},{1,5},{2,6},{3,7},{4,0},{5,1},{6,2},{7,3},{8,12},{9,13},{10,... | collective-permute-start | bytes 344072 | tf_op jit(solution)/shard_map/ppermute | solution.py:383
  59.7 10.7 %collective-permute-start.30 = (bf16[208,256]{1,0:T(8,128)(2,1)S(1)}, bf16[208,256]{1,0:T(8,128)(2,1)S(1)}, u32[]{:S(2)}, u32[]{:S(2)}) collective-permute-start(bf16[208,256]{1,0:T(8,128)(2,1)S(1)} %fusion.14), channel_id=1, source_target_pairs={{0,8},{1,9},{2,10},{3,11},{4,12},{5,13},{6,14},{7,15},{8,0},{9,1},... | collective-permute-start | bytes 319496 | tf_op jit(solution)/shard_map/ppermute | solution.py:383
  61.6 8.9 %collective-permute-start.28 = (bf16[432,256]{1,0:T(8,128)(2,1)S(1)}, bf16[432,256]{1,0:T(8,128)(2,1)S(1)}, u32[]{:S(2)}, u32[]{:S(2)}) collective-permute-start(bf16[432,256]{1,0:T(8,128)(2,1)S(1)} %get-tuple-element.71), channel_id=1, source_target_pairs={{0,4},{1,5},{2,6},{3,7},{4,0},{5,1},{6,2},{7,3},{8,12},{9,13},{10,... | collective-permute-start | bytes 663560 | tf_op jit(solution)/shard_map/ppermute | solution.py:383
  62.5 8.0 %collective-permute-start.25 = (bf16[432,256]{1,0:T(8,128)(2,1)S(1)}, bf16[432,256]{1,0:T(8,128)(2,1)S(1)}, u32[]{:S(2)}, u32[]{:S(2)}) collective-permute-start(bf16[432,256]{1,0:T(8,128)(2,1)S(1)} %fusion.1), channel_id=1, source_target_pairs={{0,2},{1,3},{2,0},{3,1},{4,6},{5,7},{6,4},{7,5},{8,10},{9,11},{10,... | collective-permute-start | bytes 663560 | tf_op jit(solution)/shard_map/ppermute | solution.py:383
  64.3 6.2 %collective-permute-start.31 = (bf16[224,256]{1,0:T(8,128)(2,1)S(1)}, bf16[224,256]{1,0:T(8,128)(2,1)S(1)}, u32[]{:S(2)}, u32[]{:S(2)}) collective-permute-start(bf16[224,256]{1,0:T(8,128)(2,1)S(1)} %fusion.11), channel_id=1, source_target_pairs={{0,8},{1,9},{2,10},{3,11},{4,12},{5,13},{6,14},{7,15},{8,0},{9,1},... | collective-permute-start | bytes 344072 | tf_op jit(solution)/shard_map/ppermute | solution.py:383
